TPU v7x, 512 devices: a whole 4x8x8 slice. The times are simulated.
512 devices in a mesh: member: 16 (over z_hi, x), space: 32 (over z_lo, y, core).
Axes of the slice: x: 4, y: 8, z: 8 (z_hi: 4, z_lo: 2; z = z_hi * 2 + z_lo), core: 2. Of those that a mesh axis runs over, the one named last changes fastest.
Arguments:
- tokens: bfloat16 [16, 32, 256, 1536], P('member', None, 'space'), may hold values from -6 to 6
- norm_gain: float32 [1536], replicated, may hold values from 0.1 to 1.9
- w_qkv: bfloat16 [1536, 2304], P('space'), may hold values from -0.15625 to 0.15625
- w_out: bfloat16 [768, 1536], P('space'), may hold values from -0.21875 to 0.21875
- rel_bias: float32 [24, 64, 64], replicated, may hold values from -4 to 402
- w_decode: bfloat16 [1536, 69], replicated, may hold values from -0.15625 to 0.15625
- obs_value: float32 [16, 32, 2, 128], P('member', 'space'), may hold values from -6 to 6
- obs_pert: float32 [16, 16, 32, 2, 128], P(None, 'member', 'space'), may hold values from -4 to 4
- obs_index: int32 [16, 32, 2, 128], P('member', 'space'), may hold values from 0 to 1103
- block_list: int32 [16, 32, 4], P('member', 'space'), may hold values from 0 to 17
- list_count: int32 [16, 32], P('member', 'space'), may hold values from 1 to 4, as said below
- gains: bfloat16 [16, 32, 4, 128, 1104], P('member', 'space'), may hold values from -0.375 to 0.375
Outputs:
- increments: float32 [16, 32, 16, 1104], P('member', 'space')
Inputs may be any that keep to these rules, and one draw needn't show every extreme that they name: `list_count`: some tile's list has exactly 4 live entries.
All inputs are finite; a program needn't handle non-finite values.
Results may differ from a plain program's by a relative error of at most 0.012.
Values may be sent and summed in bfloat16 or wider, within the bound.
No kernel may reach another device: no remote copies, remote signals or barrier semaphores. Data moves between devices by JAX's collectives and lax.ppermute only.
A program may use at most 64 MiB of HBM per device.

v0:
```python
import jax
import jax.numpy as jnp
from jax import lax
from jax.sharding import PartitionSpec as P

HEADS = 24
HS = 32
WIN = 8
SHIFT = 4


def padded(x, sides, width, wrap):
    for axis, dim in sides:
        peers, length = (lax.axis_size(axis), x.shape[dim])
        up = [(i, (i + 1) % peers) for i in range(peers if wrap else peers - 1)]
        down = [(j, i) for i, j in up]
        last = lax.slice_in_dim(x, length - width, length, axis=dim)
        initial = lax.slice_in_dim(x, 0, width, axis=dim)
        before = lax.ppermute(last, axis, up)
        after = lax.ppermute(initial, axis, down)
        x = jnp.concatenate([before, x, after], axis=dim)
    return x


def layer_norm(values, gain_row):
    widened = values.astype(jnp.float32)
    center = jnp.mean(widened, axis=-1, keepdims=True)
    spread = jnp.mean((widened - center) ** 2, axis=-1, keepdims=True)
    return ((widened - center) * lax.rsqrt(spread + 1e-05) * gain_row).astype(jnp.bfloat16)


def to_windows(array, lat_count, col_count):
    shaped = array.reshape(lat_count // WIN, WIN, col_count // WIN, WIN, HEADS, HS)
    return shaped.transpose(0, 2, 4, 1, 3, 5).reshape(
        lat_count // WIN, col_count // WIN, HEADS, WIN * WIN, HS
    )


def from_windows(blocked, lat_count, col_count):
    shaped = blocked.reshape(lat_count // WIN, col_count // WIN, HEADS, WIN, WIN, HS)
    return shaped.transpose(0, 3, 1, 4, 2, 5).reshape(lat_count, col_count, HEADS * HS)


def window_attention(queries, key_part, value_part, rel_bias):
    lat_count, col_count = (queries.shape[0], queries.shape[1])
    query_win = to_windows(queries, lat_count, col_count)
    key_win = to_windows(key_part, lat_count, col_count)
    value_win = to_windows(value_part, lat_count, col_count)
    scores = jnp.einsum(
        "abhqd,abhkd->abhqk", query_win, key_win, preferred_element_type=jnp.float32
    )
    scores = scores * HS ** (-0.5) + rel_bias
    weights = jax.nn.softmax(scores, axis=-1).astype(jnp.bfloat16)
    mixed = jnp.einsum("abhqk,abhkd->abhqd", weights, value_win, preferred_element_type=jnp.float32)
    return from_windows(mixed.astype(jnp.bfloat16), lat_count, col_count)


def body(
    tokens,
    norm_gain,
    w_qkv,
    w_out,
    rel_bias,
    w_decode,
    obs_value,
    obs_pert,
    obs_index,
    block_list,
    list_count,
    gains,
):
    member_tile = tokens[0]
    lat_count, own_cols, feature_count = (
        member_tile.shape[0],
        member_tile.shape[1],
        member_tile.shape[2],
    )
    head_width = HEADS * HS
    extended = padded(member_tile, (("space", 1),), SHIFT, True)
    ext_cols = extended.shape[1]
    normed = layer_norm(extended, norm_gain).reshape(-1, feature_count)
    left_cols = normed
    projected = (
        jnp.dot(
            left_cols,
            lax.all_gather(w_qkv, "space", axis=0, tiled=True),
            preferred_element_type=jnp.float32,
        )
        .astype(jnp.bfloat16)
        .reshape(lat_count, ext_cols, 3 * head_width)
    )
    queries = projected[:, :, :head_width]
    key_part = projected[:, :, head_width : 2 * head_width]
    value_part = projected[:, :, 2 * head_width :]
    attended = window_attention(queries, key_part, value_part, rel_bias)
    attended = attended[:, SHIFT : SHIFT + own_cols].reshape(-1, head_width)
    left_cols = attended
    output_sum = jnp.dot(
        left_cols,
        lax.all_gather(w_out, "space", axis=0, tiled=True),
        preferred_element_type=jnp.float32,
    )
    updated = (member_tile.reshape(-1, feature_count).astype(jnp.float32) + output_sum).astype(
        jnp.bfloat16
    )
    fields = jnp.dot(updated, w_decode, preferred_element_type=jnp.float32)
    channel_count = w_decode.shape[1]
    outgoing = fields.reshape(1, lat_count, own_cols * channel_count)
    ensemble = lax.all_to_all(
        outgoing.astype(jnp.bfloat16), "member", split_axis=1, concat_axis=0, tiled=True
    ).astype(outgoing.dtype)
    member_count = ensemble.shape[0]
    ensemble = ensemble.reshape(member_count, -1)
    block_count, per_block = (obs_index.shape[2], obs_index.shape[3])
    observed = ensemble[:, obs_index[0, 0].reshape(-1)].reshape(
        member_count, block_count, per_block
    )
    innovation = obs_value[0, 0][None] + obs_pert[:, 0, 0] - observed
    local_table = innovation.transpose(1, 0, 2)[None, None]
    lon_table = padded(local_table, (("space", 1),), 1, True)
    full_table = padded(lon_table.astype(jnp.bfloat16), (("member", 0),), 1, False).astype(
        lon_table.dtype
    )
    block_table = full_table.reshape(9 * block_count, member_count, per_block)
    chosen = block_table[block_list[0, 0]]
    live_mask = (jnp.arange(block_list.shape[2]) < list_count[0, 0]).astype(jnp.float32)
    chosen = (chosen * live_mask[:, None, None]).astype(jnp.bfloat16)
    increment = jnp.einsum("jmo,joc->mc", chosen, gains[0, 0], preferred_element_type=jnp.float32)
    return increment[None, None]


def solution(mesh):
    in_specs = (
        P("member", None, "space", None),
        P(),
        P("space", None),
        P("space", None),
        P(),
        P(),
        P("member", "space", None, None),
        P(None, "member", "space", None, None),
        P("member", "space", None, None),
        P("member", "space", None),
        P("member", "space"),
        P("member", "space", None, None, None),
    )
    out_specs = P("member", "space", None, None)
    return jax.shard_map(body, mesh=mesh, in_specs=in_specs, out_specs=out_specs, check_vma=False)
```

profile of v0, /device:TPU:6, one launch (start us, length us, event | category | flops | bytes accessed | tf_op | source)
XLA Modules:
  0.0 211.7 jit_solution(1581200255627720754)
XLA Ops:
  7.3 2.6 %fusion.30 = (bf16[32,4,1536]{2,1,0:T(4,128)(2,1)}, bf16[32,4,1536]{2,1,0:T(4,128)(2,1)}) fusion(bf16[32,8,1536]{2,1,0:T(8,128)(2,1)} %bitcast.81), kind=kLoop, calls=%fused_computation.53 | loop fusion | bytes 1572864 | tf_op jit(solution)/shard_map/slice | solution.py:17
  9.9 1.9 collective-permute-start
  11.8 6.6 %collective-permute-start.1 = (bf16[32,4,1536]{2,1,0:T(4,128)(2,1)}, bf16[32,4,1536]{2,1,0:T(4,128)(2,1)S(1)}, u32[]{:S(2)}, u32[]{:S(2)}) collective-permute-start(bf16[32,4,1536]{2,1,0:T(4,128)(2,1)} %get-tuple-element.9), channel_id=1, source_target_pairs={{1,0},{2,1},{3,2},{4,3},{5,4},{6,5},{7,6},{8,7},{9,8},{10,9},{11,1... | collective-permute-start | bytes 1179656 | tf_op jit(solution)/shard_map/ppermute | solution.py:20
  19.9 2.3 %collective-permute-done = bf16[32,4,1536]{2,1,0:T(4,128)(2,1)S(1)} collective-permute-done((bf16[32,4,1536]{2,1,0:T(4,128)(2,1)}, bf16[32,4,1536]{2,1,0:T(4,128)(2,1)S(1)}, u32[]{:S(2)}, u32[]{:S(2)}) %collective-permute-start) | collective-permute-done | bytes 393248 | tf_op jit(solution)/shard_map/ppermute | solution.py:19
  22.2 1.9 collective-permute-done.1
  28.5 59.5 %all-gather.3.cloned.1.call-done = bf16[1536,2304]{1,0:T(8,128)(2,1)} async-done(((bf16[48,2304]{1,0:T(8,128)(2,1)}), bf16[1536,2304]{1,0:T(8,128)(2,1)}) %all-gather.3.cloned.1.call-update) | async-done | bytes 7077904 | tf_op jit(solution)/shard_map/all_gather | solution.py:86
  88.1 7.3 %convolution_convert_fusion = bf16[512,2304]{1,0:T(8,128)(2,1)S(1)} fusion(bf16[512,1536]{1,0:T(8,128)(2,1)} %fusion.9, bf16[1536,2304]{1,0:T(8,128)(2,1)} %all-gather.3.cloned.1.call-done), kind=kOutput, calls=%fused_computation.7 | convolution fusion | flops 3625058304 | bytes 11010048 | tf_op jit(solution)/shard_map/dot_general | solution.py:84
  96.7 4.7 %reshape.200 = bf16[4,8,2,8,24,32]{5,4,3,2,1,0:T(8,128)(2,1)} reshape(bf16[32,16,768]{2,1,0:T(8,128)(2,1)} %get-tuple-element.5) | data formatting | bytes 1572864 | tf_op jit(solution)/shard_map/reshape | solution.py:33
  101.4 4.7 %reshape.202 = bf16[4,8,2,8,24,32]{5,4,3,2,1,0:T(8,128)(2,1)} reshape(bf16[32,16,768]{2,1,0:T(8,128)(2,1)} %get-tuple-element.7) | data formatting | bytes 1572864 | tf_op jit(solution)/shard_map/reshape | solution.py:33
  106.1 3.4 %reshape.204 = bf16[4,8,2,8,24,32]{5,4,3,2,1,0:T(8,128)(2,1)} reshape(bf16[32,16,768]{2,1,0:T(8,128)(2,1)S(1)} %get-tuple-element.6) | data formatting | bytes 1572864 | tf_op jit(solution)/shard_map/reshape | solution.py:33
  109.5 4.7 %fusion.4 = f32[4,2,24,64,64]{3,4,2,1,0:T(8,128)S(1)} fusion(bf16[4,2,24,8,8,32]{5,2,4,1,3,0:T(8,128)(2,1)} %bitcast.79, bf16[4,2,24,8,8,32]{5,2,4,1,3,0:T(8,128)(2,1)} %bitcast.78), kind=kOutput, calls=%fused_computation.10 | convolution fusion | flops 50331648 | bytes 4718592 | tf_op jit(solution)/shard_map/abhqd,abhkd->abhqk/dot_general | solution.py:49
  114.2 2.6 %fusion.31 = (f32[4,2,24,64]{3,2,1,0:T(8,128)S(1)}, f32[4,2,24,64,64]{3,4,2,1,0:T(8,128)S(1)}) fusion(f32[4,2,24,64,64]{3,4,2,1,0:T(8,128)S(1)} %fusion.4, f32[24,64,64]{1,2,0:T(8,128)S(1)} %copy.49), kind=kOutput, calls=%fused_computation.54 | output fusion | flops 4718655 | bytes 6733824 | tf_op jit(solution)/shard_map/sub | solution.py:53
  117.8 2.8 %copy.53 = bf16[4,2,24,64,32]{4,3,2,1,0:T(8,128)(2,1)} copy(bf16[4,2,24,64,32]{3,4,2,1,0:T(8,128)(2,1)S(1)} %fusion.16) | data formatting | bytes 1572864 | tf_op jit(solution)/shard_map/convert_element_type | solution.py:55
  120.7 7.2 %copy.54 = bf16[4,8,2,8,24,32]{5,4,3,2,1,0:T(8,128)(2,1)} copy(bf16[4,8,2,8,24,32]{5,3,1,4,2,0:T(8,128)(2,1)} %bitcast.80) | data formatting | bytes 1572864 | tf_op jit(solution)/shard_map/transpose | solution.py:41
  127.9 4.2 %reshape.207 = bf16[32,16,768]{2,1,0:T(8,128)(2,1)S(1)} reshape(bf16[4,8,2,8,24,32]{5,4,3,2,1,0:T(8,128)(2,1)} %copy.54) | data formatting | bytes 1572864 | tf_op jit(solution)/shard_map/reshape | solution.py:41
  132.1 25.2 %all-gather.5.cloned.1.call-done = bf16[768,1536]{1,0:T(8,128)(2,1)} async-done(((bf16[24,1536]{1,0:T(8,128)(2,1)}), bf16[768,1536]{1,0:T(8,128)(2,1)}) %all-gather.5.cloned.1.call-update) | async-done | bytes 2359312 | tf_op jit(solution)/shard_map/all_gather | solution.py:100
  157.4 2.7 %fusion.21 = bf16[256,69]{0,1:T(8,128)(2,1)S(1)} fusion(bf16[1536,69]{0,1:T(8,128)(2,1)S(1)} %copy-done.7, bf16[768,1536]{1,0:T(8,128)(2,1)} %all-gather.5.cloned.1.call-done, bf16[1,32,8,1536]{3,2,1,0:T(8,128)(2,1)S(1)} %copy-done.1, bf16[32,16,768]{2,1,0:T(8,128)(2,1)S(1)} %reshape.207), kind=kOutput, calls=%fused_computation.30 | convolution fusion | flops 659440896 | bytes 3795456 | tf_op jit(solution)/shard_map/dot_general | solution.py:106
  162.4 9.6 %all-to-all-start = ((bf16[16,2,552]{2,1,0:T(2,128)(2,1)}), bf16[16,2,552]{2,1,0:T(2,128)(2,1)S(1)}, u32[]{:S(2)}, u32[]{:S(2)}) async-start(bf16[16,2,552]{2,1,0:T(2,128)(2,1)} %reshape.232), calls=%async_computation | async-start | bytes 81920 | tf_op jit(solution)/shard_map/all_to_all | solution.py:109
  172.0 8.2 %all-to-all-done = bf16[16,2,552]{2,1,0:T(2,128)(2,1)S(1)} async-done(((bf16[16,2,552]{2,1,0:T(2,128)(2,1)}), bf16[16,2,552]{2,1,0:T(2,128)(2,1)S(1)}, u32[]{:S(2)}, u32[]{:S(2)}) %all-to-all-start) | async-done | bytes 35360 | tf_op jit(solution)/shard_map/all_to_all | solution.py:109
  181.6 1.9 collective-permute-start.2
  183.5 5.8 %collective-permute-start.3 = (bf16[1,1,2,16,128]{4,3,2,1,0:T(8,128)(2,1)S(1)}, bf16[1,1,2,16,128]{4,3,2,1,0:T(8,128)(2,1)S(1)}, u32[]{:S(2)}, u32[]{:S(2)}) collective-permute-start(bf16[1,1,2,16,128]{4,3,2,1,0:T(8,128)(2,1)S(1)} %fusion.24), channel_id=1, source_target_pairs={{1,0},{2,1},{3,2},{4,3},{5,4},{6,5},{7,6},{8,7},{9,8},{10,9},{11,1... | collective-permute-start | bytes 24584 | tf_op jit(solution)/shard_map/ppermute | solution.py:20
  190.6 3.9 %collective-permute-start.4 = (bf16[1,3,2,16,128]{4,3,2,1,0:T(8,128)(2,1)S(1)}, bf16[1,3,2,16,128]{4,3,2,1,0:T(8,128)(2,1)S(1)}, u32[]{:S(2)}, u32[]{:S(2)}) collective-permute-start(bf16[1,3,2,16,128]{4,3,2,1,0:T(8,128)(2,1)S(1)} %pad_maximum_fusion.1), channel_id=1, source_target_pairs={{0,32},{32,64},{64,96},{96,128},{128,160},{160,192},{192,224},{224... | collective-permute-start | bytes 73736 | tf_op jit(solution)/shard_map/ppermute | solution.py:19
  194.5 2.0 collective-permute-start.5
  196.5 6.7 %collective-permute-done.5 = bf16[1,3,2,16,128]{4,3,2,1,0:T(8,128)(2,1)S(1)} collective-permute-done((bf16[1,3,2,16,128]{4,3,2,1,0:T(8,128)(2,1)S(1)}, bf16[1,3,2,16,128]{4,3,2,1,0:T(8,128)(2,1)S(1)}, u32[]{:S(2)}, u32[]{:S(2)}) %collective-permute-start.5) | collective-permute-done | bytes 24608 | tf_op jit(solution)/shard_map/ppermute | solution.py:20
  (58 shorter events, 15.0 us)
Async XLA Ops:
  6.5 197.3 %copy-start = (bf16[1,1,4,128,1104]{3,4,2,1,0:T(8,128)(2,1)S(1)}, bf16[1,1,4,128,1104]{3,4,2,1,0:T(8,128)(2,1)}, u32[]{:S(2)}) copy-start(bf16[1,1,4,128,1104]{3,4,2,1,0:T(8,128)(2,1)} %param.23) | copy-start | bytes 3391492
  6.5 17.5 %copy-start.1 = (bf16[1,32,8,1536]{3,2,1,0:T(8,128)(2,1)S(1)}, bf16[1,32,8,1536]{3,2,1,0:T(8,128)(2,1)}, u32[]{:S(2)}) copy-start(bf16[1,32,8,1536]{3,2,1,0:T(8,128)(2,1)} %param.12) | copy-start | bytes 2359300
  6.5 13.3 %copy-start.8 = (s32[1,1,4]{2,1,0:T(1,128)S(1)}, s32[1,1,4]{2,1,0:T(1,128)}, u32[]{:S(2)}) copy-start(s32[1,1,4]{2,1,0:T(1,128)} %param.21) | copy-start | bytes 52
  6.5 13.4 %copy-start.5 = (s32[1,1,2,128]{3,2,1,0:T(2,128)S(1)}, s32[1,1,2,128]{3,2,1,0:T(2,128)}, u32[]{:S(2)}) copy-start(s32[1,1,2,128]{3,2,1,0:T(2,128)} %param.20) | copy-start | bytes 3076
  6.5 81.5 %all-gather.3.cloned.1.call-start = ((), (), s32[]{:S(2)}) async-start(), calls=%async_computation.1 | async-start | bytes 7299072 | tf_op jit(solution)/shard_map/all_gather | solution.py:86
  7.3 150.1 %all-gather.5.cloned.1.call-start = ((), (), s32[]{:S(2)}) async-start(), calls=%async_computation.2 | async-start | bytes 2433024 | tf_op jit(solution)/shard_map/all_gather | solution.py:100
  9.9 12.3 %collective-permute-start = (bf16[32,4,1536]{2,1,0:T(4,128)(2,1)}, bf16[32,4,1536]{2,1,0:T(4,128)(2,1)S(1)}, u32[]{:S(2)}, u32[]{:S(2)}) collective-permute-start(bf16[32,4,1536]{2,1,0:T(4,128)(2,1)} %get-tuple-element.8), channel_id=1, source_target_pairs={{0,1},{1,2},{2,3},{3,4},{4,5},{5,6},{6,7},{7,8},{8,9},{9,10},{10,1... | collective-permute-start | bytes 1179656 | tf_op jit(solution)/shard_map/ppermute | solution.py:19
  11.8 12.2 %collective-permute-start.1 = (bf16[32,4,1536]{2,1,0:T(4,128)(2,1)}, bf16[32,4,1536]{2,1,0:T(4,128)(2,1)S(1)}, u32[]{:S(2)}, u32[]{:S(2)}) collective-permute-start(bf16[32,4,1536]{2,1,0:T(4,128)(2,1)} %get-tuple-element.9), channel_id=1, source_target_pairs={{1,0},{2,1},{3,2},{4,3},{5,4},{6,5},{7,6},{8,7},{9,8},{10,9},{11,1... | collective-permute-start | bytes 1179656 | tf_op jit(solution)/shard_map/ppermute | solution.py:20
  24.9 2.0 copy-start.4
  114.2 2.7 %copy-start.2 = (bf16[4,8,2,8,24,32]{5,4,3,2,1,0:T(8,128)(2,1)S(1)}, bf16[4,8,2,8,24,32]{5,4,3,2,1,0:T(8,128)(2,1)}, u32[]{:S(2)}) copy-start(bf16[4,8,2,8,24,32]{5,4,3,2,1,0:T(8,128)(2,1)} %reshape.204) | copy-start | bytes 2359300
  127.9 29.5 %copy-start.7 = (bf16[1536,69]{0,1:T(8,128)(2,1)S(1)}, bf16[1536,69]{0,1:T(8,128)(2,1)}, u32[]{:S(2)}) copy-start(bf16[1536,69]{0,1:T(8,128)(2,1)} %param.17) | copy-start | bytes 635908
  132.1 49.4 %copy-start.3 = (f32[16,1,1,2,128]{4,3,2,1,0:T(2,128)S(1)}, f32[16,1,1,2,128]{4,3,2,1,0:T(2,128)}, u32[]{:S(2)}) copy-start(f32[16,1,1,2,128]{4,3,2,1,0:T(2,128)} %param.19) | copy-start | bytes 49156
  132.1 49.4 %copy-start.6 = (f32[1,1,2,128]{3,2,1,0:T(2,128)S(1)}, f32[1,1,2,128]{3,2,1,0:T(2,128)}, u32[]{:S(2)}) copy-start(f32[1,1,2,128]{3,2,1,0:T(2,128)} %param.18) | copy-start | bytes 3076
  162.4 17.8 %all-to-all-start = ((bf16[16,2,552]{2,1,0:T(2,128)(2,1)}), bf16[16,2,552]{2,1,0:T(2,128)(2,1)S(1)}, u32[]{:S(2)}, u32[]{:S(2)}) async-start(bf16[16,2,552]{2,1,0:T(2,128)(2,1)} %reshape.232), calls=%async_computation | async-start | bytes 81920 | tf_op jit(solution)/shard_map/all_to_all | solution.py:109
  181.6 8.4 %collective-permute-start.2 = (bf16[1,1,2,16,128]{4,3,2,1,0:T(8,128)(2,1)S(1)}, bf16[1,1,2,16,128]{4,3,2,1,0:T(8,128)(2,1)S(1)}, u32[]{:S(2)}, u32[]{:S(2)}) collective-permute-start(bf16[1,1,2,16,128]{4,3,2,1,0:T(8,128)(2,1)S(1)} %fusion.24), channel_id=1, source_target_pairs={{0,1},{1,2},{2,3},{3,4},{4,5},{5,6},{6,7},{7,8},{8,9},{9,10},{10,1... | collective-permute-start | bytes 24584 | tf_op jit(solution)/shard_map/ppermute | solution.py:19
  183.5 7.1 %collective-permute-start.3 = (bf16[1,1,2,16,128]{4,3,2,1,0:T(8,128)(2,1)S(1)}, bf16[1,1,2,16,128]{4,3,2,1,0:T(8,128)(2,1)S(1)}, u32[]{:S(2)}, u32[]{:S(2)}) collective-permute-start(bf16[1,1,2,16,128]{4,3,2,1,0:T(8,128)(2,1)S(1)} %fusion.24), channel_id=1, source_target_pairs={{1,0},{2,1},{3,2},{4,3},{5,4},{6,5},{7,6},{8,7},{9,8},{10,9},{11,1... | collective-permute-start | bytes 24584 | tf_op jit(solution)/shard_map/ppermute | solution.py:20
  190.6 5.9 %collective-permute-start.4 = (bf16[1,3,2,16,128]{4,3,2,1,0:T(8,128)(2,1)S(1)}, bf16[1,3,2,16,128]{4,3,2,1,0:T(8,128)(2,1)S(1)}, u32[]{:S(2)}, u32[]{:S(2)}) collective-permute-start(bf16[1,3,2,16,128]{4,3,2,1,0:T(8,128)(2,1)S(1)} %pad_maximum_fusion.1), channel_id=1, source_target_pairs={{0,32},{32,64},{64,96},{96,128},{128,160},{160,192},{192,224},{224... | collective-permute-start | bytes 73736 | tf_op jit(solution)/shard_map/ppermute | solution.py:19
  194.5 8.7 %collective-permute-start.5 = (bf16[1,3,2,16,128]{4,3,2,1,0:T(8,128)(2,1)S(1)}, bf16[1,3,2,16,128]{4,3,2,1,0:T(8,128)(2,1)S(1)}, u32[]{:S(2)}, u32[]{:S(2)}) collective-permute-start(bf16[1,3,2,16,128]{4,3,2,1,0:T(8,128)(2,1)S(1)} %pad_maximum_fusion.1), channel_id=1, source_target_pairs={{32,0},{64,32},{96,64},{128,96},{160,128},{192,160},{224,192},{256... | collective-permute-start | bytes 73736 | tf_op jit(solution)/shard_map/ppermute | solution.py:20
Sparse Core Ops, SparseCore 0:
  9.5 78.5 all-gather.2
  90.2 67.1 all-gather.4
where the time goes:
time: 212 us
  waiting for transfers between devices  105 us (50%)
  local copies, waits for them, and re-layouts  35.6 us (17%)
  starting transfers between devices  31.7 us (15%)
  matrix products  16.7 us (8%)
  between operations  14.4 us (7%)
  other arithmetic  8.11 us (4%)
    all_gather x1, waiting for transfers between devices, body(): lax.all_gather(w_qkv, 'space', axis=0, tiled=True)  59.5 us
    all_gather x1, waiting for transfers between devices, body(): lax.all_gather(w_out, 'space', axis=0, tiled=True)  25.2 us
    ppermute x3, starting transfers between devices, padded(): after = lax.ppermute(initial, axis, down)  14.3 us
    reshape x3, local copies, waits for them, and re-layouts, to_windows(): array.reshape(lat_count // WIN, WIN, col_count // WIN, WIN, HEADS, HS)  12.8 us
    all_to_all x1, starting transfers between devices, body(): lax.all_to_all(outgoing.astype(jnp.bfloat16), 'member', split_axis=1, con...  9.61 us
    ppermute x3, waiting for transfers between devices, padded(): after = lax.ppermute(initial, axis, down)  9.26 us
    all_to_all x1, waiting for transfers between devices, body(): lax.all_to_all(outgoing.astype(jnp.bfloat16), 'member', split_axis=1, con...  8.17 us
    ppermute x3, starting transfers between devices, padded(): before = lax.ppermute(last, axis, up)  7.69 us
  transfers between devices with their start and end apart: 9, of which 7 were waited for; matrix products, arithmetic and copies ran while one was open for 25% of the time, Pallas kernels for 0%

commit v1 on v0

v1 whole, which is shorter than its diff:
```python
import jax
import jax.numpy as jnp
import numpy as np
from jax import lax
from jax.experimental import pallas as pl
from jax.experimental.pallas import tpu as pltpu
from jax.sharding import Mesh, PartitionSpec as P

HEADS = 24
HS = 32
WIN = 8
SHIFT = 4
CH = 69
MEMBER = ("zhi", "x")
SPACE = ("zlo", "y", "core")
ROW = ("y", "core")
GROUP_HEADS = 12
GF = GROUP_HEADS * HS
WCOLS = 3 * GF + 128
F32 = jnp.float32
BF16 = jnp.bfloat16
NT = (((1,), (1,)), ((), ()))
VMEM_LIMIT = 48 * 1024 * 1024


def dot(a, b, dims=(((1,), (0,)), ((), ()))):
    return lax.dot_general(a, b, dims, preferred_element_type=F32)


def weights_kernel(group_ref, w_qkv_ref, w_out_ref, w_decode_ref, out_ref):
    for group in range(2):

        @pl.when(group_ref[0] == group)
        def _():
            for part in range(3):
                out_ref[:, part * GF : (part + 1) * GF] = w_qkv_ref[
                    :, (2 * part + group) * GF : (2 * part + group + 1) * GF
                ]

    folded = dot(w_out_ref[...], w_decode_ref[...], NT)
    rows, channels = folded.shape
    wide = jnp.concatenate([folded, jnp.zeros((rows, 128 - channels), F32)], axis=1)
    full = jnp.concatenate([wide, jnp.zeros((out_ref.shape[0] - rows, 128), F32)], axis=0)
    out_ref[:, 3 * GF :] = full.astype(BF16)


def norm_kernel(tokens_ref, halo_ref, gain_ref, w_decode_ref, normed_ref, residual_ref):
    own = tokens_ref[0].astype(F32)
    halo = halo_ref[...].astype(F32)
    features = own.shape[-1]
    halo = halo.reshape(WIN // 2, WIN, features)
    halo = jnp.stack([pltpu.roll(halo, 4, axis=1), halo], axis=1).reshape(WIN, WIN, features)
    spot = lax.broadcasted_iota(jnp.int32, (WIN, WIN, features), 1)
    window = jnp.where(spot < SHIFT, pltpu.roll(own, 4, axis=1), halo).reshape(WIN * WIN, features)
    center = jnp.mean(window, axis=-1, keepdims=True)
    spread = jnp.mean((window - center) ** 2, axis=-1, keepdims=True)
    normed = (window - center) * lax.rsqrt(spread + 1e-05) * gain_ref[...]
    normed_ref[...] = normed.astype(BF16)
    residual = dot(window.astype(BF16), w_decode_ref[...], NT)
    residual_ref[...] = jnp.concatenate(
        [residual, jnp.zeros((WIN * WIN, 128 - CH), F32)], axis=1
    )


def attention_kernel(
    group_ref,
    own_ref,
    mate_ref,
    residual_ref,
    weights_hbm,
    bias_ref,
    value_ref,
    pick_ref,
    both_ref,
    right_ref,
    left_ref,
    weights,
    qkv,
    fields,
    sums,
    sems,
):
    copies = []
    for block in range(16):
        for low in range(2):
            copies.append(
                pltpu.make_async_copy(
                    weights_hbm.at[pl.ds((block * 2 + low) * 48, 48)],
                    weights.at[pl.ds((low * 16 + block) * 48, 48)],
                    sems.at[block * 2 + low],
                )
            )
    for copy in copies:
        copy.start()
    for copy in copies:
        copy.wait()
    for member, source in enumerate((own_ref, mate_ref)):
        for part in range(3):
            lanes = slice(part * GF, (part + 1) * GF)
            qkv[member * 256 : (member + 1) * 256, lanes] = dot(source[...], weights[:, lanes]).astype(BF16)
    first = pl.multiple_of(group_ref[0] * 768, 768)
    folded = jnp.concatenate(
        [
            weights[pl.ds(pl.multiple_of(first + 48 * t, 48), 48), 3 * GF :].astype(F32)[:24]
            for t in range(16)
        ],
        axis=0,
    )
    folded_t = [folded[128 * j : 128 * (j + 1)].T.astype(BF16) for j in range(3)]
    head_of_row = lax.broadcasted_iota(jnp.int32, (256, 128), 0) // 64
    head_of_lane = lax.broadcasted_iota(jnp.int32, (256, 128), 1) // 32
    block_mask = head_of_row == head_of_lane
    lane = lax.broadcasted_iota(jnp.int32, (128, 128), 1)
    zero = jnp.zeros((64, 128), BF16)

    def spread_heads(tile):
        return jnp.where(block_mask, jnp.concatenate([tile] * 4, axis=0), jnp.zeros((256, 128), BF16))

    for pair in range(4):
        row_a, row_b = (128 * pair, 128 * pair + 64)
        total = None
        for j in range(3):
            def part_of(part, row):
                return qkv[row : row + 64, part * GF + 128 * j : part * GF + 128 * (j + 1)]

            query = jnp.concatenate(
                [
                    jnp.concatenate([part_of(0, row_a), zero], axis=1),
                    jnp.concatenate([zero, part_of(0, row_b)], axis=1),
                ],
                axis=0,
            )
            key = jnp.concatenate(
                [spread_heads(part_of(1, row_a)), spread_heads(part_of(1, row_b))], axis=1
            )
            scores = dot(key, query, NT) * HS ** (-0.5) + bias_ref[256 * j : 256 * (j + 1)]
            scores = scores.reshape(4, 64, 128)
            powers = jnp.exp(scores - jnp.max(scores, axis=1, keepdims=True))
            chances = powers * (1.0 / jnp.sum(powers, axis=1, keepdims=True))
            chances = chances.reshape(256, 128).astype(BF16)
            value = jnp.concatenate(
                [
                    dot(folded_t[j], spread_heads(part_of(2, row_a)), NT),
                    dot(folded_t[j], spread_heads(part_of(2, row_b)), NT),
                ],
                axis=0,
            ).astype(BF16)
            term = dot(value, chances)
            total = term if total is None else total + term
        decoded = jnp.where(lane < 64, total[:128], total[128:]).T
        if pair < 2:
            decoded = decoded + residual_ref[128 * pair : 128 * (pair + 1)]
        fields[128 * pair : 128 * (pair + 1)] = decoded
    cell = lax.broadcasted_iota(jnp.int32, (8, 128), 0)
    for tile in range(16):
        for block in range(2):
            row = 2 * tile + block
            for side in range(2):
                channel = jnp.broadcast_to(pick_ref[64 * side + row : 64 * side + row + 1], (8, 128))
                place = jnp.broadcast_to(pick_ref[64 * side + 32 + row : 64 * side + 32 + row + 1], (8, 128))
                for member in range(2):
                    found = None
                    for line in range(2):
                        at = member * 256 + 16 * tile + 8 * line
                        gathered = jnp.take_along_axis(fields[at : at + 8], channel, axis=1)
                        kept = jnp.where(place == cell + 8 * line, gathered, 0.0)
                        found = kept if found is None else found + kept
                    found = -jnp.sum(found, axis=0, keepdims=True)
                    if side == 0 and member == 0:
                        found = found + value_ref[row : row + 1]
                    sums[32 * side + row : 32 * side + row + 1, 128 * member : 128 * (member + 1)] = found
    both = sums[...].astype(BF16)
    both_ref[...] = both
    right_ref[...] = both[:32]
    left_ref[...] = both[32:]


def select_kernel(own_ref, prev_ref, next_ref, second_ref, choice_ref, out_ref):
    table = jnp.concatenate(
        [prev_ref[:32], own_ref[:32], next_ref[...], second_ref[...], prev_ref[32:], own_ref[32:]], axis=0
    )
    table = jnp.concatenate([table[:, :128], table[:, 128:]], axis=0)
    out_ref[...] = dot(choice_ref[...], table).astype(BF16).reshape(16, 8, 128)


def update_kernel(arrived_ref, gains_ref, out_ref):
    row = lax.broadcasted_iota(jnp.int32, (64, 128), 0)
    col = lax.broadcasted_iota(jnp.int32, (64, 128), 1)
    entry, member = (row // 16, row % 16)
    source, pair, source_entry = (col // 8, (col // 4) % 2, col % 4)
    same = (entry == source_entry) & ((source ^ pair) == member)
    gather = jnp.where(same, 1.0, 0.0).astype(BF16)
    chosen = dot(gather, arrived_ref[...].reshape(128, 128)).astype(BF16)
    total = None
    for j in range(4):
        term = dot(chosen[16 * j : 16 * (j + 1)], gains_ref[j], NT)
        total = term if total is None else total + term
    out_ref[...] = total


def shift(x, by):
    peers = lax.axis_size(SPACE)
    return lax.ppermute(x, SPACE, [(i, (i + by) % peers) for i in range(peers)])


def smem():
    return pl.BlockSpec(memory_space=pltpu.SMEM)


def vmem():
    return pl.BlockSpec(memory_space=pltpu.VMEM)


def params():
    return pltpu.CompilerParams(vmem_limit_bytes=VMEM_LIMIT)


def body(
    tokens,
    norm_gain,
    w_qkv,
    w_out,
    rel_bias,
    w_decode,
    obs_value,
    obs_pert,
    obs_index,
    block_list,
    list_count,
    gains,
):
    features = tokens.shape[3]
    group = (lax.axis_index("x") % 2).astype(jnp.int32)
    low = lax.axis_index("zlo")
    w_decode_t = w_decode.T

    rows = pl.pallas_call(
        weights_kernel,
        out_shape=jax.ShapeDtypeStruct((w_qkv.shape[0], WCOLS), BF16),
        in_specs=[smem(), vmem(), vmem(), vmem()],
        out_specs=vmem(),
        compiler_params=params(),
        name="weights",
    )(group.reshape(1), w_qkv, w_out, w_decode_t)
    other_rows = lax.ppermute(rows, "zlo", [(0, 1), (1, 0)])
    both_rows = jnp.where(
        low == 0,
        jnp.concatenate([rows, other_rows], axis=0),
        jnp.concatenate([other_rows, rows], axis=0),
    )
    gathered = lax.all_gather(both_rows, ROW, axis=0, tiled=True)

    left_half = tokens[0, :, :SHIFT].reshape(-1, features)
    halo = shift(left_half, -1)
    normed, residual = pl.pallas_call(
        norm_kernel,
        grid=(4,),
        out_shape=(
            jax.ShapeDtypeStruct((256, features), BF16),
            jax.ShapeDtypeStruct((256, 128), F32),
        ),
        in_specs=[
            pl.BlockSpec((1, WIN, WIN, features), lambda i: (0, i, 0, 0)),
            pl.BlockSpec((WIN * SHIFT, features), lambda i: (i, 0)),
            pl.BlockSpec((1, features), lambda i: (0, 0)),
            pl.BlockSpec(w_decode_t.shape, lambda i: (0, 0)),
        ],
        out_specs=(
            pl.BlockSpec((64, features), lambda i: (i, 0)),
            pl.BlockSpec((64, 128), lambda i: (i, 0)),
        ),
        compiler_params=params(),
        name="norm",
    )(tokens, halo, norm_gain.reshape(1, -1), w_decode_t)
    mate = lax.ppermute(normed, "x", [(0, 1), (1, 0), (2, 3), (3, 2)])

    expected = obs_value[0, 0][None] + obs_pert[:, 0, 0]
    entries = block_list.shape[2]
    lists = jnp.concatenate([block_list[0, 0], list_count[0], jnp.zeros((128 - entries - 1,), jnp.int32)])
    notes = jnp.concatenate([obs_index[0, 0], lists[None]], axis=0).astype(F32)
    outgoing = jnp.concatenate([expected, jnp.broadcast_to(notes[None], (16, 3, 128))], axis=1)
    observed = lax.all_to_all(outgoing, MEMBER, split_axis=0, concat_axis=0, tiled=True)
    expected = observed[:, :2].reshape(32, 128)
    index_f = observed[:, 2:4].reshape(32, 128)
    index_next = shift(index_f, -1).astype(jnp.int32)
    index = index_f.astype(jnp.int32)

    def decode(index, side):
        line, rest = (index // (WIN * CH), index % (WIN * CH))
        column, channel = (rest // CH, rest % CH)
        here = (column >= SHIFT) if side == 0 else (column < SHIFT)
        place = line * WIN + (column + SHIFT) % WIN
        return [channel, jnp.where(here, place, -1)]

    picks = jnp.concatenate(decode(index, 0) + decode(index_next, 1), axis=0)
    meta = observed[:, 4].astype(jnp.int32)
    listed, count = (meta[:, :entries], meta[:, entries : entries + 1])
    tile_row = jnp.arange(16)[:, None] + listed // 6 - 1
    live = (jnp.arange(entries)[None] < count) & (tile_row >= 0) & (tile_row < 16)
    table_row = jnp.where(live, (listed // 2 % 3) * 32 + tile_row * 2 + listed % 2, -1000)
    table_row = (table_row[:, None, :] + 192 * jnp.arange(2)[None, :, None]).reshape(128, 1)
    table_col = jnp.arange(384)[None]
    choice = ((table_col == table_row) | (table_col == table_row + 96)).astype(BF16)

    bias = lax.dynamic_slice_in_dim(rel_bias, group * GROUP_HEADS, GROUP_HEADS, axis=0)
    bias = bias.transpose(0, 2, 1).reshape(GROUP_HEADS * 64, 64)
    bias = jnp.concatenate([bias, bias], axis=1)

    both, right, left = pl.pallas_call(
        attention_kernel,
        out_shape=(
            jax.ShapeDtypeStruct((64, 256), BF16),
            jax.ShapeDtypeStruct((32, 256), BF16),
            jax.ShapeDtypeStruct((32, 256), BF16),
        ),
        in_specs=[
            smem(),
            vmem(),
            vmem(),
            vmem(),
            pl.BlockSpec(memory_space=pl.ANY),
            vmem(),
            vmem(),
            vmem(),
        ],
        out_specs=(vmem(), vmem(), vmem()),
        scratch_shapes=[
            pltpu.VMEM((features, WCOLS), BF16),
            pltpu.VMEM((512, 3 * GF), BF16),
            pltpu.VMEM((512, 128), F32),
            pltpu.VMEM((64, 256), F32),
            pltpu.SemaphoreType.DMA((32,)),
        ],
        compiler_params=params(),
        name="attention",
    )(group.reshape(1), normed, mate, residual, gathered, bias, expected, picks)

    previous, following, second = (shift(both, 1), shift(right, -1), shift(left, 2))
    selected = pl.pallas_call(
        select_kernel,
        out_shape=jax.ShapeDtypeStruct((16, 8, 128), BF16),
        in_specs=[vmem()] * 5,
        out_specs=vmem(),
        compiler_params=params(),
        name="select",
    )(both, previous, following, second, choice)
    arrived = lax.all_to_all(selected, MEMBER, split_axis=0, concat_axis=0, tiled=True)
    gains_t = gains[0, 0].transpose(0, 2, 1)
    increment = pl.pallas_call(
        update_kernel,
        out_shape=jax.ShapeDtypeStruct((16, gains.shape[4]), F32),
        in_specs=[vmem(), vmem()],
        out_specs=vmem(),
        compiler_params=params(),
        name="update",
    )(arrived, gains_t)
    return increment[None, None]


def solution(mesh):
    fine = Mesh(np.asarray(mesh.devices).reshape(4, 4, 2, 8, 2), ("zhi", "x", "zlo", "y", "core"))
    in_specs = (
        P(MEMBER, None, SPACE, None),
        P(),
        P(SPACE, None),
        P(SPACE, None),
        P(),
        P(),
        P(MEMBER, SPACE, None, None),
        P(None, MEMBER, SPACE, None, None),
        P(MEMBER, SPACE, None, None),
        P(MEMBER, SPACE, None),
        P(MEMBER, SPACE),
        P(MEMBER, SPACE, None, None, None),
    )
    out_specs = P(MEMBER, SPACE, None, None)
    return jax.shard_map(body, mesh=fine, in_specs=in_specs, out_specs=out_specs, check_vma=False)
```

time: 212 us -> 133 us (0.63)
  waiting for transfers between devices: 105 us -> 32.8 us
  local copies, waits for them, and re-layouts: 35.6 us -> 10.3 us
  blocking collectives: 0 us -> 17.9 us
  matrix products: 16.7 us -> 0 us
  Pallas kernels: 0 us -> 15.1 us
  starting transfers between devices: 31.7 us -> 37.9 us
  other arithmetic: 8.11 us -> 3.44 us
    all_gather x2 -> x1, waiting for transfers between devices: 84.8 us -> 0.01 us  [body(): gathered = lax.all_gather(both_rows, ROW, axis=0, tiled=True)]
    ppermute x6 -> x7, waiting for transfers between devices: 11.5 us -> 31.4 us  [the longest x1 14.5 us: body(): mate = lax.ppermute(normed, 'x', [(0, 1), (1, 0), (2, 3), (3, 2)])]
    all_to_all x0 -> x1, blocking collectives: none -> 17.9 us  [body(): lax.all_to_all(selected, MEMBER, split_axis=0, concat_axis=0, tiled=True)]
    reshape x5 -> x1, local copies, waits for them, and re-layouts: 17.1 us -> 0.01 us  [body(): norm_gain.reshape(1, -1)]
    dot_general x5 -> x0, matrix products: 16.7 us -> none  [the longest x1 7.31 us: body(): jnp.dot(left_cols, lax.all_gather(w_qkv, 'space', axis=0, tiled=True), pr...]
    pallas_call x0 -> x5, Pallas kernels: none -> 15.1 us  [the longest x1 10.9 us: body(): pl.pallas_call(attention_kernel, out_shape=(jax.ShapeDtypeStruct((64, 256...]
    transpose x1 -> x2, local copies, waits for them, and re-layouts: 7.23 us -> 0.2 us  [body(): bias = bias.transpose(0, 2, 1).reshape(GROUP_HEADS * 64, 64)]
    all_to_all x1, waiting for transfers between devices: 8.17 us -> 1.41 us  [body(): lax.all_to_all(outgoing, MEMBER, split_axis=0, concat_axis=0, tiled=True)]
  transfers between devices with their start and end apart: 9 -> 9, of which waited for: 7 -> 5; matrix products, arithmetic and copies ran while one was open for 25% -> 5% of each run, Pallas kernels for 0% -> 2%
where the time goes in v1:
time: 133 us; the launch traced here: 132 us
  starting transfers between devices  37.9 us (28%)
  waiting for transfers between devices  32.8 us (25%)
  blocking collectives  17.9 us (13%)
  Pallas kernels  15.1 us (11%)
  between operations  14.3 us (11%)
  local copies, waits for them, and re-layouts  10.3 us (8%)
  other arithmetic  3.44 us (3%)
    ppermute x5, starting transfers between devices, shift(): return lax.ppermute(x, SPACE, [(i, (i + by) % peers) for i in range(peers)])  18.3 us
    all_to_all x1, blocking collectives, body(): lax.all_to_all(selected, MEMBER, split_axis=0, concat_axis=0, tiled=True)  17.9 us
    ppermute x1, waiting for transfers between devices, body(): mate = lax.ppermute(normed, 'x', [(0, 1), (1, 0), (2, 3), (3, 2)])  14.5 us
    ppermute x5, waiting for transfers between devices, shift(): return lax.ppermute(x, SPACE, [(i, (i + by) % peers) for i in range(peers)])  13.6 us
    all_to_all x1, starting transfers between devices, body(): lax.all_to_all(outgoing, MEMBER, split_axis=0, concat_axis=0, tiled=True)  12.6 us
    pallas_call x1, Pallas kernels, body(): pl.pallas_call(attention_kernel, out_shape=(jax.ShapeDtypeStruct((64, 256...  10.9 us
    unnamed x22, local copies, waits for them, and re-layouts  7.02 us
    ppermute x1, starting transfers between devices, body(): other_rows = lax.ppermute(rows, 'zlo', [(0, 1), (1, 0)])  4.3 us
  transfers between devices with their start and end apart: 9, of which 5 were waited for; matrix products, arithmetic and copies ran while one was open for 5% of the time, Pallas kernels for 2%

profile of v1, /device:TPU:6, one launch (start us, length us, event | category | flops | bytes accessed | tf_op | source)
XLA Modules:
  0.0 131.7 jit_solution(6783575727548989900)
XLA Ops:
  6.5 1.0 copy-done.4
  7.6 0.9 copy-done.8
  8.5 0.9 copy-done.9
  9.6 4.3 %collective-permute-start.2 = (bf16[48,1280]{1,0:T(8,128)(2,1)S(1)}, bf16[48,1280]{1,0:T(8,128)(2,1)S(1)}, u32[]{:S(2)}, u32[]{:S(2)}) collective-permute-start(bf16[48,1280]{1,0:T(8,128)(2,1)S(1)} %weights.1), channel_id=1, source_target_pairs={{0,16},{16,0},{1,17},{17,1},{2,18},{18,2},{3,19},{19,3},{4,20},{20... | collective-permute-start | bytes 368648 | tf_op jit(solution)/shard_map/ppermute | solution.py:245
  13.9 3.3 %collective-permute-done.2 = bf16[48,1280]{1,0:T(8,128)(2,1)S(1)} collective-permute-done((bf16[48,1280]{1,0:T(8,128)(2,1)S(1)}, bf16[48,1280]{1,0:T(8,128)(2,1)S(1)}, u32[]{:S(2)}, u32[]{:S(2)}) %collective-permute-start.2) | collective-permute-done | bytes 122912 | tf_op jit(solution)/shard_map/ppermute | solution.py:245
  21.4 12.6 %all-to-all-start = ((f32[16,5,128]{2,1,0:T(8,128)}), f32[16,5,128]{2,1,0:T(8,128)S(1)}, u32[]{:S(2)}, u32[]{:S(2)}) async-start(f32[16,5,128]{2,1,0:T(8,128)} %copy.28), calls=%async_computation | async-start | bytes 131072 | tf_op jit(solution)/shard_map/all_to_all | solution.py:282
  34.1 1.2 slice.18
  36.1 4.3 %collective-permute-start = (bf16[128,1536]{1,0:T(8,128)(2,1)}, bf16[128,1536]{1,0:T(8,128)(2,1)}, u32[]{:S(2)}, u32[]{:S(2)}) collective-permute-start(bf16[128,1536]{1,0:T(8,128)(2,1)} %reshape_squeeze.3), channel_id=1, source_target_pairs={{0,31},{1,0},{2,1},{3,2},{4,3},{5,4},{6,5},{7,6},{8,7},{9,8},{10,9... | collective-permute-start | bytes 1179656 | tf_op jit(solution)/shard_map/ppermute | solution.py:203
  40.9 1.4 %all-to-all-done = f32[16,5,128]{2,1,0:T(8,128)S(1)} async-done(((f32[16,5,128]{2,1,0:T(8,128)}), f32[16,5,128]{2,1,0:T(8,128)S(1)}, u32[]{:S(2)}, u32[]{:S(2)}) %all-to-all-start) | async-done | bytes 40992 | tf_op jit(solution)/shard_map/all_to_all | solution.py:282
  42.3 3.3 %collective-permute-start.3 = (f32[32,128]{1,0:T(8,128)S(1)}, f32[32,128]{1,0:T(8,128)S(1)}, u32[]{:S(2)}, u32[]{:S(2)}) collective-permute-start(f32[32,128]{1,0:T(8,128)S(1)} %bitcast.28), channel_id=1, source_target_pairs={{0,31},{1,0},{2,1},{3,2},{4,3},{5,4},{6,5},{7,6},{8,7},{9,8},{10,9... | collective-permute-start | bytes 49160 | tf_op jit(solution)/shard_map/ppermute | solution.py:203
  46.1 7.9 %collective-permute-done.halo_ref = bf16[128,1536]{1,0:T(8,128)(2,1)} collective-permute-done((bf16[128,1536]{1,0:T(8,128)(2,1)}, bf16[128,1536]{1,0:T(8,128)(2,1)}, u32[]{:S(2)}, u32[]{:S(2)}) %collective-permute-start) | collective-permute-done | bytes 393248 | tf_op jit(solution)/shard_map/ppermute | solution.py:203
  54.0 2.7 %norm.1 = (bf16[256,1536]{1,0:T(8,128)(2,1)S(1)}, f32[256,128]{1,0:T(8,128)S(1)}) custom-call(bf16[1,32,8,1536]{3,2,1,0:T(8,128)(2,1)S(1)} %copy-done.2, bf16[128,1536]{1,0:T(8,128)(2,1)} %collective-permute-done.halo_ref, f32[1,1536]{1,0:T(1,128)S(1)} %reshape.68.gain_ref, bf16[69,1536]{1,0:T(8,128)(2,1)S(1)} %bitcast.23), custom_call_target="tpu_custom_call" | custom-call | tf_op jit(solution)/shard_map/norm/pallas_call | solution.py:255
  56.6 2.7 %collective-permute-start.1 = (bf16[256,1536]{1,0:T(8,128)(2,1)S(1)}, bf16[256,1536]{1,0:T(8,128)(2,1)S(1)}, u32[]{:S(2)}, u32[]{:S(2)}) collective-permute-start(bf16[256,1536]{1,0:T(8,128)(2,1)S(1)} %get-tuple-element.10.own_ref), channel_id=1, source_target_pairs={{0,32},{32,0},{64,96},{96,64},{1,33},{33,1},{65,97},{97,65},{2,34}... | collective-permute-start | bytes 2359304 | tf_op jit(solution)/shard_map/ppermute | solution.py:275
  59.4 0.9 copy-done.6
  60.4 14.5 %collective-permute-done.1.mate_ref = bf16[256,1536]{1,0:T(8,128)(2,1)S(1)} collective-permute-done((bf16[256,1536]{1,0:T(8,128)(2,1)S(1)}, bf16[256,1536]{1,0:T(8,128)(2,1)S(1)}, u32[]{:S(2)}, u32[]{:S(2)}) %collective-permute-start.1) | collective-permute-done | bytes 786464 | tf_op jit(solution)/shard_map/ppermute | solution.py:275
  75.0 2.1 %copy-done.1 = bf16[1536,1280]{1,0:T(8,128)(2,1)S(1)} copy-done((bf16[1536,1280]{1,0:T(8,128)(2,1)S(1)}, bf16[1536,1280]{1,0:T(8,128)(2,1)}, u32[]{:S(2)}) %copy-start.1) | copy-done | bytes 3932184
  77.1 1.1 copy-done.7
  78.2 10.9 %attention.1 = (bf16[64,256]{1,0:T(8,128)(2,1)S(1)}, bf16[32,256]{1,0:T(8,128)(2,1)S(1)}, bf16[32,256]{1,0:T(8,128)(2,1)S(1)}) custom-call(s32[1]{0:T(128)} %bitcast.group_ref, bf16[256,1536]{1,0:T(8,128)(2,1)S(1)} %copy-done.7, bf16[256,1536]{1,0:T(8,128)(2,1)S(1)} %collective-permute-done.1.mate_ref, f32[256,128]{1,0:T(8,128)S(1)} %get-tuple-element.11.residual_ref, ...), custom_call_target="tpu_custom_call" | custom-call | tf_op jit(solution)/shard_map/attention/pallas_call | solution.py:309
  89.1 1.9 %collective-permute-start.4 = (bf16[64,256]{1,0:T(8,128)(2,1)S(1)}, bf16[64,256]{1,0:T(8,128)(2,1)S(1)}, u32[]{:S(2)}, u32[]{:S(2)}) collective-permute-start(bf16[64,256]{1,0:T(8,128)(2,1)S(1)} %get-tuple-element.12.own_ref), channel_id=1, source_target_pairs={{0,1},{1,2},{2,3},{3,4},{4,5},{5,6},{6,7},{7,8},{8,9},{9,10},{10,1... | collective-permute-start | bytes 98312 | tf_op jit(solution)/shard_map/ppermute | solution.py:203
  91.0 6.8 %collective-permute-start.5 = (bf16[32,256]{1,0:T(8,128)(2,1)S(1)}, bf16[32,256]{1,0:T(8,128)(2,1)S(1)}, u32[]{:S(2)}, u32[]{:S(2)}) collective-permute-start(bf16[32,256]{1,0:T(8,128)(2,1)S(1)} %get-tuple-element.13), channel_id=1, source_target_pairs={{0,31},{1,0},{2,1},{3,2},{4,3},{5,4},{6,5},{7,6},{8,7},{9,8},{10,9... | collective-permute-start | bytes 49160 | tf_op jit(solution)/shard_map/ppermute | solution.py:203
  97.9 1.9 %collective-permute-start.6 = (bf16[32,256]{1,0:T(8,128)(2,1)S(1)}, bf16[32,256]{1,0:T(8,128)(2,1)S(1)}, u32[]{:S(2)}, u32[]{:S(2)}) collective-permute-start(bf16[32,256]{1,0:T(8,128)(2,1)S(1)} %get-tuple-element.14), channel_id=1, source_target_pairs={{0,2},{1,3},{2,4},{3,5},{4,6},{5,7},{6,8},{7,9},{8,10},{9,11},{10,... | collective-permute-start | bytes 49160 | tf_op jit(solution)/shard_map/ppermute | solution.py:203
  99.9 5.7 %collective-permute-done.6.second_ref = bf16[32,256]{1,0:T(8,128)(2,1)S(1)} collective-permute-done((bf16[32,256]{1,0:T(8,128)(2,1)S(1)}, bf16[32,256]{1,0:T(8,128)(2,1)S(1)}, u32[]{:S(2)}, u32[]{:S(2)}) %collective-permute-start.6) | collective-permute-done | bytes 16416 | tf_op jit(solution)/shard_map/ppermute | solution.py:203
  105.8 17.9 %all_to_all.10.arrived_ref = bf16[16,8,128]{2,1,0:T(8,128)(2,1)S(1)} all-to-all(bf16[16,8,128]{2,1,0:T(8,128)(2,1)S(1)} %select.13), channel_id=1, replica_groups=mesh['zhi'=4,'x'=4,'zlo'=2,'y'=8,'core'=2] {'zhi','x'}, dimensions={0} | all-to-all | bytes 65536 | tf_op jit(solution)/shard_map/all_to_all | solution.py:347
  123.6 1.2 update.1
  (49 shorter events, 5.9 us)
Async XLA Ops:
  6.5 33.9 %copy-start = (f32[24,64,64]{2,1,0:T(8,128)S(1)}, f32[24,64,64]{2,1,0:T(8,128)}, u32[]{:S(2)}) copy-start(f32[24,64,64]{2,1,0:T(8,128)} %param.16) | copy-start | bytes 1179652
  6.5 47.4 %copy-start.2 = (bf16[1,32,8,1536]{3,2,1,0:T(8,128)(2,1)S(1)}, bf16[1,32,8,1536]{3,2,1,0:T(8,128)(2,1)}, u32[]{:S(2)}) copy-start(bf16[1,32,8,1536]{3,2,1,0:T(8,128)(2,1)} %tokens_ref.1) | copy-start | bytes 2359300
  6.5 68.4 %all-gather.2.cloned.1.call-start = ((), (), s32[]{:S(2)}) async-start(), calls=%async_computation.2 | async-start | bytes 4177920 | tf_op jit(solution)/shard_map/all_gather | solution.py:251
  6.5 1.1 copy-start.4
  7.6 0.9 copy-start.8
  8.5 0.9 copy-start.9
  9.4 31.2 %copy-start.10 = (f32[1536]{0:T(1024)S(1)}, f32[1536]{0:T(1024)}, u32[]{:S(2)}) copy-start(f32[1536]{0:T(1024)} %param.13) | copy-start | bytes 18436
  9.4 44.5 %copy-start.5 = (bf16[1536,69]{0,1:T(8,128)(2,1)S(1)}, bf16[1536,69]{0,1:T(8,128)(2,1)}, u32[]{:S(2)}) copy-start(bf16[1536,69]{0,1:T(8,128)(2,1)} %param.17) | copy-start | bytes 635908
  9.6 7.6 %collective-permute-start.2 = (bf16[48,1280]{1,0:T(8,128)(2,1)S(1)}, bf16[48,1280]{1,0:T(8,128)(2,1)S(1)}, u32[]{:S(2)}, u32[]{:S(2)}) collective-permute-start(bf16[48,1280]{1,0:T(8,128)(2,1)S(1)} %weights.1), channel_id=1, source_target_pairs={{0,16},{16,0},{1,17},{17,1},{2,18},{18,2},{3,19},{19,3},{4,20},{20... | collective-permute-start | bytes 368648 | tf_op jit(solution)/shard_map/ppermute | solution.py:245
  21.4 20.8 %all-to-all-start = ((f32[16,5,128]{2,1,0:T(8,128)}), f32[16,5,128]{2,1,0:T(8,128)S(1)}, u32[]{:S(2)}, u32[]{:S(2)}) async-start(f32[16,5,128]{2,1,0:T(8,128)} %copy.28), calls=%async_computation | async-start | bytes 131072 | tf_op jit(solution)/shard_map/all_to_all | solution.py:282
  36.1 17.8 %collective-permute-start = (bf16[128,1536]{1,0:T(8,128)(2,1)}, bf16[128,1536]{1,0:T(8,128)(2,1)}, u32[]{:S(2)}, u32[]{:S(2)}) collective-permute-start(bf16[128,1536]{1,0:T(8,128)(2,1)} %reshape_squeeze.3), channel_id=1, source_target_pairs={{0,31},{1,0},{2,1},{3,2},{4,3},{5,4},{6,5},{7,6},{8,7},{9,8},{10,9... | collective-permute-start | bytes 1179656 | tf_op jit(solution)/shard_map/ppermute | solution.py:203
  42.3 18.1 %collective-permute-start.3 = (f32[32,128]{1,0:T(8,128)S(1)}, f32[32,128]{1,0:T(8,128)S(1)}, u32[]{:S(2)}, u32[]{:S(2)}) collective-permute-start(f32[32,128]{1,0:T(8,128)S(1)} %bitcast.28), channel_id=1, source_target_pairs={{0,31},{1,0},{2,1},{3,2},{4,3},{5,4},{6,5},{7,6},{8,7},{9,8},{10,9... | collective-permute-start | bytes 49160 | tf_op jit(solution)/shard_map/ppermute | solution.py:203
  46.1 77.6 %copy-start.3 = (bf16[1,1,4,128,1104]{3,4,2,1,0:T(8,128)(2,1)S(1)}, bf16[1,1,4,128,1104]{3,4,2,1,0:T(8,128)(2,1)}, u32[]{:S(2)}) copy-start(bf16[1,1,4,128,1104]{3,4,2,1,0:T(8,128)(2,1)} %param.23) | copy-start | bytes 3391492
  56.6 18.3 %collective-permute-start.1 = (bf16[256,1536]{1,0:T(8,128)(2,1)S(1)}, bf16[256,1536]{1,0:T(8,128)(2,1)S(1)}, u32[]{:S(2)}, u32[]{:S(2)}) collective-permute-start(bf16[256,1536]{1,0:T(8,128)(2,1)S(1)} %get-tuple-element.10.own_ref), channel_id=1, source_target_pairs={{0,32},{32,0},{64,96},{96,64},{1,33},{33,1},{65,97},{97,65},{2,34}... | collective-permute-start | bytes 2359304 | tf_op jit(solution)/shard_map/ppermute | solution.py:275
  59.4 0.9 copy-start.6
  75.0 2.1 %copy-start.1 = (bf16[1536,1280]{1,0:T(8,128)(2,1)S(1)}, bf16[1536,1280]{1,0:T(8,128)(2,1)}, u32[]{:S(2)}) copy-start(bf16[1536,1280]{1,0:T(8,128)(2,1)} %all-gather.2.cloned.1.call-done.weights_hbm) | copy-start | bytes 11796484
  77.1 1.1 copy-start.7
  89.1 16.5 %collective-permute-start.4 = (bf16[64,256]{1,0:T(8,128)(2,1)S(1)}, bf16[64,256]{1,0:T(8,128)(2,1)S(1)}, u32[]{:S(2)}, u32[]{:S(2)}) collective-permute-start(bf16[64,256]{1,0:T(8,128)(2,1)S(1)} %get-tuple-element.12.own_ref), channel_id=1, source_target_pairs={{0,1},{1,2},{2,3},{3,4},{4,5},{5,6},{6,7},{7,8},{8,9},{9,10},{10,1... | collective-permute-start | bytes 98312 | tf_op jit(solution)/shard_map/ppermute | solution.py:203
  91.0 8.9 %collective-permute-start.5 = (bf16[32,256]{1,0:T(8,128)(2,1)S(1)}, bf16[32,256]{1,0:T(8,128)(2,1)S(1)}, u32[]{:S(2)}, u32[]{:S(2)}) collective-permute-start(bf16[32,256]{1,0:T(8,128)(2,1)S(1)} %get-tuple-element.13), channel_id=1, source_target_pairs={{0,31},{1,0},{2,1},{3,2},{4,3},{5,4},{6,5},{7,6},{8,7},{9,8},{10,9... | collective-permute-start | bytes 49160 | tf_op jit(solution)/shard_map/ppermute | solution.py:203
  97.9 7.7 %collective-permute-start.6 = (bf16[32,256]{1,0:T(8,128)(2,1)S(1)}, bf16[32,256]{1,0:T(8,128)(2,1)S(1)}, u32[]{:S(2)}, u32[]{:S(2)}) collective-permute-start(bf16[32,256]{1,0:T(8,128)(2,1)S(1)} %get-tuple-element.14), channel_id=1, source_target_pairs={{0,2},{1,3},{2,4},{3,5},{4,6},{5,7},{6,8},{7,9},{8,10},{9,11},{10,... | collective-permute-start | bytes 49160 | tf_op jit(solution)/shard_map/ppermute | solution.py:203
Sparse Core Ops, SparseCore 0:
  18.1 49.0 all-gather.1

commit v2 on v1

--- a/solution.py
+++ b/solution.py
@@ -10,6 +10,7 @@
 HS = 32
 WIN = 8
 SHIFT = 4
+MAXL = 4
 CH = 69
 MEMBER = ("zhi", "x")
 SPACE = ("zlo", "y", "core")
@@ -20,7 +21,7 @@
 F32 = jnp.float32
 BF16 = jnp.bfloat16
 NT = (((1,), (1,)), ((), ()))
-VMEM_LIMIT = 48 * 1024 * 1024
+VMEM_LIMIT = 8 * 1024 * 1024
 
 
 def dot(a, b, dims=(((1,), (0,)), ((), ()))):
@@ -44,7 +45,58 @@
     out_ref[:, 3 * GF :] = full.astype(BF16)
 
 
-def norm_kernel(tokens_ref, halo_ref, gain_ref, w_decode_ref, normed_ref, residual_ref):
+def edge_kernel(tokens_ref, index_ref, out_ref):
+    tile = tokens_ref[0].astype(F32)
+    lines, _, features = tile.shape
+    tile = tile.reshape(lines // 2, 2, WIN, features)
+    spot = lax.broadcasted_iota(jnp.int32, (lines // 2, WIN, features), 1)
+    packed = jnp.where(spot < SHIFT, tile[:, 0], pltpu.roll(tile[:, 1], 4, axis=1))
+    rows = lines * SHIFT
+    out_ref[:rows] = packed.reshape(rows, features).astype(BF16)
+    index = index_ref[...]
+    upper = (index // 32).astype(F32)
+    lower = (index % 32).astype(F32)
+    wide = jnp.concatenate(
+        [upper[:1], upper[1:], lower[:1], lower[1:], jnp.zeros((1, features - 512), F32)], axis=1
+    )
+    out_ref[rows:] = jnp.broadcast_to(wide, (16, features)).astype(BF16)
+
+
+def bias_kernel(group_ref, rel_bias_ref, out_ref):
+    for head in range(GROUP_HEADS):
+        turned = rel_bias_ref[head].T
+        out_ref[64 * head : 64 * (head + 1)] = jnp.concatenate([turned, turned], axis=1)
+
+
+def norm_kernel(
+    list_ref,
+    count_ref,
+    tokens_ref,
+    halo_ref,
+    extra_ref,
+    gain_ref,
+    w_decode_ref,
+    value_ref,
+    pert_ref,
+    index_ref,
+    normed_ref,
+    residual_ref,
+    notes_ref,
+):
+    @pl.when(pl.program_id(0) == 0)
+    def _():
+        parts = extra_ref[:8].astype(F32)
+        following = [parts[:1, 128 * b : 128 * (b + 1)] * 32.0 + parts[:1, 256 + 128 * b : 384 + 128 * b] for b in range(2)]
+        lane = lax.broadcasted_iota(jnp.int32, (1, 128), 1)
+        listed = jnp.where(lane == MAXL, count_ref[0], 0)
+        for j in range(MAXL):
+            listed = jnp.where(lane == j, list_ref[j], listed)
+        same = jnp.concatenate(
+            [index_ref[...].astype(F32)] + following + [listed.astype(F32), jnp.zeros((1, 128), F32)], axis=0
+        )
+        for member in range(16):
+            notes_ref[member] = jnp.concatenate([value_ref[...] + pert_ref[member], same], axis=0)
+
     own = tokens_ref[0].astype(F32)
     halo = halo_ref[...].astype(F32)
     features = own.shape[-1]
@@ -64,10 +116,11 @@
 
 def attention_kernel(
     group_ref,
+    starts_ref,
     own_ref,
     mate_ref,
     residual_ref,
-    weights_hbm,
+    blocks,
     bias_ref,
     value_ref,
     pick_ref,
@@ -81,15 +134,17 @@
     sems,
 ):
     copies = []
-    for block in range(16):
-        for low in range(2):
-            copies.append(
-                pltpu.make_async_copy(
-                    weights_hbm.at[pl.ds((block * 2 + low) * 48, 48)],
-                    weights.at[pl.ds((low * 16 + block) * 48, 48)],
-                    sems.at[block * 2 + low],
+    for i, block in enumerate(blocks):
+        for half in range(2):
+            for low in range(2):
+                start = pl.multiple_of(starts_ref[2 * i + half] + 768 * low, 48)
+                copies.append(
+                    pltpu.make_async_copy(
+                        block.at[pl.ds(96 * half + 48 * low, 48)],
+                        weights.at[pl.ds(start, 48)],
+                        sems.at[4 * i + 2 * half + low],
+                    )
                 )
-            )
     for copy in copies:
         copy.start()
     for copy in copies:
@@ -203,6 +258,40 @@
     return lax.ppermute(x, SPACE, [(i, (i + by) % peers) for i in range(peers)])
 
 
+def swap_pairs(first):
+    pairs = []
+    for y in range(8):
+        for core in range(2):
+            odd_pairing = (core == 0) != first
+            other = (y ^ 1) if not odd_pairing else ((y + 1) % 8 if y % 2 else (y - 1) % 8)
+            pairs.append((2 * y + core, 2 * other + core))
+    return pairs
+
+
+def swap_index(y, core, first):
+    odd_pairing = (core == 0) != first
+    even = jnp.where(y % 2 == 1, y - 1, y + 1)
+    odd = jnp.where(y % 2 == 1, (y + 1) % 8, (y + 7) % 8)
+    return jnp.where(odd_pairing, odd, even)
+
+
+def core_swap(x):
+    return lax.ppermute(x, "core", [(0, 1), (1, 0)])
+
+
+def block_starts(y, core):
+    starts = []
+    for of_core in (core, 1 - core):
+        places = [y, swap_index(y, of_core, True)]
+        for chain in ([False], [True, False], [False, True, False]):
+            at = y
+            for step in chain:
+                at = swap_index(at, of_core, step)
+            places += [at, swap_index(at, of_core, True)]
+        starts += [place * 96 + of_core * 48 for place in places]
+    return jnp.stack(starts).astype(jnp.int32)
+
+
 def smem():
     return pl.BlockSpec(memory_space=pltpu.SMEM)
 
@@ -211,8 +300,8 @@
     return pl.BlockSpec(memory_space=pltpu.VMEM)
 
 
-def params():
-    return pltpu.CompilerParams(vmem_limit_bytes=VMEM_LIMIT)
+def params(limit=VMEM_LIMIT):
+    return pltpu.CompilerParams(vmem_limit_bytes=limit)
 
 
 def body(
@@ -231,7 +320,6 @@
 ):
     features = tokens.shape[3]
     group = (lax.axis_index("x") % 2).astype(jnp.int32)
-    low = lax.axis_index("zlo")
     w_decode_t = w_decode.T
 
     rows = pl.pallas_call(
@@ -242,48 +330,82 @@
         compiler_params=params(),
         name="weights",
     )(group.reshape(1), w_qkv, w_out, w_decode_t)
-    other_rows = lax.ppermute(rows, "zlo", [(0, 1), (1, 0)])
-    both_rows = jnp.where(
-        low == 0,
-        jnp.concatenate([rows, other_rows], axis=0),
-        jnp.concatenate([other_rows, rows], axis=0),
-    )
-    gathered = lax.all_gather(both_rows, ROW, axis=0, tiled=True)
-
-    left_half = tokens[0, :, :SHIFT].reshape(-1, features)
-    halo = shift(left_half, -1)
-    normed, residual = pl.pallas_call(
+    core, low, y = (lax.axis_index("core"), lax.axis_index("zlo"), lax.axis_index("y"))
+    far = lax.ppermute(rows, "zlo", [(0, 1), (1, 0)])
+    block = jnp.where(
+        low == 0, jnp.concatenate([rows, far], axis=0), jnp.concatenate([far, rows], axis=0)
+    )
+    first, second = (swap_pairs(True), swap_pairs(False))
+    near = lax.ppermute(block, ROW, first)
+
+    edge = pl.pallas_call(
+        edge_kernel,
+        out_shape=jax.ShapeDtypeStruct((32 * SHIFT + 16, features), BF16),
+        in_specs=[vmem(), vmem()],
+        out_specs=vmem(),
+        compiler_params=params(),
+        name="edge",
+    )(tokens, obs_index[0, 0])
+    halo = shift(edge, -1)
+    near, halo = lax.optimization_barrier((near, halo))
+    held = [jnp.concatenate([block, near], axis=0)]
+    held.append(lax.ppermute(held[0], ROW, second))
+    normed, residual, notes = pl.pallas_call(
         norm_kernel,
         grid=(4,),
         out_shape=(
             jax.ShapeDtypeStruct((256, features), BF16),
             jax.ShapeDtypeStruct((256, 128), F32),
+            jax.ShapeDtypeStruct((16, 8, 128), F32),
         ),
         in_specs=[
+            smem(),
+            smem(),
             pl.BlockSpec((1, WIN, WIN, features), lambda i: (0, i, 0, 0)),
             pl.BlockSpec((WIN * SHIFT, features), lambda i: (i, 0)),
+            pl.BlockSpec((16, features), lambda i: (8, 0)),
             pl.BlockSpec((1, features), lambda i: (0, 0)),
             pl.BlockSpec(w_decode_t.shape, lambda i: (0, 0)),
+            pl.BlockSpec((2, 128), lambda i: (0, 0)),
+            pl.BlockSpec((16, 2, 128), lambda i: (0, 0, 0)),
+            pl.BlockSpec((2, 128), lambda i: (0, 0)),
         ],
         out_specs=(
             pl.BlockSpec((64, features), lambda i: (i, 0)),
             pl.BlockSpec((64, 128), lambda i: (i, 0)),
+            pl.BlockSpec((16, 8, 128), lambda i: (0, 0, 0)),
         ),
         compiler_params=params(),
         name="norm",
-    )(tokens, halo, norm_gain.reshape(1, -1), w_decode_t)
+    )(
+        block_list[0, 0],
+        list_count[0],
+        tokens,
+        halo,
+        halo,
+        norm_gain.reshape(1, -1),
+        w_decode_t,
+        obs_value[0, 0],
+        obs_pert[:, 0, 0],
+        obs_index[0, 0],
+    )
     mate = lax.ppermute(normed, "x", [(0, 1), (1, 0), (2, 3), (3, 2)])
-
-    expected = obs_value[0, 0][None] + obs_pert[:, 0, 0]
+    held[1], _ = lax.optimization_barrier((held[1], normed))
+    held.append(lax.ppermute(held[1], ROW, first))
+    swapped = [core_swap(held[0]), core_swap(held[1])]
+    held[2], *swapped = lax.optimization_barrier((held[2], *swapped))
+    held.append(lax.ppermute(held[2], ROW, second))
+    last, mate = lax.optimization_barrier((held[3], mate))
+    swapped += [core_swap(held[2]), core_swap(last)]
+    blocks = held + swapped
+    starts = block_starts(y, core)
+
+    notes, _ = lax.optimization_barrier((notes, blocks[6]))
+    observed = lax.all_to_all(notes, MEMBER, split_axis=0, concat_axis=0, tiled=True)
     entries = block_list.shape[2]
-    lists = jnp.concatenate([block_list[0, 0], list_count[0], jnp.zeros((128 - entries - 1,), jnp.int32)])
-    notes = jnp.concatenate([obs_index[0, 0], lists[None]], axis=0).astype(F32)
-    outgoing = jnp.concatenate([expected, jnp.broadcast_to(notes[None], (16, 3, 128))], axis=1)
-    observed = lax.all_to_all(outgoing, MEMBER, split_axis=0, concat_axis=0, tiled=True)
     expected = observed[:, :2].reshape(32, 128)
-    index_f = observed[:, 2:4].reshape(32, 128)
-    index_next = shift(index_f, -1).astype(jnp.int32)
-    index = index_f.astype(jnp.int32)
+    index = observed[:, 2:4].reshape(32, 128).astype(jnp.int32)
+    index_next = observed[:, 4:6].reshape(32, 128).astype(jnp.int32)
 
     def decode(index, side):
         line, rest = (index // (WIN * CH), index % (WIN * CH))
@@ -293,7 +415,7 @@
         return [channel, jnp.where(here, place, -1)]
 
     picks = jnp.concatenate(decode(index, 0) + decode(index_next, 1), axis=0)
-    meta = observed[:, 4].astype(jnp.int32)
+    meta = observed[:, 6].astype(jnp.int32)
     listed, count = (meta[:, :entries], meta[:, entries : entries + 1])
     tile_row = jnp.arange(16)[:, None] + listed // 6 - 1
     live = (jnp.arange(entries)[None] < count) & (tile_row >= 0) & (tile_row < 16)
@@ -302,9 +424,18 @@
     table_col = jnp.arange(384)[None]
     choice = ((table_col == table_row) | (table_col == table_row + 96)).astype(BF16)
 
-    bias = lax.dynamic_slice_in_dim(rel_bias, group * GROUP_HEADS, GROUP_HEADS, axis=0)
-    bias = bias.transpose(0, 2, 1).reshape(GROUP_HEADS * 64, 64)
-    bias = jnp.concatenate([bias, bias], axis=1)
+    bias = pl.pallas_call(
+        bias_kernel,
+        grid_spec=pltpu.PrefetchScalarGridSpec(
+            num_scalar_prefetch=1,
+            grid=(1,),
+            in_specs=[pl.BlockSpec((GROUP_HEADS, 64, 64), lambda i, group: (group[0], 0, 0))],
+            out_specs=pl.BlockSpec((GROUP_HEADS * 64, 128), lambda i, group: (0, 0)),
+        ),
+        out_shape=jax.ShapeDtypeStruct((GROUP_HEADS * 64, 128), F32),
+        compiler_params=params(),
+        name="bias",
+    )(group.reshape(1), rel_bias)
 
     both, right, left = pl.pallas_call(
         attention_kernel,
@@ -315,10 +446,11 @@
         ),
         in_specs=[
             smem(),
+            smem(),
             vmem(),
             vmem(),
             vmem(),
-            pl.BlockSpec(memory_space=pl.ANY),
+            [pl.BlockSpec(memory_space=pl.ANY)] * 8,
             vmem(),
             vmem(),
             vmem(),
@@ -331,9 +463,9 @@
             pltpu.VMEM((64, 256), F32),
             pltpu.SemaphoreType.DMA((32,)),
         ],
-        compiler_params=params(),
+        compiler_params=params(61 * 1024 * 1024),
         name="attention",
-    )(group.reshape(1), normed, mate, residual, gathered, bias, expected, picks)
+    )(group.reshape(1), starts, normed, mate, residual, blocks, bias, expected, picks)
 
     previous, following, second = (shift(both, 1), shift(right, -1), shift(left, 2))
     selected = pl.pallas_call(

time: 133 us -> 117 us (0.88)
  starting transfers between devices: 37.9 us -> 55.6 us
  between operations: 14.3 us -> 1.43 us
  waiting for transfers between devices: 32.8 us -> 21.6 us
  blocking collectives: 17.9 us -> 13.2 us
  other arithmetic: 3.44 us -> 1.19 us
  local copies, waits for them, and re-layouts: 10.3 us -> 8.56 us
    ppermute x1 -> x9, starting transfers between devices: 4.3 us -> 26.5 us  [the longest x4 9.97 us: core_swap(): return lax.ppermute(x, 'core', [(0, 1), (1, 0)])]
    ppermute x1, waiting for transfers between devices: 14.5 us -> 0.01 us  [body(): mate = lax.ppermute(normed, 'x', [(0, 1), (1, 0), (2, 3), (3, 2)])]
    ppermute x1 -> x9, waiting for transfers between devices: 3.3 us -> 11.2 us  [the longest x1 6.16 us: body(): near = lax.ppermute(block, ROW, first)]
    ppermute x5 -> x4, waiting for transfers between devices: 13.6 us -> 5.91 us  [shift(): return lax.ppermute(x, SPACE, [(i, (i + by) % peers) for i in range(peers)])]
    all_to_all x1, blocking collectives: 17.9 us -> 13.2 us  [body(): lax.all_to_all(selected, MEMBER, split_axis=0, concat_axis=0, tiled=True)]
    ppermute x5 -> x4, starting transfers between devices: 18.3 us -> 14 us  [shift(): return lax.ppermute(x, SPACE, [(i, (i + by) % peers) for i in range(peers)])]
    all_to_all x1, waiting for transfers between devices: 1.41 us -> 4.43 us  [body(): lax.all_to_all(notes, MEMBER, split_axis=0, concat_axis=0, tiled=True)]
    unnamed x22 -> x50, local copies, waits for them, and re-layouts: 7.02 us -> 6.93 us
  transfers between devices with their start and end apart: 9 -> 15, of which waited for: 5 -> 5; matrix products, arithmetic and copies ran while one was open for 5% -> 2% of each run, Pallas kernels for 2% -> 2%
where the time goes in v2:
time: 117 us; the launch traced here: 116 us
  starting transfers between devices  55.6 us (48%)
  waiting for transfers between devices  21.6 us (18%)
  Pallas kernels  14.4 us (12%)
  blocking collectives  13.2 us (11%)
  local copies, waits for them, and re-layouts  8.56 us (7%)
  between operations  1.43 us (1%)
  other arithmetic  1.19 us (1%)
    ppermute x4, starting transfers between devices, shift(): return lax.ppermute(x, SPACE, [(i, (i + by) % peers) for i in range(peers)])  14 us
    all_to_all x1, blocking collectives, body(): lax.all_to_all(selected, MEMBER, split_axis=0, concat_axis=0, tiled=True)  13.2 us
    all_to_all x1, starting transfers between devices, body(): lax.all_to_all(notes, MEMBER, split_axis=0, concat_axis=0, tiled=True)  12.4 us
    pallas_call x1, Pallas kernels, body(): pl.pallas_call(attention_kernel, out_shape=(jax.ShapeDtypeStruct((64, 256...  10.2 us
    ppermute x4, starting transfers between devices, core_swap(): return lax.ppermute(x, 'core', [(0, 1), (1, 0)])  9.97 us
    unnamed x50, local copies, waits for them, and re-layouts  6.93 us
    ppermute x1, waiting for transfers between devices, body(): near = lax.ppermute(block, ROW, first)  6.16 us
    ppermute x4, waiting for transfers between devices, shift(): return lax.ppermute(x, SPACE, [(i, (i + by) % peers) for i in range(peers)])  5.91 us
  transfers between devices with their start and end apart: 15, of which 5 were waited for; matrix products, arithmetic and copies ran while one was open for 2% of the time, Pallas kernels for 2%

profile of v2, /device:TPU:6, one launch (start us, length us, event | category | flops | bytes accessed | tf_op | source)
XLA Modules:
  0.0 115.8 jit_solution(14725323159327109216)
XLA Ops:
  2.9 4.3 %collective-permute-start = (bf16[48,1280]{1,0:T(8,128)(2,1)S(1)}, bf16[48,1280]{1,0:T(8,128)(2,1)S(1)}, u32[]{:S(2)}, u32[]{:S(2)}) collective-permute-start(bf16[48,1280]{1,0:T(8,128)(2,1)S(1)} %weights.1), channel_id=1, source_target_pairs={{0,16},{16,0},{1,17},{17,1},{2,18},{18,2},{3,19},{19,3},{4,20},{20... | collective-permute-start | bytes 368648 | tf_op jit(solution)/shard_map/ppermute | solution.py:334
  9.2 4.4 %collective-permute-start.2 = (bf16[144,1536]{1,0:T(8,128)(2,1)S(1)}, bf16[144,1536]{1,0:T(8,128)(2,1)S(1)}, u32[]{:S(2)}, u32[]{:S(2)}) collective-permute-start(bf16[144,1536]{1,0:T(8,128)(2,1)S(1)} %edge.1), channel_id=1, source_target_pairs={{0,31},{1,0},{2,1},{3,2},{4,3},{5,4},{6,5},{7,6},{8,7},{9,8},{10,9... | collective-permute-start | bytes 1327112 | tf_op jit(solution)/shard_map/ppermute | solution.py:258
  13.7 1.9 %collective-permute-start.1 = (bf16[96,1280]{1,0:T(8,128)(2,1)S(1)}, bf16[96,1280]{1,0:T(8,128)(2,1)S(1)}, u32[]{:S(2)}, u32[]{:S(2)}) collective-permute-start(bf16[96,1280]{1,0:T(8,128)(2,1)S(1)} %maximum_select_fusion), channel_id=1, source_target_pairs={{0,2},{1,15},{2,0},{3,5},{4,6},{5,3},{6,4},{7,9},{8,10},{9,7},{10,... | collective-permute-start | bytes 737288 | tf_op jit(solution)/shard_map/ppermute | solution.py:339
  15.6 6.2 %collective-permute-done.1 = bf16[96,1280]{1,0:T(8,128)(2,1)S(1)} collective-permute-done((bf16[96,1280]{1,0:T(8,128)(2,1)S(1)}, bf16[96,1280]{1,0:T(8,128)(2,1)S(1)}, u32[]{:S(2)}, u32[]{:S(2)}) %collective-permute-start.1) | collective-permute-done | bytes 245792 | tf_op jit(solution)/shard_map/ppermute | solution.py:339
  21.9 3.8 %collective-permute-start.3 = (bf16[192,1280]{1,0:T(8,128)(2,1)S(1)}, bf16[192,1280]{1,0:T(8,128)(2,1)S(1)}, u32[]{:S(2)}, u32[]{:S(2)}) collective-permute-start(bf16[192,1280]{1,0:T(8,128)(2,1)S(1)} %pad_maximum_fusion.blocks_0_), channel_id=1, source_target_pairs={{0,14},{1,3},{2,4},{3,1},{4,2},{5,7},{6,8},{7,5},{8,6},{9,11},{10,... | collective-permute-start | bytes 1474568 | tf_op jit(solution)/shard_map/ppermute | solution.py:352
  26.3 1.9 %collective-permute-start.5 = (bf16[192,1280]{1,0:T(8,128)(2,1)S(1)}, bf16[192,1280]{1,0:T(8,128)(2,1)S(1)}, u32[]{:S(2)}, u32[]{:S(2)}) collective-permute-start(bf16[192,1280]{1,0:T(8,128)(2,1)S(1)} %pad_maximum_fusion.blocks_0_), channel_id=1, source_target_pairs={{0,1},{1,0},{2,3},{3,2},{4,5},{5,4},{6,7},{7,6},{8,9},{9,8},{10,11... | collective-permute-start | bytes 1474568 | tf_op jit(solution)/shard_map/ppermute | solution.py:279
  28.3 2.2 %norm.1 = (bf16[256,1536]{1,0:T(8,128)(2,1)S(1)}, f32[256,128]{1,0:T(8,128)S(1)}, f32[16,8,128]{2,1,0:T(8,128)}) custom-call(s32[4]{0:T(128)S(1)} %bitcast.41, s32[1]{0:T(128)} %bitcast.33.count_ref, bf16[1,32,8,1536]{3,2,1,0:T(8,128)(2,1)S(1)} %copy-done.1, bf16[144,1536]{1,0:T(8,128)(2,1)S(1)} %collective-permute-done.2.halo_ref.extra_ref, ...), custom_call_target="tpu_custom_call" | custom-call | tf_op jit(solution)/shard_map/norm/pallas_call | solution.py:353
  30.5 3.3 %collective-permute-done.3.blocks_1_ = bf16[192,1280]{1,0:T(8,128)(2,1)S(1)} collective-permute-done((bf16[192,1280]{1,0:T(8,128)(2,1)S(1)}, bf16[192,1280]{1,0:T(8,128)(2,1)S(1)}, u32[]{:S(2)}, u32[]{:S(2)}) %collective-permute-start.3) | collective-permute-done | bytes 491552 | tf_op jit(solution)/shard_map/ppermute | solution.py:352
  33.8 1.9 %collective-permute-start.4 = (bf16[192,1280]{1,0:T(8,128)(2,1)S(1)}, bf16[192,1280]{1,0:T(8,128)(2,1)S(1)}, u32[]{:S(2)}, u32[]{:S(2)}) collective-permute-start(bf16[192,1280]{1,0:T(8,128)(2,1)S(1)} %collective-permute-done.3.blocks_1_), channel_id=1, source_target_pairs={{0,2},{1,15},{2,0},{3,5},{4,6},{5,3},{6,4},{7,9},{8,10},{9,7},{10,... | collective-permute-start | bytes 1474568 | tf_op jit(solution)/shard_map/ppermute | solution.py:394
  35.7 4.2 %collective-permute-start.6 = (bf16[192,1280]{1,0:T(8,128)(2,1)S(1)}, bf16[192,1280]{1,0:T(8,128)(2,1)S(1)}, u32[]{:S(2)}, u32[]{:S(2)}) collective-permute-start(bf16[192,1280]{1,0:T(8,128)(2,1)S(1)} %collective-permute-done.3.blocks_1_), channel_id=1, source_target_pairs={{0,1},{1,0},{2,3},{3,2},{4,5},{5,4},{6,7},{7,6},{8,9},{9,8},{10,11... | collective-permute-start | bytes 1474568 | tf_op jit(solution)/shard_map/ppermute | solution.py:279
  39.9 2.7 %collective-permute-start.8 = (bf16[256,1536]{1,0:T(8,128)(2,1)S(1)}, bf16[256,1536]{1,0:T(8,128)(2,1)S(1)}, u32[]{:S(2)}, u32[]{:S(2)}) collective-permute-start(bf16[256,1536]{1,0:T(8,128)(2,1)S(1)} %get-tuple-element.21.own_ref), channel_id=1, source_target_pairs={{0,32},{32,0},{64,96},{96,64},{1,33},{33,1},{65,97},{97,65},{2,34}... | collective-permute-start | bytes 2359304 | tf_op jit(solution)/shard_map/ppermute | solution.py:392
  42.7 1.8 %collective-permute-done.4.blocks_2_ = bf16[192,1280]{1,0:T(8,128)(2,1)S(1)} collective-permute-done((bf16[192,1280]{1,0:T(8,128)(2,1)S(1)}, bf16[192,1280]{1,0:T(8,128)(2,1)S(1)}, u32[]{:S(2)}, u32[]{:S(2)}) %collective-permute-start.4) | collective-permute-done | bytes 491552 | tf_op jit(solution)/shard_map/ppermute | solution.py:394
  44.5 1.9 %collective-permute-start.9 = (bf16[192,1280]{1,0:T(8,128)(2,1)S(1)}, bf16[192,1280]{1,0:T(8,128)(2,1)}, u32[]{:S(2)}, u32[]{:S(2)}) collective-permute-start(bf16[192,1280]{1,0:T(8,128)(2,1)S(1)} %collective-permute-done.4.blocks_2_), channel_id=1, source_target_pairs={{0,1},{1,0},{2,3},{3,2},{4,5},{5,4},{6,7},{7,6},{8,9},{9,8},{10,11... | collective-permute-start | bytes 1474568 | tf_op jit(solution)/shard_map/ppermute | solution.py:279
  46.5 4.6 %collective-permute-start.7 = (bf16[192,1280]{1,0:T(8,128)(2,1)S(1)}, bf16[192,1280]{1,0:T(8,128)(2,1)}, u32[]{:S(2)}, u32[]{:S(2)}) collective-permute-start(bf16[192,1280]{1,0:T(8,128)(2,1)S(1)} %collective-permute-done.4.blocks_2_), channel_id=1, source_target_pairs={{0,14},{1,3},{2,4},{3,1},{4,2},{5,7},{6,8},{7,5},{8,6},{9,11},{10,... | collective-permute-start | bytes 1474568 | tf_op jit(solution)/shard_map/ppermute | solution.py:397
  51.4 12.4 %all-to-all-start = ((f32[16,8,128]{2,1,0:T(8,128)}), f32[16,8,128]{2,1,0:T(8,128)S(1)}, u32[]{:S(2)}, u32[]{:S(2)}) async-start(f32[16,8,128]{2,1,0:T(8,128)} %get-tuple-element.31), calls=%async_computation | async-start | bytes 131072 | tf_op jit(solution)/shard_map/all_to_all | solution.py:404
  65.6 1.9 %collective-permute-start.10 = (bf16[192,1280]{1,0:T(8,128)(2,1)}, bf16[192,1280]{1,0:T(8,128)(2,1)S(1)}, u32[]{:S(2)}, u32[]{:S(2)}) collective-permute-start(bf16[192,1280]{1,0:T(8,128)(2,1)} %collective-permute-done.7.blocks_3_), channel_id=1, source_target_pairs={{0,1},{1,0},{2,3},{3,2},{4,5},{5,4},{6,7},{7,6},{8,9},{9,8},{10,11... | collective-permute-start | bytes 1474568 | tf_op jit(solution)/shard_map/ppermute | solution.py:279
  67.5 4.4 %all-to-all-done = f32[16,8,128]{2,1,0:T(8,128)S(1)} async-done(((f32[16,8,128]{2,1,0:T(8,128)}), f32[16,8,128]{2,1,0:T(8,128)S(1)}, u32[]{:S(2)}, u32[]{:S(2)}) %all-to-all-start) | async-done | bytes 65568 | tf_op jit(solution)/shard_map/all_to_all | solution.py:404
  74.7 10.2 %attention.1 = (bf16[64,256]{1,0:T(8,128)(2,1)}, bf16[32,256]{1,0:T(8,128)(2,1)}, bf16[32,256]{1,0:T(8,128)(2,1)}) custom-call(s32[1]{0:T(128)} %bitcast.group_ref, s32[16]{0:T(128)} %stack.67.starts_ref, bf16[256,1536]{1,0:T(8,128)(2,1)} %copy-done.6, bf16[256,1536]{1,0:T(8,128)(2,1)} %copy-done.18, f32[256,128]{1,0:T(8,128)} %copy-done.9, ...), custom_call_target="tpu_custom_call" | custom-call | tf_op jit(solution)/shard_map/attention/pallas_call | solution.py:440
  84.9 1.9 %collective-permute-start.11 = (bf16[64,256]{1,0:T(8,128)(2,1)}, bf16[64,256]{1,0:T(8,128)(2,1)S(1)}, u32[]{:S(2)}, u32[]{:S(2)}) collective-permute-start(bf16[64,256]{1,0:T(8,128)(2,1)} %get-tuple-element.32.own_ref), channel_id=1, source_target_pairs={{0,1},{1,2},{2,3},{3,4},{4,5},{5,6},{6,7},{7,8},{8,9},{9,10},{10,1... | collective-permute-start | bytes 98312 | tf_op jit(solution)/shard_map/ppermute | solution.py:258
  86.9 5.8 %collective-permute-start.12 = (bf16[32,256]{1,0:T(8,128)(2,1)}, bf16[32,256]{1,0:T(8,128)(2,1)S(1)}, u32[]{:S(2)}, u32[]{:S(2)}) collective-permute-start(bf16[32,256]{1,0:T(8,128)(2,1)} %get-tuple-element.33), channel_id=1, source_target_pairs={{0,31},{1,0},{2,1},{3,2},{4,3},{5,4},{6,5},{7,6},{8,7},{9,8},{10,9... | collective-permute-start | bytes 49160 | tf_op jit(solution)/shard_map/ppermute | solution.py:258
  92.6 1.9 %collective-permute-start.13 = (bf16[32,256]{1,0:T(8,128)(2,1)}, bf16[32,256]{1,0:T(8,128)(2,1)S(1)}, u32[]{:S(2)}, u32[]{:S(2)}) collective-permute-start(bf16[32,256]{1,0:T(8,128)(2,1)} %get-tuple-element.34), channel_id=1, source_target_pairs={{0,2},{1,3},{2,4},{3,5},{4,6},{5,7},{6,8},{7,9},{8,10},{9,11},{10,... | collective-permute-start | bytes 49160 | tf_op jit(solution)/shard_map/ppermute | solution.py:258
  94.7 5.9 %collective-permute-done.13.second_ref = bf16[32,256]{1,0:T(8,128)(2,1)S(1)} collective-permute-done((bf16[32,256]{1,0:T(8,128)(2,1)}, bf16[32,256]{1,0:T(8,128)(2,1)S(1)}, u32[]{:S(2)}, u32[]{:S(2)}) %collective-permute-start.13) | collective-permute-done | bytes 16416 | tf_op jit(solution)/shard_map/ppermute | solution.py:258
  101.5 13.2 %all_to_all.10.arrived_ref = bf16[16,8,128]{2,1,0:T(8,128)(2,1)S(1)} all-to-all(bf16[16,8,128]{2,1,0:T(8,128)(2,1)S(1)} %select.79), channel_id=1, replica_groups=mesh['zhi'=4,'x'=4,'zlo'=2,'y'=8,'core'=2] {'zhi','x'}, dimensions={0} | all-to-all | bytes 65536 | tf_op jit(solution)/shard_map/all_to_all | solution.py:479
  114.7 1.2 %update.1 = f32[16,1104]{1,0:T(8,128)} custom-call(bf16[16,8,128]{2,1,0:T(8,128)(2,1)S(1)} %all_to_all.10.arrived_ref, bf16[4,1104,128]{2,1,0:T(8,128)(2,1)S(1)} %bitcast.34), custom_call_target="tpu_custom_call" | custom-call | tf_op jit(solution)/shard_map/update/pallas_call | solution.py:481
  (83 shorter events, 10.6 us)
Async XLA Ops:
  2.9 10.7 %collective-permute-start = (bf16[48,1280]{1,0:T(8,128)(2,1)S(1)}, bf16[48,1280]{1,0:T(8,128)(2,1)S(1)}, u32[]{:S(2)}, u32[]{:S(2)}) collective-permute-start(bf16[48,1280]{1,0:T(8,128)(2,1)S(1)} %weights.1), channel_id=1, source_target_pairs={{0,16},{16,0},{1,17},{17,1},{2,18},{18,2},{3,19},{19,3},{4,20},{20... | collective-permute-start | bytes 368648 | tf_op jit(solution)/shard_map/ppermute | solution.py:334
  9.1 19.2 %copy-start.12 = (f32[16,1,1,2,128]{4,3,2,1,0:T(2,128)S(1)}, f32[16,1,1,2,128]{4,3,2,1,0:T(2,128)}, u32[]{:S(2)}) copy-start(f32[16,1,1,2,128]{4,3,2,1,0:T(2,128)} %param.19) | copy-start | bytes 49156
  9.1 19.2 %copy-start.14 = (s32[1,1,2,128]{3,2,1,0:T(2,128)S(1)}, s32[1,1,2,128]{3,2,1,0:T(2,128)}, u32[]{:S(2)}) copy-start(s32[1,1,2,128]{3,2,1,0:T(2,128)} %param.20) | copy-start | bytes 3076
  9.1 19.2 %copy-start.15 = (f32[1,1,2,128]{3,2,1,0:T(2,128)S(1)}, f32[1,1,2,128]{3,2,1,0:T(2,128)}, u32[]{:S(2)}) copy-start(f32[1,1,2,128]{3,2,1,0:T(2,128)} %param.18) | copy-start | bytes 3076
  9.1 19.2 %copy-start.16 = (s32[1,1,4]{2,1,0:T(1,128)S(1)}, s32[1,1,4]{2,1,0:T(1,128)}, u32[]{:S(2)}) copy-start(s32[1,1,4]{2,1,0:T(1,128)} %param.21) | copy-start | bytes 52
  9.2 12.6 %collective-permute-start.2 = (bf16[144,1536]{1,0:T(8,128)(2,1)S(1)}, bf16[144,1536]{1,0:T(8,128)(2,1)S(1)}, u32[]{:S(2)}, u32[]{:S(2)}) collective-permute-start(bf16[144,1536]{1,0:T(8,128)(2,1)S(1)} %edge.1), channel_id=1, source_target_pairs={{0,31},{1,0},{2,1},{3,2},{4,3},{5,4},{6,5},{7,6},{8,7},{9,8},{10,9... | collective-permute-start | bytes 1327112 | tf_op jit(solution)/shard_map/ppermute | solution.py:258
  13.7 8.1 %collective-permute-start.1 = (bf16[96,1280]{1,0:T(8,128)(2,1)S(1)}, bf16[96,1280]{1,0:T(8,128)(2,1)S(1)}, u32[]{:S(2)}, u32[]{:S(2)}) collective-permute-start(bf16[96,1280]{1,0:T(8,128)(2,1)S(1)} %maximum_select_fusion), channel_id=1, source_target_pairs={{0,2},{1,15},{2,0},{3,5},{4,6},{5,3},{6,4},{7,9},{8,10},{9,7},{10,... | collective-permute-start | bytes 737288 | tf_op jit(solution)/shard_map/ppermute | solution.py:339
  21.9 11.9 %collective-permute-start.3 = (bf16[192,1280]{1,0:T(8,128)(2,1)S(1)}, bf16[192,1280]{1,0:T(8,128)(2,1)S(1)}, u32[]{:S(2)}, u32[]{:S(2)}) collective-permute-start(bf16[192,1280]{1,0:T(8,128)(2,1)S(1)} %pad_maximum_fusion.blocks_0_), channel_id=1, source_target_pairs={{0,14},{1,3},{2,4},{3,1},{4,2},{5,7},{6,8},{7,5},{8,6},{9,11},{10,... | collective-permute-start | bytes 1474568 | tf_op jit(solution)/shard_map/ppermute | solution.py:352
  26.3 16.4 %collective-permute-start.5 = (bf16[192,1280]{1,0:T(8,128)(2,1)S(1)}, bf16[192,1280]{1,0:T(8,128)(2,1)S(1)}, u32[]{:S(2)}, u32[]{:S(2)}) collective-permute-start(bf16[192,1280]{1,0:T(8,128)(2,1)S(1)} %pad_maximum_fusion.blocks_0_), channel_id=1, source_target_pairs={{0,1},{1,0},{2,3},{3,2},{4,5},{5,4},{6,7},{7,6},{8,9},{9,8},{10,11... | collective-permute-start | bytes 1474568 | tf_op jit(solution)/shard_map/ppermute | solution.py:279
  28.3 35.4 %copy-start.7 = (f32[24,64,64]{2,1,0:T(8,128)S(1)}, f32[24,64,64]{2,1,0:T(8,128)}, u32[]{:S(2)}) copy-start(f32[24,64,64]{2,1,0:T(8,128)} %rel_bias_ref.1) | copy-start | bytes 1179652
  30.5 33.6 %copy-start.6 = (bf16[256,1536]{1,0:T(8,128)(2,1)}, bf16[256,1536]{1,0:T(8,128)(2,1)S(1)}, u32[]{:S(2)}) copy-start(bf16[256,1536]{1,0:T(8,128)(2,1)S(1)} %get-tuple-element.21.own_ref) | copy-start | bytes 2359300
  30.5 33.6 %copy-start.9 = (f32[256,128]{1,0:T(8,128)}, f32[256,128]{1,0:T(8,128)S(1)}, u32[]{:S(2)}) copy-start(f32[256,128]{1,0:T(8,128)S(1)} %get-tuple-element.26.residual_ref) | copy-start | bytes 393220
  33.8 10.7 %collective-permute-start.4 = (bf16[192,1280]{1,0:T(8,128)(2,1)S(1)}, bf16[192,1280]{1,0:T(8,128)(2,1)S(1)}, u32[]{:S(2)}, u32[]{:S(2)}) collective-permute-start(bf16[192,1280]{1,0:T(8,128)(2,1)S(1)} %collective-permute-done.3.blocks_1_), channel_id=1, source_target_pairs={{0,2},{1,15},{2,0},{3,5},{4,6},{5,3},{6,4},{7,9},{8,10},{9,7},{10,... | collective-permute-start | bytes 1474568 | tf_op jit(solution)/shard_map/ppermute | solution.py:394
  35.7 8.8 %collective-permute-start.6 = (bf16[192,1280]{1,0:T(8,128)(2,1)S(1)}, bf16[192,1280]{1,0:T(8,128)(2,1)S(1)}, u32[]{:S(2)}, u32[]{:S(2)}) collective-permute-start(bf16[192,1280]{1,0:T(8,128)(2,1)S(1)} %collective-permute-done.3.blocks_1_), channel_id=1, source_target_pairs={{0,1},{1,0},{2,3},{3,2},{4,5},{5,4},{6,7},{7,6},{8,9},{9,8},{10,11... | collective-permute-start | bytes 1474568 | tf_op jit(solution)/shard_map/ppermute | solution.py:279
  39.9 25.6 %collective-permute-start.8 = (bf16[256,1536]{1,0:T(8,128)(2,1)S(1)}, bf16[256,1536]{1,0:T(8,128)(2,1)S(1)}, u32[]{:S(2)}, u32[]{:S(2)}) collective-permute-start(bf16[256,1536]{1,0:T(8,128)(2,1)S(1)} %get-tuple-element.21.own_ref), channel_id=1, source_target_pairs={{0,32},{32,0},{64,96},{96,64},{1,33},{33,1},{65,97},{97,65},{2,34}... | collective-permute-start | bytes 2359304 | tf_op jit(solution)/shard_map/ppermute | solution.py:392
  44.5 19.6 %copy-start.21 = (bf16[192,1280]{1,0:T(8,128)(2,1)}, bf16[192,1280]{1,0:T(8,128)(2,1)S(1)}, u32[]{:S(2)}) copy-start(bf16[192,1280]{1,0:T(8,128)(2,1)S(1)} %collective-permute-done.4.blocks_2_) | copy-start | bytes 1474564
  44.5 6.8 %collective-permute-start.9 = (bf16[192,1280]{1,0:T(8,128)(2,1)S(1)}, bf16[192,1280]{1,0:T(8,128)(2,1)}, u32[]{:S(2)}, u32[]{:S(2)}) collective-permute-start(bf16[192,1280]{1,0:T(8,128)(2,1)S(1)} %collective-permute-done.4.blocks_2_), channel_id=1, source_target_pairs={{0,1},{1,0},{2,3},{3,2},{4,5},{5,4},{6,7},{7,6},{8,9},{9,8},{10,11... | collective-permute-start | bytes 1474568 | tf_op jit(solution)/shard_map/ppermute | solution.py:279
  46.5 19.1 %collective-permute-start.7 = (bf16[192,1280]{1,0:T(8,128)(2,1)S(1)}, bf16[192,1280]{1,0:T(8,128)(2,1)}, u32[]{:S(2)}, u32[]{:S(2)}) collective-permute-start(bf16[192,1280]{1,0:T(8,128)(2,1)S(1)} %collective-permute-done.4.blocks_2_), channel_id=1, source_target_pairs={{0,14},{1,3},{2,4},{3,1},{4,2},{5,7},{6,8},{7,5},{8,6},{9,11},{10,... | collective-permute-start | bytes 1474568 | tf_op jit(solution)/shard_map/ppermute | solution.py:397
  51.4 20.6 %all-to-all-start = ((f32[16,8,128]{2,1,0:T(8,128)}), f32[16,8,128]{2,1,0:T(8,128)S(1)}, u32[]{:S(2)}, u32[]{:S(2)}) async-start(f32[16,8,128]{2,1,0:T(8,128)} %get-tuple-element.31), calls=%async_computation | async-start | bytes 131072 | tf_op jit(solution)/shard_map/all_to_all | solution.py:404
  65.6 8.3 %collective-permute-start.10 = (bf16[192,1280]{1,0:T(8,128)(2,1)}, bf16[192,1280]{1,0:T(8,128)(2,1)S(1)}, u32[]{:S(2)}, u32[]{:S(2)}) collective-permute-start(bf16[192,1280]{1,0:T(8,128)(2,1)} %collective-permute-done.7.blocks_3_), channel_id=1, source_target_pairs={{0,1},{1,0},{2,3},{3,2},{4,5},{5,4},{6,7},{7,6},{8,9},{9,8},{10,11... | collective-permute-start | bytes 1474568 | tf_op jit(solution)/shard_map/ppermute | solution.py:279
  74.7 39.9 %copy-start.3 = (bf16[1,1,4,128,1104]{3,4,2,1,0:T(8,128)(2,1)S(1)}, bf16[1,1,4,128,1104]{3,4,2,1,0:T(8,128)(2,1)}, u32[]{:S(2)}) copy-start(bf16[1,1,4,128,1104]{3,4,2,1,0:T(8,128)(2,1)} %param.23) | copy-start | bytes 3391492
  84.9 15.6 %collective-permute-start.11 = (bf16[64,256]{1,0:T(8,128)(2,1)}, bf16[64,256]{1,0:T(8,128)(2,1)S(1)}, u32[]{:S(2)}, u32[]{:S(2)}) collective-permute-start(bf16[64,256]{1,0:T(8,128)(2,1)} %get-tuple-element.32.own_ref), channel_id=1, source_target_pairs={{0,1},{1,2},{2,3},{3,4},{4,5},{5,6},{6,7},{7,8},{8,9},{9,10},{10,1... | collective-permute-start | bytes 98312 | tf_op jit(solution)/shard_map/ppermute | solution.py:258
  86.9 7.8 %collective-permute-start.12 = (bf16[32,256]{1,0:T(8,128)(2,1)}, bf16[32,256]{1,0:T(8,128)(2,1)S(1)}, u32[]{:S(2)}, u32[]{:S(2)}) collective-permute-start(bf16[32,256]{1,0:T(8,128)(2,1)} %get-tuple-element.33), channel_id=1, source_target_pairs={{0,31},{1,0},{2,1},{3,2},{4,3},{5,4},{6,5},{7,6},{8,7},{9,8},{10,9... | collective-permute-start | bytes 49160 | tf_op jit(solution)/shard_map/ppermute | solution.py:258
  92.6 8.0 %collective-permute-start.13 = (bf16[32,256]{1,0:T(8,128)(2,1)}, bf16[32,256]{1,0:T(8,128)(2,1)S(1)}, u32[]{:S(2)}, u32[]{:S(2)}) collective-permute-start(bf16[32,256]{1,0:T(8,128)(2,1)} %get-tuple-element.34), channel_id=1, source_target_pairs={{0,2},{1,3},{2,4},{3,5},{4,6},{5,7},{6,8},{7,9},{8,10},{9,11},{10,... | collective-permute-start | bytes 49160 | tf_op jit(solution)/shard_map/ppermute | solution.py:258
  (16 other events, 97.4 us)

commit v3 on v2

--- a/solution.py
+++ b/solution.py
@@ -122,8 +122,7 @@
     residual_ref,
     blocks,
     bias_ref,
-    value_ref,
-    pick_ref,
+    observed_ref,
     both_ref,
     right_ref,
     left_ref,
@@ -134,24 +133,25 @@
     sems,
 ):
     copies = []
-    for i, block in enumerate(blocks):
-        for half in range(2):
-            for low in range(2):
-                start = pl.multiple_of(starts_ref[2 * i + half] + 768 * low, 48)
-                copies.append(
-                    pltpu.make_async_copy(
-                        block.at[pl.ds(96 * half + 48 * low, 48)],
-                        weights.at[pl.ds(start, 48)],
-                        sems.at[4 * i + 2 * half + low],
+    for part, lanes in enumerate((slice(0, GF), slice(GF, 2 * GF), slice(2 * GF, WCOLS))):
+        for i, block in enumerate(blocks):
+            for half in range(2):
+                for low in range(2):
+                    start = pl.multiple_of(starts_ref[2 * i + half] + 768 * low, 48)
+                    copies.append(
+                        pltpu.make_async_copy(
+                            block.at[pl.ds(96 * half + 48 * low, 48), lanes],
+                            weights.at[pl.ds(start, 48), lanes],
+                            sems.at[part, 4 * i + 2 * half + low],
+                        )
                     )
-                )
     for copy in copies:
         copy.start()
-    for copy in copies:
-        copy.wait()
-    for member, source in enumerate((own_ref, mate_ref)):
-        for part in range(3):
-            lanes = slice(part * GF, (part + 1) * GF)
+    for part in range(3):
+        for copy in copies[32 * part : 32 * (part + 1)]:
+            copy.wait()
+        lanes = slice(part * GF, (part + 1) * GF)
+        for member, source in enumerate((own_ref, mate_ref)):
             qkv[member * 256 : (member + 1) * 256, lanes] = dot(source[...], weights[:, lanes]).astype(BF16)
     first = pl.multiple_of(group_ref[0] * 768, 768)
     folded = jnp.concatenate(
@@ -209,33 +209,57 @@
     cell = lax.broadcasted_iota(jnp.int32, (8, 128), 0)
     for tile in range(16):
         for block in range(2):
-            row = 2 * tile + block
             for side in range(2):
-                channel = jnp.broadcast_to(pick_ref[64 * side + row : 64 * side + row + 1], (8, 128))
-                place = jnp.broadcast_to(pick_ref[64 * side + 32 + row : 64 * side + 32 + row + 1], (8, 128))
+                at = 2 + 2 * side + block
+                code = jnp.broadcast_to(observed_ref[tile, at : at + 1].astype(jnp.int32), (8, 128))
+                channel, place = (code & 127, code >> 7)
                 for member in range(2):
                     found = None
-                    for line in range(2):
-                        at = member * 256 + 16 * tile + 8 * line
-                        gathered = jnp.take_along_axis(fields[at : at + 8], channel, axis=1)
-                        kept = jnp.where(place == cell + 8 * line, gathered, 0.0)
+                    for half in range(2):
+                        row = member * 256 + 16 * tile + 8 * half
+                        gathered = jnp.take_along_axis(fields[row : row + 8], channel, axis=1)
+                        kept = jnp.where(place == cell + 8 * half, gathered, 0.0)
                         found = kept if found is None else found + kept
                     found = -jnp.sum(found, axis=0, keepdims=True)
                     if side == 0 and member == 0:
-                        found = found + value_ref[row : row + 1]
-                    sums[32 * side + row : 32 * side + row + 1, 128 * member : 128 * (member + 1)] = found
+                        found = found + observed_ref[tile, block : block + 1]
+                    row = 32 * side + 2 * tile + block
+                    sums[row : row + 1, 128 * member : 128 * (member + 1)] = found
     both = sums[...].astype(BF16)
     both_ref[...] = both
     right_ref[...] = both[:32]
     left_ref[...] = both[32:]
 
 
-def select_kernel(own_ref, prev_ref, next_ref, second_ref, choice_ref, out_ref):
-    table = jnp.concatenate(
-        [prev_ref[:32], own_ref[:32], next_ref[...], second_ref[...], prev_ref[32:], own_ref[32:]], axis=0
-    )
-    table = jnp.concatenate([table[:, :128], table[:, 128:]], axis=0)
-    out_ref[...] = dot(choice_ref[...], table).astype(BF16).reshape(16, 8, 128)
+def decode_kernel(observed_ref, out_ref):
+    index = observed_ref[...]
+    line = jnp.where(index >= WIN * CH, 1.0, 0.0)
+    rest = index - line * (WIN * CH)
+    column = jnp.floor((rest + 0.5) * (1.0 / CH))
+    channel = rest - column * CH
+    side = lax.broadcasted_iota(jnp.int32, index.shape, 1)
+    late = column >= SHIFT
+    place = line * WIN + jnp.where(late, column - SHIFT, column + SHIFT)
+    inside = late == (side < 4)
+    place = jnp.where(inside, place, 64.0)
+    out_ref[...] = jnp.where(side < 2, index, place * 128.0 + channel)
+
+
+def select_kernel(chosen_ref, own_ref, prev_ref, next_ref, second_ref, out_ref, table, picked):
+    for place, part in enumerate(
+        (prev_ref[:32], own_ref[:32], next_ref[...], second_ref[...], prev_ref[32:], own_ref[32:])
+    ):
+        table[32 * place : 32 * (place + 1)] = part.astype(F32)
+    table[192:200] = jnp.zeros((8, 256), F32)
+    table[288:296] = jnp.zeros((8, 256), F32)
+    for band in range(16):
+        for j in range(MAXL):
+            row = chosen_ref[MAXL * band + j]
+            found = table[pl.ds(row, 1)] + table[pl.ds(row + 96, 1)]
+            for member in range(2):
+                to = MAXL * member + j
+                picked[band, to : to + 1] = found[:, 128 * member : 128 * (member + 1)]
+    out_ref[...] = picked[...].astype(BF16)
 
 
 def update_kernel(arrived_ref, gains_ref, out_ref):
@@ -327,7 +351,7 @@
         out_shape=jax.ShapeDtypeStruct((w_qkv.shape[0], WCOLS), BF16),
         in_specs=[smem(), vmem(), vmem(), vmem()],
         out_specs=vmem(),
-        compiler_params=params(),
+        compiler_params=params(63 * 1024 * 1024),
         name="weights",
     )(group.reshape(1), w_qkv, w_out, w_decode_t)
     core, low, y = (lax.axis_index("core"), lax.axis_index("zlo"), lax.axis_index("y"))
@@ -390,40 +414,6 @@
         obs_index[0, 0],
     )
     mate = lax.ppermute(normed, "x", [(0, 1), (1, 0), (2, 3), (3, 2)])
-    held[1], _ = lax.optimization_barrier((held[1], normed))
-    held.append(lax.ppermute(held[1], ROW, first))
-    swapped = [core_swap(held[0]), core_swap(held[1])]
-    held[2], *swapped = lax.optimization_barrier((held[2], *swapped))
-    held.append(lax.ppermute(held[2], ROW, second))
-    last, mate = lax.optimization_barrier((held[3], mate))
-    swapped += [core_swap(held[2]), core_swap(last)]
-    blocks = held + swapped
-    starts = block_starts(y, core)
-
-    notes, _ = lax.optimization_barrier((notes, blocks[6]))
-    observed = lax.all_to_all(notes, MEMBER, split_axis=0, concat_axis=0, tiled=True)
-    entries = block_list.shape[2]
-    expected = observed[:, :2].reshape(32, 128)
-    index = observed[:, 2:4].reshape(32, 128).astype(jnp.int32)
-    index_next = observed[:, 4:6].reshape(32, 128).astype(jnp.int32)
-
-    def decode(index, side):
-        line, rest = (index // (WIN * CH), index % (WIN * CH))
-        column, channel = (rest // CH, rest % CH)
-        here = (column >= SHIFT) if side == 0 else (column < SHIFT)
-        place = line * WIN + (column + SHIFT) % WIN
-        return [channel, jnp.where(here, place, -1)]
-
-    picks = jnp.concatenate(decode(index, 0) + decode(index_next, 1), axis=0)
-    meta = observed[:, 6].astype(jnp.int32)
-    listed, count = (meta[:, :entries], meta[:, entries : entries + 1])
-    tile_row = jnp.arange(16)[:, None] + listed // 6 - 1
-    live = (jnp.arange(entries)[None] < count) & (tile_row >= 0) & (tile_row < 16)
-    table_row = jnp.where(live, (listed // 2 % 3) * 32 + tile_row * 2 + listed % 2, -1000)
-    table_row = (table_row[:, None, :] + 192 * jnp.arange(2)[None, :, None]).reshape(128, 1)
-    table_col = jnp.arange(384)[None]
-    choice = ((table_col == table_row) | (table_col == table_row + 96)).astype(BF16)
-
     bias = pl.pallas_call(
         bias_kernel,
         grid_spec=pltpu.PrefetchScalarGridSpec(
@@ -436,6 +426,34 @@
         compiler_params=params(),
         name="bias",
     )(group.reshape(1), rel_bias)
+    starts = block_starts(y, core)
+    held[1], bias, starts, _ = lax.optimization_barrier((held[1], bias, starts, normed))
+    held.append(lax.ppermute(held[1], ROW, first))
+    swapped = [core_swap(held[0]), core_swap(held[1])]
+    held[2], *swapped = lax.optimization_barrier((held[2], *swapped))
+    held.append(lax.ppermute(held[2], ROW, second))
+    swapped.append(core_swap(held[2]))
+
+    notes, _ = lax.optimization_barrier((notes, held[2]))
+    observed = lax.all_to_all(notes, MEMBER, split_axis=0, concat_axis=0, tiled=True)
+    entries = pl.pallas_call(
+        decode_kernel,
+        out_shape=jax.ShapeDtypeStruct((16, 8, 128), F32),
+        in_specs=[vmem()],
+        out_specs=vmem(),
+        cost_estimate=pl.CostEstimate(flops=4 * 10**9, bytes_accessed=10**6, transcendentals=0),
+        compiler_params=params(),
+        name="decode",
+    )(observed)
+    last, mate = lax.optimization_barrier((held[3], mate))
+    swapped.append(core_swap(last))
+    blocks = held + swapped
+
+    meta = observed[:, 6].astype(jnp.int32)
+    listed, count = (meta[:, :MAXL], meta[:, MAXL : MAXL + 1])
+    band = jnp.arange(16)[:, None] + listed // 6 - 1
+    live = (jnp.arange(MAXL)[None] < count) & (band >= 0) & (band < 16)
+    chosen = jnp.where(live, (listed // 2 % 3) * 32 + band * 2 + listed % 2, 192).reshape(16 * MAXL)
 
     both, right, left = pl.pallas_call(
         attention_kernel,
@@ -453,7 +471,6 @@
             [pl.BlockSpec(memory_space=pl.ANY)] * 8,
             vmem(),
             vmem(),
-            vmem(),
         ],
         out_specs=(vmem(), vmem(), vmem()),
         scratch_shapes=[
@@ -461,21 +478,22 @@
             pltpu.VMEM((512, 3 * GF), BF16),
             pltpu.VMEM((512, 128), F32),
             pltpu.VMEM((64, 256), F32),
-            pltpu.SemaphoreType.DMA((32,)),
+            pltpu.SemaphoreType.DMA((3, 32)),
         ],
-        compiler_params=params(61 * 1024 * 1024),
+        compiler_params=params(48 * 1024 * 1024),
         name="attention",
-    )(group.reshape(1), starts, normed, mate, residual, blocks, bias, expected, picks)
+    )(group.reshape(1), starts, normed, mate, residual, blocks, bias, entries)
 
     previous, following, second = (shift(both, 1), shift(right, -1), shift(left, 2))
     selected = pl.pallas_call(
         select_kernel,
         out_shape=jax.ShapeDtypeStruct((16, 8, 128), BF16),
-        in_specs=[vmem()] * 5,
+        in_specs=[smem()] + [vmem()] * 4,
         out_specs=vmem(),
+        scratch_shapes=[pltpu.VMEM((296, 256), F32), pltpu.VMEM((16, 8, 128), F32)],
         compiler_params=params(),
         name="select",
-    )(both, previous, following, second, choice)
+    )(chosen, both, previous, following, second)
     arrived = lax.all_to_all(selected, MEMBER, split_axis=0, concat_axis=0, tiled=True)
     gains_t = gains[0, 0].transpose(0, 2, 1)
     increment = pl.pallas_call(

time: 117 us -> 113 us (0.966)
  starting transfers between devices: 55.6 us -> 50.1 us
  blocking collectives: 13.2 us -> 16.1 us
  local copies, waits for them, and re-layouts: 8.56 us -> 6.02 us
    ppermute x4, starting transfers between devices: 14 us -> 10.5 us  [shift(): return lax.ppermute(x, SPACE, [(i, (i + by) % peers) for i in range(peers)])]
    ppermute x1, waiting for transfers between devices: 1.79 us -> 4.77 us  [body(): held.append(lax.ppermute(held[1], ROW, first))]
    all_to_all x1, blocking collectives: 13.2 us -> 16.1 us  [body(): lax.all_to_all(selected, MEMBER, split_axis=0, concat_axis=0, tiled=True)]
    ppermute x4, starting transfers between devices: 9.97 us -> 8.15 us  [core_swap(): return lax.ppermute(x, 'core', [(0, 1), (1, 0)])]
    pallas_call x1, Pallas kernels: 0.18 us -> 1.93 us  [body(): pl.pallas_call(weights_kernel, out_shape=jax.ShapeDtypeStruct((w_qkv.shap...]
    pallas_call x1, Pallas kernels: 10.2 us -> 8.55 us  [body(): pl.pallas_call(attention_kernel, out_shape=(jax.ShapeDtypeStruct((64, 256...]
    unnamed x50 -> x36, local copies, waits for them, and re-layouts: 6.93 us -> 5.65 us
  transfers between devices with their start and end apart: 15 -> 15, of which waited for: 5 -> 6; matrix products, arithmetic and copies ran while one was open for 2% -> 0% of each run, Pallas kernels for 2% -> 2%
where the time goes in v3:
time: 113 us; the launch traced here: 111 us
  starting transfers between devices  50.1 us (44%)
  waiting for transfers between devices  22.1 us (20%)
  blocking collectives  16.1 us (14%)
  Pallas kernels  15.1 us (13%)
  local copies, waits for them, and re-layouts  6.02 us (5%)
  between operations  1.73 us (2%)
    all_to_all x1, blocking collectives, body(): lax.all_to_all(selected, MEMBER, split_axis=0, concat_axis=0, tiled=True)  16.1 us
    all_to_all x1, starting transfers between devices, body(): lax.all_to_all(notes, MEMBER, split_axis=0, concat_axis=0, tiled=True)  12.4 us
    ppermute x4, starting transfers between devices, shift(): return lax.ppermute(x, SPACE, [(i, (i + by) % peers) for i in range(peers)])  10.5 us
    pallas_call x1, Pallas kernels, body(): pl.pallas_call(attention_kernel, out_shape=(jax.ShapeDtypeStruct((64, 256...  8.55 us
    ppermute x4, starting transfers between devices, core_swap(): return lax.ppermute(x, 'core', [(0, 1), (1, 0)])  8.15 us
    ppermute x1, waiting for transfers between devices, body(): near = lax.ppermute(block, ROW, first)  6.16 us
    unnamed x36, local copies, waits for them, and re-layouts  5.65 us
    ppermute x4, waiting for transfers between devices, shift(): return lax.ppermute(x, SPACE, [(i, (i + by) % peers) for i in range(peers)])  4.86 us
  transfers between devices with their start and end apart: 15, of which 6 were waited for; matrix products, arithmetic and copies ran while one was open for 0% of the time, Pallas kernels for 2%

profile of v3, /device:TPU:6, one launch (start us, length us, event | category | flops | bytes accessed | tf_op | source)
XLA Modules:
  0.0 111.3 jit_solution(12036803948231351113)
XLA Ops:
  0.0 1.9 %weights.1 = bf16[48,1280]{1,0:T(8,128)(2,1)} custom-call(s32[1]{0:T(128)} %bitcast.2.group_ref, bf16[48,2304]{1,0:T(8,128)(2,1)} %w_qkv_ref.1, bf16[24,1536]{1,0:T(8,128)(2,1)} %w_out_ref.1, bf16[69,1536]{1,0:T(8,128)(2,1)} %bitcast.30), custom_call_target="tpu_custom_call" | custom-call | tf_op jit(solution)/shard_map/weights/pallas_call | solution.py:349
  1.9 4.3 %collective-permute-start = (bf16[48,1280]{1,0:T(8,128)(2,1)}, bf16[48,1280]{1,0:T(8,128)(2,1)S(1)}, u32[]{:S(2)}, u32[]{:S(2)}) collective-permute-start(bf16[48,1280]{1,0:T(8,128)(2,1)} %weights.1), channel_id=1, source_target_pairs={{0,16},{16,0},{1,17},{17,1},{2,18},{18,2},{3,19},{19,3},{4,20},{20... | collective-permute-start | bytes 368648 | tf_op jit(solution)/shard_map/ppermute | solution.py:358
  8.2 4.3 %collective-permute-start.2 = (bf16[144,1536]{1,0:T(8,128)(2,1)S(1)}, bf16[144,1536]{1,0:T(8,128)(2,1)S(1)}, u32[]{:S(2)}, u32[]{:S(2)}) collective-permute-start(bf16[144,1536]{1,0:T(8,128)(2,1)S(1)} %edge.1), channel_id=1, source_target_pairs={{0,31},{1,0},{2,1},{3,2},{4,3},{5,4},{6,5},{7,6},{8,7},{9,8},{10,9... | collective-permute-start | bytes 1327112 | tf_op jit(solution)/shard_map/ppermute | solution.py:282
  12.5 2.1 %collective-permute-start.1 = (bf16[96,1280]{1,0:T(8,128)(2,1)S(1)}, bf16[96,1280]{1,0:T(8,128)(2,1)S(1)}, u32[]{:S(2)}, u32[]{:S(2)}) collective-permute-start(bf16[96,1280]{1,0:T(8,128)(2,1)S(1)} %maximum_select_fusion), channel_id=1, source_target_pairs={{0,2},{1,15},{2,0},{3,5},{4,6},{5,3},{6,4},{7,9},{8,10},{9,7},{10,... | collective-permute-start | bytes 737288 | tf_op jit(solution)/shard_map/ppermute | solution.py:363
  14.6 6.2 %collective-permute-done.1 = bf16[96,1280]{1,0:T(8,128)(2,1)S(1)} collective-permute-done((bf16[96,1280]{1,0:T(8,128)(2,1)S(1)}, bf16[96,1280]{1,0:T(8,128)(2,1)S(1)}, u32[]{:S(2)}, u32[]{:S(2)}) %collective-permute-start.1) | collective-permute-done | bytes 245792 | tf_op jit(solution)/shard_map/ppermute | solution.py:363
  20.9 3.8 %collective-permute-start.3 = (bf16[192,1280]{1,0:T(8,128)(2,1)S(1)}, bf16[192,1280]{1,0:T(8,128)(2,1)}, u32[]{:S(2)}, u32[]{:S(2)}) collective-permute-start(bf16[192,1280]{1,0:T(8,128)(2,1)S(1)} %pad_maximum_fusion.blocks_0_), channel_id=1, source_target_pairs={{0,14},{1,3},{2,4},{3,1},{4,2},{5,7},{6,8},{7,5},{8,6},{9,11},{10,... | collective-permute-start | bytes 1474568 | tf_op jit(solution)/shard_map/ppermute | solution.py:376
  26.5 1.9 %collective-permute-start.5 = (bf16[192,1280]{1,0:T(8,128)(2,1)S(1)}, bf16[192,1280]{1,0:T(8,128)(2,1)S(1)}, u32[]{:S(2)}, u32[]{:S(2)}) collective-permute-start(bf16[192,1280]{1,0:T(8,128)(2,1)S(1)} %pad_maximum_fusion.blocks_0_), channel_id=1, source_target_pairs={{0,1},{1,0},{2,3},{3,2},{4,5},{5,4},{6,7},{7,6},{8,9},{9,8},{10,11... | collective-permute-start | bytes 1474568 | tf_op jit(solution)/shard_map/ppermute | solution.py:303
  28.4 2.2 %norm.1 = (bf16[256,1536]{1,0:T(8,128)(2,1)S(1)}, f32[256,128]{1,0:T(8,128)S(1)}, f32[16,8,128]{2,1,0:T(8,128)}) custom-call(s32[4]{0:T(128)S(1)} %bitcast.36, s32[1]{0:T(128)} %bitcast.28.count_ref, bf16[1,32,8,1536]{3,2,1,0:T(8,128)(2,1)S(1)} %copy-done.1, bf16[144,1536]{1,0:T(8,128)(2,1)S(1)} %collective-permute-done.2.halo_ref.extra_ref, ...), custom_call_target="tpu_custom_call" | custom-call | tf_op jit(solution)/shard_map/norm/pallas_call | solution.py:377
  30.6 2.4 %collective-permute-done.3.blocks_1_ = bf16[192,1280]{1,0:T(8,128)(2,1)} collective-permute-done((bf16[192,1280]{1,0:T(8,128)(2,1)S(1)}, bf16[192,1280]{1,0:T(8,128)(2,1)}, u32[]{:S(2)}, u32[]{:S(2)}) %collective-permute-start.3) | collective-permute-done | bytes 491552 | tf_op jit(solution)/shard_map/ppermute | solution.py:376
  33.0 1.9 %collective-permute-start.6 = (bf16[192,1280]{1,0:T(8,128)(2,1)}, bf16[192,1280]{1,0:T(8,128)(2,1)S(1)}, u32[]{:S(2)}, u32[]{:S(2)}) collective-permute-start(bf16[192,1280]{1,0:T(8,128)(2,1)} %collective-permute-done.3.blocks_1_), channel_id=1, source_target_pairs={{0,1},{1,0},{2,3},{3,2},{4,5},{5,4},{6,7},{7,6},{8,9},{9,8},{10,11... | collective-permute-start | bytes 1474568 | tf_op jit(solution)/shard_map/ppermute | solution.py:303
  35.0 1.9 %collective-permute-start.4 = (bf16[192,1280]{1,0:T(8,128)(2,1)}, bf16[192,1280]{1,0:T(8,128)(2,1)}, u32[]{:S(2)}, u32[]{:S(2)}) collective-permute-start(bf16[192,1280]{1,0:T(8,128)(2,1)} %collective-permute-done.3.blocks_1_), channel_id=1, source_target_pairs={{0,2},{1,15},{2,0},{3,5},{4,6},{5,3},{6,4},{7,9},{8,10},{9,7},{10,... | collective-permute-start | bytes 1474568 | tf_op jit(solution)/shard_map/ppermute | solution.py:431
  36.9 2.7 %collective-permute-start.8 = (bf16[256,1536]{1,0:T(8,128)(2,1)S(1)}, bf16[256,1536]{1,0:T(8,128)(2,1)S(1)}, u32[]{:S(2)}, u32[]{:S(2)}) collective-permute-start(bf16[256,1536]{1,0:T(8,128)(2,1)S(1)} %get-tuple-element.25.own_ref), channel_id=1, source_target_pairs={{0,32},{32,0},{64,96},{96,64},{1,33},{33,1},{65,97},{97,65},{2,34}... | collective-permute-start | bytes 2359304 | tf_op jit(solution)/shard_map/ppermute | solution.py:416
  41.2 4.8 %collective-permute-done.4.blocks_2_ = bf16[192,1280]{1,0:T(8,128)(2,1)} collective-permute-done((bf16[192,1280]{1,0:T(8,128)(2,1)}, bf16[192,1280]{1,0:T(8,128)(2,1)}, u32[]{:S(2)}, u32[]{:S(2)}) %collective-permute-start.4) | collective-permute-done | bytes 491552 | tf_op jit(solution)/shard_map/ppermute | solution.py:431
  46.0 4.3 %collective-permute-start.7 = (bf16[192,1280]{1,0:T(8,128)(2,1)}, bf16[192,1280]{1,0:T(8,128)(2,1)}, u32[]{:S(2)}, u32[]{:S(2)}) collective-permute-start(bf16[192,1280]{1,0:T(8,128)(2,1)} %collective-permute-done.4.blocks_2_), channel_id=1, source_target_pairs={{0,14},{1,3},{2,4},{3,1},{4,2},{5,7},{6,8},{7,5},{8,6},{9,11},{10,... | collective-permute-start | bytes 1474568 | tf_op jit(solution)/shard_map/ppermute | solution.py:434
  50.3 12.4 %all-to-all-start = ((f32[16,8,128]{2,1,0:T(8,128)}), f32[16,8,128]{2,1,0:T(8,128)S(1)}, u32[]{:S(2)}, u32[]{:S(2)}) async-start(f32[16,8,128]{2,1,0:T(8,128)} %get-tuple-element.28), calls=%async_computation | async-start | bytes 131072 | tf_op jit(solution)/shard_map/all_to_all | solution.py:438
  62.7 1.9 %collective-permute-start.9 = (bf16[192,1280]{1,0:T(8,128)(2,1)}, bf16[192,1280]{1,0:T(8,128)(2,1)}, u32[]{:S(2)}, u32[]{:S(2)}) collective-permute-start(bf16[192,1280]{1,0:T(8,128)(2,1)} %collective-permute-done.4.blocks_2_), channel_id=1, source_target_pairs={{0,1},{1,0},{2,3},{3,2},{4,5},{5,4},{6,7},{7,6},{8,9},{9,8},{10,11... | collective-permute-start | bytes 1474568 | tf_op jit(solution)/shard_map/ppermute | solution.py:303
  64.6 2.4 %collective-permute-start.10 = (bf16[192,1280]{1,0:T(8,128)(2,1)}, bf16[192,1280]{1,0:T(8,128)(2,1)}, u32[]{:S(2)}, u32[]{:S(2)}) collective-permute-start(bf16[192,1280]{1,0:T(8,128)(2,1)} %collective-permute-done.7.blocks_3_), channel_id=1, source_target_pairs={{0,1},{1,0},{2,3},{3,2},{4,5},{5,4},{6,7},{7,6},{8,9},{9,8},{10,11... | collective-permute-start | bytes 1474568 | tf_op jit(solution)/shard_map/ppermute | solution.py:303
  67.0 3.8 %all-to-all-done.observed_ref = f32[16,8,128]{2,1,0:T(8,128)S(1)} async-done(((f32[16,8,128]{2,1,0:T(8,128)}), f32[16,8,128]{2,1,0:T(8,128)S(1)}, u32[]{:S(2)}, u32[]{:S(2)}) %all-to-all-start) | async-done | bytes 65568 | tf_op jit(solution)/shard_map/all_to_all | solution.py:438
  73.4 8.6 %attention.1 = (bf16[64,256]{1,0:T(8,128)(2,1)S(1)}, bf16[32,256]{1,0:T(8,128)(2,1)S(1)}, bf16[32,256]{1,0:T(8,128)(2,1)S(1)}) custom-call(s32[1]{0:T(128)} %bitcast.2.group_ref, s32[16]{0:T(128)S(1)} %stack.67.starts_ref, bf16[256,1536]{1,0:T(8,128)(2,1)S(1)} %copy-done.5, bf16[256,1536]{1,0:T(8,128)(2,1)S(1)} %collective-permute-done.8.mate_ref, ...), custom_call_target="tpu_custom_call" | custom-call | tf_op jit(solution)/shard_map/attention/pallas_call | solution.py:458
  82.0 1.9 %collective-permute-start.12 = (bf16[32,256]{1,0:T(8,128)(2,1)S(1)}, bf16[32,256]{1,0:T(8,128)(2,1)S(1)}, u32[]{:S(2)}, u32[]{:S(2)}) collective-permute-start(bf16[32,256]{1,0:T(8,128)(2,1)S(1)} %get-tuple-element.37), channel_id=1, source_target_pairs={{0,31},{1,0},{2,1},{3,2},{4,3},{5,4},{6,5},{7,6},{8,7},{9,8},{10,9... | collective-permute-start | bytes 49160 | tf_op jit(solution)/shard_map/ppermute | solution.py:282
  83.9 1.9 %collective-permute-start.13 = (bf16[32,256]{1,0:T(8,128)(2,1)S(1)}, bf16[32,256]{1,0:T(8,128)(2,1)S(1)}, u32[]{:S(2)}, u32[]{:S(2)}) collective-permute-start(bf16[32,256]{1,0:T(8,128)(2,1)S(1)} %get-tuple-element.38), channel_id=1, source_target_pairs={{0,2},{1,3},{2,4},{3,5},{4,6},{5,7},{6,8},{7,9},{8,10},{9,11},{10,... | collective-permute-start | bytes 49160 | tf_op jit(solution)/shard_map/ppermute | solution.py:282
  85.8 2.4 %collective-permute-start.11 = (bf16[64,256]{1,0:T(8,128)(2,1)S(1)}, bf16[64,256]{1,0:T(8,128)(2,1)S(1)}, u32[]{:S(2)}, u32[]{:S(2)}) collective-permute-start(bf16[64,256]{1,0:T(8,128)(2,1)S(1)} %get-tuple-element.36.own_ref), channel_id=1, source_target_pairs={{0,1},{1,2},{2,3},{3,4},{4,5},{5,6},{6,7},{7,8},{8,9},{9,10},{10,1... | collective-permute-start | bytes 98312 | tf_op jit(solution)/shard_map/ppermute | solution.py:282
  88.4 3.2 %collective-permute-done.13.second_ref = bf16[32,256]{1,0:T(8,128)(2,1)S(1)} collective-permute-done((bf16[32,256]{1,0:T(8,128)(2,1)S(1)}, bf16[32,256]{1,0:T(8,128)(2,1)S(1)}, u32[]{:S(2)}, u32[]{:S(2)}) %collective-permute-start.13) | collective-permute-done | bytes 16416 | tf_op jit(solution)/shard_map/ppermute | solution.py:282
  94.0 16.1 %all_to_all.10.arrived_ref = bf16[16,8,128]{2,1,0:T(8,128)(2,1)S(1)} all-to-all(bf16[16,8,128]{2,1,0:T(8,128)(2,1)S(1)} %select.75), channel_id=1, replica_groups=mesh['zhi'=4,'x'=4,'zlo'=2,'y'=8,'core'=2] {'zhi','x'}, dimensions={0} | all-to-all | bytes 65536 | tf_op jit(solution)/shard_map/all_to_all | solution.py:497
  (59 shorter events, 10.3 us)
Async XLA Ops:
  1.9 10.5 %collective-permute-start = (bf16[48,1280]{1,0:T(8,128)(2,1)}, bf16[48,1280]{1,0:T(8,128)(2,1)S(1)}, u32[]{:S(2)}, u32[]{:S(2)}) collective-permute-start(bf16[48,1280]{1,0:T(8,128)(2,1)} %weights.1), channel_id=1, source_target_pairs={{0,16},{16,0},{1,17},{17,1},{2,18},{18,2},{3,19},{19,3},{4,20},{20... | collective-permute-start | bytes 368648 | tf_op jit(solution)/shard_map/ppermute | solution.py:358
  8.2 12.6 %collective-permute-start.2 = (bf16[144,1536]{1,0:T(8,128)(2,1)S(1)}, bf16[144,1536]{1,0:T(8,128)(2,1)S(1)}, u32[]{:S(2)}, u32[]{:S(2)}) collective-permute-start(bf16[144,1536]{1,0:T(8,128)(2,1)S(1)} %edge.1), channel_id=1, source_target_pairs={{0,31},{1,0},{2,1},{3,2},{4,3},{5,4},{6,5},{7,6},{8,7},{9,8},{10,9... | collective-permute-start | bytes 1327112 | tf_op jit(solution)/shard_map/ppermute | solution.py:282
  12.4 13.5 %copy-start.17 = (f32[1536]{0:T(1024)S(1)}, f32[1536]{0:T(1024)}, u32[]{:S(2)}) copy-start(f32[1536]{0:T(1024)} %param.13) | copy-start | bytes 18436
  12.4 13.5 %copy-start.6 = (f32[24,64,64]{2,1,0:T(8,128)S(1)}, f32[24,64,64]{2,1,0:T(8,128)}, u32[]{:S(2)}) copy-start(f32[24,64,64]{2,1,0:T(8,128)} %rel_bias_ref.1) | copy-start | bytes 1179652
  12.5 8.2 %collective-permute-start.1 = (bf16[96,1280]{1,0:T(8,128)(2,1)S(1)}, bf16[96,1280]{1,0:T(8,128)(2,1)S(1)}, u32[]{:S(2)}, u32[]{:S(2)}) collective-permute-start(bf16[96,1280]{1,0:T(8,128)(2,1)S(1)} %maximum_select_fusion), channel_id=1, source_target_pairs={{0,2},{1,15},{2,0},{3,5},{4,6},{5,3},{6,4},{7,9},{8,10},{9,7},{10,... | collective-permute-start | bytes 737288 | tf_op jit(solution)/shard_map/ppermute | solution.py:363
  20.8 7.6 %copy-start.1 = (bf16[1,32,8,1536]{3,2,1,0:T(8,128)(2,1)S(1)}, bf16[1,32,8,1536]{3,2,1,0:T(8,128)(2,1)}, u32[]{:S(2)}) copy-start(bf16[1,32,8,1536]{3,2,1,0:T(8,128)(2,1)} %tokens_ref.3) | copy-start | bytes 2359300
  20.8 7.6 %copy-start.3 = (bf16[1536,69]{0,1:T(8,128)(2,1)S(1)}, bf16[1536,69]{0,1:T(8,128)(2,1)}, u32[]{:S(2)}) copy-start(bf16[1536,69]{0,1:T(8,128)(2,1)} %param.17) | copy-start | bytes 635908
  20.8 7.6 %copy-start.11 = (f32[16,1,1,2,128]{4,3,2,1,0:T(2,128)S(1)}, f32[16,1,1,2,128]{4,3,2,1,0:T(2,128)}, u32[]{:S(2)}) copy-start(f32[16,1,1,2,128]{4,3,2,1,0:T(2,128)} %param.19) | copy-start | bytes 49156
  20.8 7.6 %copy-start.13 = (s32[1,1,2,128]{3,2,1,0:T(2,128)S(1)}, s32[1,1,2,128]{3,2,1,0:T(2,128)}, u32[]{:S(2)}) copy-start(s32[1,1,2,128]{3,2,1,0:T(2,128)} %param.20) | copy-start | bytes 3076
  20.8 7.6 %copy-start.14 = (f32[1,1,2,128]{3,2,1,0:T(2,128)S(1)}, f32[1,1,2,128]{3,2,1,0:T(2,128)}, u32[]{:S(2)}) copy-start(f32[1,1,2,128]{3,2,1,0:T(2,128)} %param.18) | copy-start | bytes 3076
  20.9 12.2 %collective-permute-start.3 = (bf16[192,1280]{1,0:T(8,128)(2,1)S(1)}, bf16[192,1280]{1,0:T(8,128)(2,1)}, u32[]{:S(2)}, u32[]{:S(2)}) collective-permute-start(bf16[192,1280]{1,0:T(8,128)(2,1)S(1)} %pad_maximum_fusion.blocks_0_), channel_id=1, source_target_pairs={{0,14},{1,3},{2,4},{3,1},{4,2},{5,7},{6,8},{7,5},{8,6},{9,11},{10,... | collective-permute-start | bytes 1474568 | tf_op jit(solution)/shard_map/ppermute | solution.py:376
  26.5 13.2 %collective-permute-start.5 = (bf16[192,1280]{1,0:T(8,128)(2,1)S(1)}, bf16[192,1280]{1,0:T(8,128)(2,1)S(1)}, u32[]{:S(2)}, u32[]{:S(2)}) collective-permute-start(bf16[192,1280]{1,0:T(8,128)(2,1)S(1)} %pad_maximum_fusion.blocks_0_), channel_id=1, source_target_pairs={{0,1},{1,0},{2,3},{3,2},{4,5},{5,4},{6,7},{7,6},{8,9},{9,8},{10,11... | collective-permute-start | bytes 1474568 | tf_op jit(solution)/shard_map/ppermute | solution.py:303
  30.6 40.5 %copy-start.4 = (bf16[256,1536]{1,0:T(8,128)(2,1)}, bf16[256,1536]{1,0:T(8,128)(2,1)S(1)}, u32[]{:S(2)}) copy-start(bf16[256,1536]{1,0:T(8,128)(2,1)S(1)} %get-tuple-element.25.own_ref) | copy-start | bytes 2359300
  33.0 7.4 %collective-permute-start.6 = (bf16[192,1280]{1,0:T(8,128)(2,1)}, bf16[192,1280]{1,0:T(8,128)(2,1)S(1)}, u32[]{:S(2)}, u32[]{:S(2)}) collective-permute-start(bf16[192,1280]{1,0:T(8,128)(2,1)} %collective-permute-done.3.blocks_1_), channel_id=1, source_target_pairs={{0,1},{1,0},{2,3},{3,2},{4,5},{5,4},{6,7},{7,6},{8,9},{9,8},{10,11... | collective-permute-start | bytes 1474568 | tf_op jit(solution)/shard_map/ppermute | solution.py:303
  35.0 11.0 %collective-permute-start.4 = (bf16[192,1280]{1,0:T(8,128)(2,1)}, bf16[192,1280]{1,0:T(8,128)(2,1)}, u32[]{:S(2)}, u32[]{:S(2)}) collective-permute-start(bf16[192,1280]{1,0:T(8,128)(2,1)} %collective-permute-done.3.blocks_1_), channel_id=1, source_target_pairs={{0,2},{1,15},{2,0},{3,5},{4,6},{5,3},{6,4},{7,9},{8,10},{9,7},{10,... | collective-permute-start | bytes 1474568 | tf_op jit(solution)/shard_map/ppermute | solution.py:431
  36.9 27.7 %collective-permute-start.8 = (bf16[256,1536]{1,0:T(8,128)(2,1)S(1)}, bf16[256,1536]{1,0:T(8,128)(2,1)S(1)}, u32[]{:S(2)}, u32[]{:S(2)}) collective-permute-start(bf16[256,1536]{1,0:T(8,128)(2,1)S(1)} %get-tuple-element.25.own_ref), channel_id=1, source_target_pairs={{0,32},{32,0},{64,96},{96,64},{1,33},{33,1},{65,97},{97,65},{2,34}... | collective-permute-start | bytes 2359304 | tf_op jit(solution)/shard_map/ppermute | solution.py:416
  46.0 18.6 %collective-permute-start.7 = (bf16[192,1280]{1,0:T(8,128)(2,1)}, bf16[192,1280]{1,0:T(8,128)(2,1)}, u32[]{:S(2)}, u32[]{:S(2)}) collective-permute-start(bf16[192,1280]{1,0:T(8,128)(2,1)} %collective-permute-done.4.blocks_2_), channel_id=1, source_target_pairs={{0,14},{1,3},{2,4},{3,1},{4,2},{5,7},{6,8},{7,5},{8,6},{9,11},{10,... | collective-permute-start | bytes 1474568 | tf_op jit(solution)/shard_map/ppermute | solution.py:434
  50.3 20.6 %all-to-all-start = ((f32[16,8,128]{2,1,0:T(8,128)}), f32[16,8,128]{2,1,0:T(8,128)S(1)}, u32[]{:S(2)}, u32[]{:S(2)}) async-start(f32[16,8,128]{2,1,0:T(8,128)} %get-tuple-element.28), calls=%async_computation | async-start | bytes 131072 | tf_op jit(solution)/shard_map/all_to_all | solution.py:438
  62.7 8.5 %collective-permute-start.9 = (bf16[192,1280]{1,0:T(8,128)(2,1)}, bf16[192,1280]{1,0:T(8,128)(2,1)}, u32[]{:S(2)}, u32[]{:S(2)}) collective-permute-start(bf16[192,1280]{1,0:T(8,128)(2,1)} %collective-permute-done.4.blocks_2_), channel_id=1, source_target_pairs={{0,1},{1,0},{2,3},{3,2},{4,5},{5,4},{6,7},{7,6},{8,9},{9,8},{10,11... | collective-permute-start | bytes 1474568 | tf_op jit(solution)/shard_map/ppermute | solution.py:303
  64.6 6.6 %collective-permute-start.10 = (bf16[192,1280]{1,0:T(8,128)(2,1)}, bf16[192,1280]{1,0:T(8,128)(2,1)}, u32[]{:S(2)}, u32[]{:S(2)}) collective-permute-start(bf16[192,1280]{1,0:T(8,128)(2,1)} %collective-permute-done.7.blocks_3_), channel_id=1, source_target_pairs={{0,1},{1,0},{2,3},{3,2},{4,5},{5,4},{6,7},{7,6},{8,9},{9,8},{10,11... | collective-permute-start | bytes 1474568 | tf_op jit(solution)/shard_map/ppermute | solution.py:303
  73.4 36.7 %copy-start.2 = (bf16[1,1,4,128,1104]{3,4,2,1,0:T(8,128)(2,1)S(1)}, bf16[1,1,4,128,1104]{3,4,2,1,0:T(8,128)(2,1)}, u32[]{:S(2)}) copy-start(bf16[1,1,4,128,1104]{3,4,2,1,0:T(8,128)(2,1)} %param.23) | copy-start | bytes 3391492
  82.0 6.4 %collective-permute-start.12 = (bf16[32,256]{1,0:T(8,128)(2,1)S(1)}, bf16[32,256]{1,0:T(8,128)(2,1)S(1)}, u32[]{:S(2)}, u32[]{:S(2)}) collective-permute-start(bf16[32,256]{1,0:T(8,128)(2,1)S(1)} %get-tuple-element.37), channel_id=1, source_target_pairs={{0,31},{1,0},{2,1},{3,2},{4,3},{5,4},{6,5},{7,6},{8,7},{9,8},{10,9... | collective-permute-start | bytes 49160 | tf_op jit(solution)/shard_map/ppermute | solution.py:282
  83.9 7.7 %collective-permute-start.13 = (bf16[32,256]{1,0:T(8,128)(2,1)S(1)}, bf16[32,256]{1,0:T(8,128)(2,1)S(1)}, u32[]{:S(2)}, u32[]{:S(2)}) collective-permute-start(bf16[32,256]{1,0:T(8,128)(2,1)S(1)} %get-tuple-element.38), channel_id=1, source_target_pairs={{0,2},{1,3},{2,4},{3,5},{4,6},{5,7},{6,8},{7,9},{8,10},{9,11},{10,... | collective-permute-start | bytes 49160 | tf_op jit(solution)/shard_map/ppermute | solution.py:282
  85.8 7.4 %collective-permute-start.11 = (bf16[64,256]{1,0:T(8,128)(2,1)S(1)}, bf16[64,256]{1,0:T(8,128)(2,1)S(1)}, u32[]{:S(2)}, u32[]{:S(2)}) collective-permute-start(bf16[64,256]{1,0:T(8,128)(2,1)S(1)} %get-tuple-element.36.own_ref), channel_id=1, source_target_pairs={{0,1},{1,2},{2,3},{3,4},{4,5},{5,6},{6,7},{7,8},{8,9},{9,10},{10,1... | collective-permute-start | bytes 98312 | tf_op jit(solution)/shard_map/ppermute | solution.py:282
  (9 other events, 18.8 us)

commit v4 on v3

--- a/solution.py
+++ b/solution.py
@@ -130,26 +130,14 @@
     qkv,
     fields,
     sums,
-    sems,
 ):
-    copies = []
-    for part, lanes in enumerate((slice(0, GF), slice(GF, 2 * GF), slice(2 * GF, WCOLS))):
-        for i, block in enumerate(blocks):
-            for half in range(2):
-                for low in range(2):
-                    start = pl.multiple_of(starts_ref[2 * i + half] + 768 * low, 48)
-                    copies.append(
-                        pltpu.make_async_copy(
-                            block.at[pl.ds(96 * half + 48 * low, 48), lanes],
-                            weights.at[pl.ds(start, 48), lanes],
-                            sems.at[part, 4 * i + 2 * half + low],
-                        )
-                    )
-    for copy in copies:
-        copy.start()
+    for i, block in enumerate(blocks):
+        for half in range(2):
+            for low in range(2):
+                start = pl.multiple_of(starts_ref[2 * i + half] + 768 * low, 48)
+                row = 96 * half + 48 * low
+                weights[pl.ds(start, 48), :] = block[row : row + 48]
     for part in range(3):
-        for copy in copies[32 * part : 32 * (part + 1)]:
-            copy.wait()
         lanes = slice(part * GF, (part + 1) * GF)
         for member, source in enumerate((own_ref, mate_ref)):
             qkv[member * 256 : (member + 1) * 256, lanes] = dot(source[...], weights[:, lanes]).astype(BF16)
@@ -430,7 +418,7 @@
     held[1], bias, starts, _ = lax.optimization_barrier((held[1], bias, starts, normed))
     held.append(lax.ppermute(held[1], ROW, first))
     swapped = [core_swap(held[0]), core_swap(held[1])]
-    held[2], *swapped = lax.optimization_barrier((held[2], *swapped))
+    held[2], swapped[0] = lax.optimization_barrier((held[2], swapped[0]))
     held.append(lax.ppermute(held[2], ROW, second))
     swapped.append(core_swap(held[2]))
 
@@ -445,7 +433,7 @@
         compiler_params=params(),
         name="decode",
     )(observed)
-    last, mate = lax.optimization_barrier((held[3], mate))
+    last, mate, swapped[1] = lax.optimization_barrier((held[3], mate, swapped[1]))
     swapped.append(core_swap(last))
     blocks = held + swapped
 
@@ -468,7 +456,7 @@
             vmem(),
             vmem(),
             vmem(),
-            [pl.BlockSpec(memory_space=pl.ANY)] * 8,
+            [vmem()] * 8,
             vmem(),
             vmem(),
         ],
@@ -478,7 +466,6 @@
             pltpu.VMEM((512, 3 * GF), BF16),
             pltpu.VMEM((512, 128), F32),
             pltpu.VMEM((64, 256), F32),
-            pltpu.SemaphoreType.DMA((3, 32)),
         ],
         compiler_params=params(48 * 1024 * 1024),
         name="attention",

time: 113 us -> 110 us (0.973)
  waiting for transfers between devices: 22.1 us -> 19.1 us
    ppermute x1, waiting for transfers between devices: 4.77 us -> 1.79 us  [body(): held.append(lax.ppermute(held[1], ROW, first))]
    ppermute x4, starting transfers between devices: 8.15 us -> 10 us  [core_swap(): return lax.ppermute(x, 'core', [(0, 1), (1, 0)])]
    unnamed x36 -> x32, local copies, waits for them, and re-layouts: 5.65 us -> 4.73 us
where the time goes in v4:
time: 110 us; the launch traced here: 108 us
  starting transfers between devices  51.2 us (47%)
  waiting for transfers between devices  19.1 us (17%)
  blocking collectives  16.9 us (15%)
  Pallas kernels  14.2 us (13%)
  local copies, waits for them, and re-layouts  5.1 us (5%)
  between operations  1.73 us (2%)
    all_to_all x1, blocking collectives, body(): lax.all_to_all(selected, MEMBER, split_axis=0, concat_axis=0, tiled=True)  16.9 us
    all_to_all x1, starting transfers between devices, body(): lax.all_to_all(notes, MEMBER, split_axis=0, concat_axis=0, tiled=True)  12.4 us
    ppermute x4, starting transfers between devices, shift(): return lax.ppermute(x, SPACE, [(i, (i + by) % peers) for i in range(peers)])  10.5 us
    ppermute x4, starting transfers between devices, core_swap(): return lax.ppermute(x, 'core', [(0, 1), (1, 0)])  10 us
    pallas_call x1, Pallas kernels, body(): pl.pallas_call(attention_kernel, out_shape=(jax.ShapeDtypeStruct((64, 256...  7.63 us
    ppermute x1, waiting for transfers between devices, body(): near = lax.ppermute(block, ROW, first)  6.16 us
    ppermute x4, waiting for transfers between devices, shift(): return lax.ppermute(x, SPACE, [(i, (i + by) % peers) for i in range(peers)])  4.86 us
    unnamed x32, local copies, waits for them, and re-layouts  4.73 us
  transfers between devices with their start and end apart: 15, of which 6 were waited for; matrix products, arithmetic and copies ran while one was open for 0% of the time, Pallas kernels for 2%

profile of v4, /device:TPU:6, one launch (start us, length us, event | category | flops | bytes accessed | tf_op | source)
XLA Modules:
  0.0 108.4 jit_solution(13329376851338125540)
XLA Ops:
  0.0 1.9 %weights.1 = bf16[48,1280]{1,0:T(8,128)(2,1)} custom-call(s32[1]{0:T(128)} %bitcast.2.group_ref, bf16[48,2304]{1,0:T(8,128)(2,1)} %w_qkv_ref.1, bf16[24,1536]{1,0:T(8,128)(2,1)} %w_out_ref.1, bf16[69,1536]{1,0:T(8,128)(2,1)} %bitcast.30), custom_call_target="tpu_custom_call" | custom-call | tf_op jit(solution)/shard_map/weights/pallas_call | solution.py:337
  1.9 4.3 %collective-permute-start = (bf16[48,1280]{1,0:T(8,128)(2,1)}, bf16[48,1280]{1,0:T(8,128)(2,1)S(1)}, u32[]{:S(2)}, u32[]{:S(2)}) collective-permute-start(bf16[48,1280]{1,0:T(8,128)(2,1)} %weights.1), channel_id=1, source_target_pairs={{0,16},{16,0},{1,17},{17,1},{2,18},{18,2},{3,19},{19,3},{4,20},{20... | collective-permute-start | bytes 368648 | tf_op jit(solution)/shard_map/ppermute | solution.py:346
  8.2 4.3 %collective-permute-start.2 = (bf16[144,1536]{1,0:T(8,128)(2,1)S(1)}, bf16[144,1536]{1,0:T(8,128)(2,1)S(1)}, u32[]{:S(2)}, u32[]{:S(2)}) collective-permute-start(bf16[144,1536]{1,0:T(8,128)(2,1)S(1)} %edge.1), channel_id=1, source_target_pairs={{0,31},{1,0},{2,1},{3,2},{4,3},{5,4},{6,5},{7,6},{8,7},{9,8},{10,9... | collective-permute-start | bytes 1327112 | tf_op jit(solution)/shard_map/ppermute | solution.py:270
  12.5 2.1 %collective-permute-start.1 = (bf16[96,1280]{1,0:T(8,128)(2,1)S(1)}, bf16[96,1280]{1,0:T(8,128)(2,1)S(1)}, u32[]{:S(2)}, u32[]{:S(2)}) collective-permute-start(bf16[96,1280]{1,0:T(8,128)(2,1)S(1)} %maximum_select_fusion), channel_id=1, source_target_pairs={{0,2},{1,15},{2,0},{3,5},{4,6},{5,3},{6,4},{7,9},{8,10},{9,7},{10,... | collective-permute-start | bytes 737288 | tf_op jit(solution)/shard_map/ppermute | solution.py:351
  14.6 6.2 %collective-permute-done.1 = bf16[96,1280]{1,0:T(8,128)(2,1)S(1)} collective-permute-done((bf16[96,1280]{1,0:T(8,128)(2,1)S(1)}, bf16[96,1280]{1,0:T(8,128)(2,1)S(1)}, u32[]{:S(2)}, u32[]{:S(2)}) %collective-permute-start.1) | collective-permute-done | bytes 245792 | tf_op jit(solution)/shard_map/ppermute | solution.py:351
  20.9 3.8 %collective-permute-start.3 = (bf16[192,1280]{1,0:T(8,128)(2,1)S(1)}, bf16[192,1280]{1,0:T(8,128)(2,1)}, u32[]{:S(2)}, u32[]{:S(2)}) collective-permute-start(bf16[192,1280]{1,0:T(8,128)(2,1)S(1)} %pad_maximum_fusion.blocks_0_), channel_id=1, source_target_pairs={{0,14},{1,3},{2,4},{3,1},{4,2},{5,7},{6,8},{7,5},{8,6},{9,11},{10,... | collective-permute-start | bytes 1474568 | tf_op jit(solution)/shard_map/ppermute | solution.py:364
  26.5 1.9 %collective-permute-start.5 = (bf16[192,1280]{1,0:T(8,128)(2,1)S(1)}, bf16[192,1280]{1,0:T(8,128)(2,1)S(1)}, u32[]{:S(2)}, u32[]{:S(2)}) collective-permute-start(bf16[192,1280]{1,0:T(8,128)(2,1)S(1)} %pad_maximum_fusion.blocks_0_), channel_id=1, source_target_pairs={{0,1},{1,0},{2,3},{3,2},{4,5},{5,4},{6,7},{7,6},{8,9},{9,8},{10,11... | collective-permute-start | bytes 1474568 | tf_op jit(solution)/shard_map/ppermute | solution.py:291
  28.4 2.2 %norm.1 = (bf16[256,1536]{1,0:T(8,128)(2,1)S(1)}, f32[256,128]{1,0:T(8,128)S(1)}, f32[16,8,128]{2,1,0:T(8,128)}) custom-call(s32[4]{0:T(128)S(1)} %bitcast.36, s32[1]{0:T(128)} %bitcast.28.count_ref, bf16[1,32,8,1536]{3,2,1,0:T(8,128)(2,1)S(1)} %copy-done.1, bf16[144,1536]{1,0:T(8,128)(2,1)S(1)} %collective-permute-done.2.halo_ref.extra_ref, ...), custom_call_target="tpu_custom_call" | custom-call | tf_op jit(solution)/shard_map/norm/pallas_call | solution.py:365
  30.6 2.4 %collective-permute-done.3.blocks_1_ = bf16[192,1280]{1,0:T(8,128)(2,1)} collective-permute-done((bf16[192,1280]{1,0:T(8,128)(2,1)S(1)}, bf16[192,1280]{1,0:T(8,128)(2,1)}, u32[]{:S(2)}, u32[]{:S(2)}) %collective-permute-start.3) | collective-permute-done | bytes 491552 | tf_op jit(solution)/shard_map/ppermute | solution.py:364
  33.0 1.9 %collective-permute-start.4 = (bf16[192,1280]{1,0:T(8,128)(2,1)}, bf16[192,1280]{1,0:T(8,128)(2,1)}, u32[]{:S(2)}, u32[]{:S(2)}) collective-permute-start(bf16[192,1280]{1,0:T(8,128)(2,1)} %collective-permute-done.3.blocks_1_), channel_id=1, source_target_pairs={{0,2},{1,15},{2,0},{3,5},{4,6},{5,3},{6,4},{7,9},{8,10},{9,7},{10,... | collective-permute-start | bytes 1474568 | tf_op jit(solution)/shard_map/ppermute | solution.py:419
  35.0 2.7 %collective-permute-start.7 = (bf16[256,1536]{1,0:T(8,128)(2,1)S(1)}, bf16[256,1536]{1,0:T(8,128)(2,1)S(1)}, u32[]{:S(2)}, u32[]{:S(2)}) collective-permute-start(bf16[256,1536]{1,0:T(8,128)(2,1)S(1)} %get-tuple-element.25.own_ref), channel_id=1, source_target_pairs={{0,32},{32,0},{64,96},{96,64},{1,33},{33,1},{65,97},{97,65},{2,34}... | collective-permute-start | bytes 2359304 | tf_op jit(solution)/shard_map/ppermute | solution.py:404
  37.7 3.8 %collective-permute-start.8 = (bf16[192,1280]{1,0:T(8,128)(2,1)}, bf16[192,1280]{1,0:T(8,128)(2,1)}, u32[]{:S(2)}, u32[]{:S(2)}) collective-permute-start(bf16[192,1280]{1,0:T(8,128)(2,1)} %collective-permute-done.3.blocks_1_), channel_id=1, source_target_pairs={{0,1},{1,0},{2,3},{3,2},{4,5},{5,4},{6,7},{7,6},{8,9},{9,8},{10,11... | collective-permute-start | bytes 1474568 | tf_op jit(solution)/shard_map/ppermute | solution.py:291
  42.3 1.8 %collective-permute-done.4.blocks_2_ = bf16[192,1280]{1,0:T(8,128)(2,1)} collective-permute-done((bf16[192,1280]{1,0:T(8,128)(2,1)}, bf16[192,1280]{1,0:T(8,128)(2,1)}, u32[]{:S(2)}, u32[]{:S(2)}) %collective-permute-start.4) | collective-permute-done | bytes 491552 | tf_op jit(solution)/shard_map/ppermute | solution.py:419
  44.1 3.6 %collective-permute-start.6 = (bf16[192,1280]{1,0:T(8,128)(2,1)}, bf16[192,1280]{1,0:T(8,128)(2,1)}, u32[]{:S(2)}, u32[]{:S(2)}) collective-permute-start(bf16[192,1280]{1,0:T(8,128)(2,1)} %collective-permute-done.4.blocks_2_), channel_id=1, source_target_pairs={{0,14},{1,3},{2,4},{3,1},{4,2},{5,7},{6,8},{7,5},{8,6},{9,11},{10,... | collective-permute-start | bytes 1474568 | tf_op jit(solution)/shard_map/ppermute | solution.py:422
  47.7 12.4 %all-to-all-start = ((f32[16,8,128]{2,1,0:T(8,128)}), f32[16,8,128]{2,1,0:T(8,128)S(1)}, u32[]{:S(2)}, u32[]{:S(2)}) async-start(f32[16,8,128]{2,1,0:T(8,128)} %get-tuple-element.28), calls=%async_computation | async-start | bytes 131072 | tf_op jit(solution)/shard_map/all_to_all | solution.py:426
  60.1 1.9 %collective-permute-start.9 = (bf16[192,1280]{1,0:T(8,128)(2,1)}, bf16[192,1280]{1,0:T(8,128)(2,1)}, u32[]{:S(2)}, u32[]{:S(2)}) collective-permute-start(bf16[192,1280]{1,0:T(8,128)(2,1)} %collective-permute-done.4.blocks_2_), channel_id=1, source_target_pairs={{0,1},{1,0},{2,3},{3,2},{4,5},{5,4},{6,7},{7,6},{8,9},{9,8},{10,11... | collective-permute-start | bytes 1474568 | tf_op jit(solution)/shard_map/ppermute | solution.py:291
  62.0 2.4 %collective-permute-start.10 = (bf16[192,1280]{1,0:T(8,128)(2,1)}, bf16[192,1280]{1,0:T(8,128)(2,1)}, u32[]{:S(2)}, u32[]{:S(2)}) collective-permute-start(bf16[192,1280]{1,0:T(8,128)(2,1)} %collective-permute-done.6.blocks_3_), channel_id=1, source_target_pairs={{0,1},{1,0},{2,3},{3,2},{4,5},{5,4},{6,7},{7,6},{8,9},{9,8},{10,11... | collective-permute-start | bytes 1474568 | tf_op jit(solution)/shard_map/ppermute | solution.py:291
  64.4 3.8 %all-to-all-done.observed_ref = f32[16,8,128]{2,1,0:T(8,128)S(1)} async-done(((f32[16,8,128]{2,1,0:T(8,128)}), f32[16,8,128]{2,1,0:T(8,128)S(1)}, u32[]{:S(2)}, u32[]{:S(2)}) %all-to-all-start) | async-done | bytes 65568 | tf_op jit(solution)/shard_map/all_to_all | solution.py:426
  70.6 7.6 %attention.1 = (bf16[64,256]{1,0:T(8,128)(2,1)S(1)}, bf16[32,256]{1,0:T(8,128)(2,1)S(1)}, bf16[32,256]{1,0:T(8,128)(2,1)S(1)}) custom-call(s32[1]{0:T(128)} %bitcast.2.group_ref, s32[16]{0:T(128)S(1)} %stack.67.starts_ref, bf16[256,1536]{1,0:T(8,128)(2,1)S(1)} %copy-done.5, bf16[256,1536]{1,0:T(8,128)(2,1)S(1)} %collective-permute-done.7.mate_ref, ...), custom_call_target="tpu_custom_call" | custom-call | tf_op jit(solution)/shard_map/attention/pallas_call | solution.py:446
  78.3 1.9 %collective-permute-start.12 = (bf16[32,256]{1,0:T(8,128)(2,1)S(1)}, bf16[32,256]{1,0:T(8,128)(2,1)S(1)}, u32[]{:S(2)}, u32[]{:S(2)}) collective-permute-start(bf16[32,256]{1,0:T(8,128)(2,1)S(1)} %get-tuple-element.37), channel_id=1, source_target_pairs={{0,31},{1,0},{2,1},{3,2},{4,3},{5,4},{6,5},{7,6},{8,7},{9,8},{10,9... | collective-permute-start | bytes 49160 | tf_op jit(solution)/shard_map/ppermute | solution.py:270
  80.2 1.9 %collective-permute-start.13 = (bf16[32,256]{1,0:T(8,128)(2,1)S(1)}, bf16[32,256]{1,0:T(8,128)(2,1)S(1)}, u32[]{:S(2)}, u32[]{:S(2)}) collective-permute-start(bf16[32,256]{1,0:T(8,128)(2,1)S(1)} %get-tuple-element.38), channel_id=1, source_target_pairs={{0,2},{1,3},{2,4},{3,5},{4,6},{5,7},{6,8},{7,9},{8,10},{9,11},{10,... | collective-permute-start | bytes 49160 | tf_op jit(solution)/shard_map/ppermute | solution.py:270
  82.1 2.4 %collective-permute-start.11 = (bf16[64,256]{1,0:T(8,128)(2,1)S(1)}, bf16[64,256]{1,0:T(8,128)(2,1)S(1)}, u32[]{:S(2)}, u32[]{:S(2)}) collective-permute-start(bf16[64,256]{1,0:T(8,128)(2,1)S(1)} %get-tuple-element.36.own_ref), channel_id=1, source_target_pairs={{0,1},{1,2},{2,3},{3,4},{4,5},{5,6},{6,7},{7,8},{8,9},{9,10},{10,1... | collective-permute-start | bytes 98312 | tf_op jit(solution)/shard_map/ppermute | solution.py:270
  84.7 3.2 %collective-permute-done.13.second_ref = bf16[32,256]{1,0:T(8,128)(2,1)S(1)} collective-permute-done((bf16[32,256]{1,0:T(8,128)(2,1)S(1)}, bf16[32,256]{1,0:T(8,128)(2,1)S(1)}, u32[]{:S(2)}, u32[]{:S(2)}) %collective-permute-start.13) | collective-permute-done | bytes 16416 | tf_op jit(solution)/shard_map/ppermute | solution.py:270
  90.4 16.9 %all_to_all.10.arrived_ref = bf16[16,8,128]{2,1,0:T(8,128)(2,1)S(1)} all-to-all(bf16[16,8,128]{2,1,0:T(8,128)(2,1)S(1)} %select.75), channel_id=1, replica_groups=mesh['zhi'=4,'x'=4,'zlo'=2,'y'=8,'core'=2] {'zhi','x'}, dimensions={0} | all-to-all | bytes 65536 | tf_op jit(solution)/shard_map/all_to_all | solution.py:484
  (55 shorter events, 9.4 us)
Async XLA Ops:
  1.9 10.5 %collective-permute-start = (bf16[48,1280]{1,0:T(8,128)(2,1)}, bf16[48,1280]{1,0:T(8,128)(2,1)S(1)}, u32[]{:S(2)}, u32[]{:S(2)}) collective-permute-start(bf16[48,1280]{1,0:T(8,128)(2,1)} %weights.1), channel_id=1, source_target_pairs={{0,16},{16,0},{1,17},{17,1},{2,18},{18,2},{3,19},{19,3},{4,20},{20... | collective-permute-start | bytes 368648 | tf_op jit(solution)/shard_map/ppermute | solution.py:346
  8.2 12.6 %collective-permute-start.2 = (bf16[144,1536]{1,0:T(8,128)(2,1)S(1)}, bf16[144,1536]{1,0:T(8,128)(2,1)S(1)}, u32[]{:S(2)}, u32[]{:S(2)}) collective-permute-start(bf16[144,1536]{1,0:T(8,128)(2,1)S(1)} %edge.1), channel_id=1, source_target_pairs={{0,31},{1,0},{2,1},{3,2},{4,3},{5,4},{6,5},{7,6},{8,7},{9,8},{10,9... | collective-permute-start | bytes 1327112 | tf_op jit(solution)/shard_map/ppermute | solution.py:270
  12.4 13.5 %copy-start.15 = (f32[1536]{0:T(1024)S(1)}, f32[1536]{0:T(1024)}, u32[]{:S(2)}) copy-start(f32[1536]{0:T(1024)} %param.13) | copy-start | bytes 18436
  12.4 13.5 %copy-start.6 = (f32[24,64,64]{2,1,0:T(8,128)S(1)}, f32[24,64,64]{2,1,0:T(8,128)}, u32[]{:S(2)}) copy-start(f32[24,64,64]{2,1,0:T(8,128)} %rel_bias_ref.1) | copy-start | bytes 1179652
  12.5 8.2 %collective-permute-start.1 = (bf16[96,1280]{1,0:T(8,128)(2,1)S(1)}, bf16[96,1280]{1,0:T(8,128)(2,1)S(1)}, u32[]{:S(2)}, u32[]{:S(2)}) collective-permute-start(bf16[96,1280]{1,0:T(8,128)(2,1)S(1)} %maximum_select_fusion), channel_id=1, source_target_pairs={{0,2},{1,15},{2,0},{3,5},{4,6},{5,3},{6,4},{7,9},{8,10},{9,7},{10,... | collective-permute-start | bytes 737288 | tf_op jit(solution)/shard_map/ppermute | solution.py:351
  20.8 7.6 %copy-start.1 = (bf16[1,32,8,1536]{3,2,1,0:T(8,128)(2,1)S(1)}, bf16[1,32,8,1536]{3,2,1,0:T(8,128)(2,1)}, u32[]{:S(2)}) copy-start(bf16[1,32,8,1536]{3,2,1,0:T(8,128)(2,1)} %tokens_ref.3) | copy-start | bytes 2359300
  20.8 7.6 %copy-start.3 = (bf16[1536,69]{0,1:T(8,128)(2,1)S(1)}, bf16[1536,69]{0,1:T(8,128)(2,1)}, u32[]{:S(2)}) copy-start(bf16[1536,69]{0,1:T(8,128)(2,1)} %param.17) | copy-start | bytes 635908
  20.8 7.6 %copy-start.9 = (f32[16,1,1,2,128]{4,3,2,1,0:T(2,128)S(1)}, f32[16,1,1,2,128]{4,3,2,1,0:T(2,128)}, u32[]{:S(2)}) copy-start(f32[16,1,1,2,128]{4,3,2,1,0:T(2,128)} %param.19) | copy-start | bytes 49156
  20.8 7.6 %copy-start.11 = (s32[1,1,2,128]{3,2,1,0:T(2,128)S(1)}, s32[1,1,2,128]{3,2,1,0:T(2,128)}, u32[]{:S(2)}) copy-start(s32[1,1,2,128]{3,2,1,0:T(2,128)} %param.20) | copy-start | bytes 3076
  20.8 7.6 %copy-start.12 = (f32[1,1,2,128]{3,2,1,0:T(2,128)S(1)}, f32[1,1,2,128]{3,2,1,0:T(2,128)}, u32[]{:S(2)}) copy-start(f32[1,1,2,128]{3,2,1,0:T(2,128)} %param.18) | copy-start | bytes 3076
  20.9 12.2 %collective-permute-start.3 = (bf16[192,1280]{1,0:T(8,128)(2,1)S(1)}, bf16[192,1280]{1,0:T(8,128)(2,1)}, u32[]{:S(2)}, u32[]{:S(2)}) collective-permute-start(bf16[192,1280]{1,0:T(8,128)(2,1)S(1)} %pad_maximum_fusion.blocks_0_), channel_id=1, source_target_pairs={{0,14},{1,3},{2,4},{3,1},{4,2},{5,7},{6,8},{7,5},{8,6},{9,11},{10,... | collective-permute-start | bytes 1474568 | tf_op jit(solution)/shard_map/ppermute | solution.py:364
  26.5 15.0 %collective-permute-start.5 = (bf16[192,1280]{1,0:T(8,128)(2,1)S(1)}, bf16[192,1280]{1,0:T(8,128)(2,1)S(1)}, u32[]{:S(2)}, u32[]{:S(2)}) collective-permute-start(bf16[192,1280]{1,0:T(8,128)(2,1)S(1)} %pad_maximum_fusion.blocks_0_), channel_id=1, source_target_pairs={{0,1},{1,0},{2,3},{3,2},{4,5},{5,4},{6,7},{7,6},{8,9},{9,8},{10,11... | collective-permute-start | bytes 1474568 | tf_op jit(solution)/shard_map/ppermute | solution.py:291
  30.6 37.9 %copy-start.4 = (bf16[256,1536]{1,0:T(8,128)(2,1)}, bf16[256,1536]{1,0:T(8,128)(2,1)S(1)}, u32[]{:S(2)}) copy-start(bf16[256,1536]{1,0:T(8,128)(2,1)S(1)} %get-tuple-element.25.own_ref) | copy-start | bytes 2359300
  33.0 11.0 %collective-permute-start.4 = (bf16[192,1280]{1,0:T(8,128)(2,1)}, bf16[192,1280]{1,0:T(8,128)(2,1)}, u32[]{:S(2)}, u32[]{:S(2)}) collective-permute-start(bf16[192,1280]{1,0:T(8,128)(2,1)} %collective-permute-done.3.blocks_1_), channel_id=1, source_target_pairs={{0,2},{1,15},{2,0},{3,5},{4,6},{5,3},{6,4},{7,9},{8,10},{9,7},{10,... | collective-permute-start | bytes 1474568 | tf_op jit(solution)/shard_map/ppermute | solution.py:419
  35.0 27.0 %collective-permute-start.7 = (bf16[256,1536]{1,0:T(8,128)(2,1)S(1)}, bf16[256,1536]{1,0:T(8,128)(2,1)S(1)}, u32[]{:S(2)}, u32[]{:S(2)}) collective-permute-start(bf16[256,1536]{1,0:T(8,128)(2,1)S(1)} %get-tuple-element.25.own_ref), channel_id=1, source_target_pairs={{0,32},{32,0},{64,96},{96,64},{1,33},{33,1},{65,97},{97,65},{2,34}... | collective-permute-start | bytes 2359304 | tf_op jit(solution)/shard_map/ppermute | solution.py:404
  37.7 24.3 %collective-permute-start.8 = (bf16[192,1280]{1,0:T(8,128)(2,1)}, bf16[192,1280]{1,0:T(8,128)(2,1)}, u32[]{:S(2)}, u32[]{:S(2)}) collective-permute-start(bf16[192,1280]{1,0:T(8,128)(2,1)} %collective-permute-done.3.blocks_1_), channel_id=1, source_target_pairs={{0,1},{1,0},{2,3},{3,2},{4,5},{5,4},{6,7},{7,6},{8,9},{9,8},{10,11... | collective-permute-start | bytes 1474568 | tf_op jit(solution)/shard_map/ppermute | solution.py:291
  44.1 17.9 %collective-permute-start.6 = (bf16[192,1280]{1,0:T(8,128)(2,1)}, bf16[192,1280]{1,0:T(8,128)(2,1)}, u32[]{:S(2)}, u32[]{:S(2)}) collective-permute-start(bf16[192,1280]{1,0:T(8,128)(2,1)} %collective-permute-done.4.blocks_2_), channel_id=1, source_target_pairs={{0,14},{1,3},{2,4},{3,1},{4,2},{5,7},{6,8},{7,5},{8,6},{9,11},{10,... | collective-permute-start | bytes 1474568 | tf_op jit(solution)/shard_map/ppermute | solution.py:422
  47.7 20.6 %all-to-all-start = ((f32[16,8,128]{2,1,0:T(8,128)}), f32[16,8,128]{2,1,0:T(8,128)S(1)}, u32[]{:S(2)}, u32[]{:S(2)}) async-start(f32[16,8,128]{2,1,0:T(8,128)} %get-tuple-element.28), calls=%async_computation | async-start | bytes 131072 | tf_op jit(solution)/shard_map/all_to_all | solution.py:426
  60.1 8.5 %collective-permute-start.9 = (bf16[192,1280]{1,0:T(8,128)(2,1)}, bf16[192,1280]{1,0:T(8,128)(2,1)}, u32[]{:S(2)}, u32[]{:S(2)}) collective-permute-start(bf16[192,1280]{1,0:T(8,128)(2,1)} %collective-permute-done.4.blocks_2_), channel_id=1, source_target_pairs={{0,1},{1,0},{2,3},{3,2},{4,5},{5,4},{6,7},{7,6},{8,9},{9,8},{10,11... | collective-permute-start | bytes 1474568 | tf_op jit(solution)/shard_map/ppermute | solution.py:291
  62.0 6.5 %collective-permute-start.10 = (bf16[192,1280]{1,0:T(8,128)(2,1)}, bf16[192,1280]{1,0:T(8,128)(2,1)}, u32[]{:S(2)}, u32[]{:S(2)}) collective-permute-start(bf16[192,1280]{1,0:T(8,128)(2,1)} %collective-permute-done.6.blocks_3_), channel_id=1, source_target_pairs={{0,1},{1,0},{2,3},{3,2},{4,5},{5,4},{6,7},{7,6},{8,9},{9,8},{10,11... | collective-permute-start | bytes 1474568 | tf_op jit(solution)/shard_map/ppermute | solution.py:291
  70.6 36.6 %copy-start.2 = (bf16[1,1,4,128,1104]{3,4,2,1,0:T(8,128)(2,1)S(1)}, bf16[1,1,4,128,1104]{3,4,2,1,0:T(8,128)(2,1)}, u32[]{:S(2)}) copy-start(bf16[1,1,4,128,1104]{3,4,2,1,0:T(8,128)(2,1)} %param.23) | copy-start | bytes 3391492
  78.3 6.4 %collective-permute-start.12 = (bf16[32,256]{1,0:T(8,128)(2,1)S(1)}, bf16[32,256]{1,0:T(8,128)(2,1)S(1)}, u32[]{:S(2)}, u32[]{:S(2)}) collective-permute-start(bf16[32,256]{1,0:T(8,128)(2,1)S(1)} %get-tuple-element.37), channel_id=1, source_target_pairs={{0,31},{1,0},{2,1},{3,2},{4,3},{5,4},{6,5},{7,6},{8,7},{9,8},{10,9... | collective-permute-start | bytes 49160 | tf_op jit(solution)/shard_map/ppermute | solution.py:270
  80.2 7.7 %collective-permute-start.13 = (bf16[32,256]{1,0:T(8,128)(2,1)S(1)}, bf16[32,256]{1,0:T(8,128)(2,1)S(1)}, u32[]{:S(2)}, u32[]{:S(2)}) collective-permute-start(bf16[32,256]{1,0:T(8,128)(2,1)S(1)} %get-tuple-element.38), channel_id=1, source_target_pairs={{0,2},{1,3},{2,4},{3,5},{4,6},{5,7},{6,8},{7,9},{8,10},{9,11},{10,... | collective-permute-start | bytes 49160 | tf_op jit(solution)/shard_map/ppermute | solution.py:270
  82.1 7.4 %collective-permute-start.11 = (bf16[64,256]{1,0:T(8,128)(2,1)S(1)}, bf16[64,256]{1,0:T(8,128)(2,1)S(1)}, u32[]{:S(2)}, u32[]{:S(2)}) collective-permute-start(bf16[64,256]{1,0:T(8,128)(2,1)S(1)} %get-tuple-element.36.own_ref), channel_id=1, source_target_pairs={{0,1},{1,2},{2,3},{3,4},{4,5},{5,6},{6,7},{7,8},{8,9},{9,10},{10,1... | collective-permute-start | bytes 98312 | tf_op jit(solution)/shard_map/ppermute | solution.py:270
  (7 other events, 16.8 us)

commit v5 on v4

--- a/solution.py
+++ b/solution.py
@@ -68,6 +68,28 @@
         out_ref[64 * head : 64 * (head + 1)] = jnp.concatenate([turned, turned], axis=1)
 
 
+def norm_window(tokens_ref, halo_ref, gain_ref):
+    own = tokens_ref[0].astype(F32)
+    halo = halo_ref[...].astype(F32)
+    features = own.shape[-1]
+    halo = halo.reshape(WIN // 2, WIN, features)
+    halo = jnp.stack([pltpu.roll(halo, 4, axis=1), halo], axis=1).reshape(WIN, WIN, features)
+    spot = lax.broadcasted_iota(jnp.int32, (WIN, WIN, features), 1)
+    window = jnp.where(spot < SHIFT, pltpu.roll(own, 4, axis=1), halo).reshape(WIN * WIN, features)
+    center = jnp.mean(window, axis=-1, keepdims=True)
+    spread = jnp.mean((window - center) ** 2, axis=-1, keepdims=True)
+    normed = (window - center) * lax.rsqrt(spread + 1e-05) * gain_ref[...]
+    return window, normed.astype(BF16)
+
+
+def own_kernel(tokens_ref, halo_ref, gain_ref, w_decode_ref, normed_ref, residual_ref):
+    window, normed_ref[...] = norm_window(tokens_ref, halo_ref, gain_ref)
+    residual = dot(window.astype(BF16), w_decode_ref[...], NT)
+    residual_ref[...] = jnp.concatenate(
+        [residual, jnp.zeros((WIN * WIN, 128 - CH), F32)], axis=1
+    )
+
+
 def norm_kernel(
     list_ref,
     count_ref,
@@ -75,12 +97,10 @@
     halo_ref,
     extra_ref,
     gain_ref,
-    w_decode_ref,
     value_ref,
     pert_ref,
     index_ref,
     normed_ref,
-    residual_ref,
     notes_ref,
 ):
     @pl.when(pl.program_id(0) == 0)
@@ -97,21 +117,7 @@
         for member in range(16):
             notes_ref[member] = jnp.concatenate([value_ref[...] + pert_ref[member], same], axis=0)
 
-    own = tokens_ref[0].astype(F32)
-    halo = halo_ref[...].astype(F32)
-    features = own.shape[-1]
-    halo = halo.reshape(WIN // 2, WIN, features)
-    halo = jnp.stack([pltpu.roll(halo, 4, axis=1), halo], axis=1).reshape(WIN, WIN, features)
-    spot = lax.broadcasted_iota(jnp.int32, (WIN, WIN, features), 1)
-    window = jnp.where(spot < SHIFT, pltpu.roll(own, 4, axis=1), halo).reshape(WIN * WIN, features)
-    center = jnp.mean(window, axis=-1, keepdims=True)
-    spread = jnp.mean((window - center) ** 2, axis=-1, keepdims=True)
-    normed = (window - center) * lax.rsqrt(spread + 1e-05) * gain_ref[...]
-    normed_ref[...] = normed.astype(BF16)
-    residual = dot(window.astype(BF16), w_decode_ref[...], NT)
-    residual_ref[...] = jnp.concatenate(
-        [residual, jnp.zeros((WIN * WIN, 128 - CH), F32)], axis=1
-    )
+    normed_ref[...] = norm_window(tokens_ref, halo_ref, gain_ref)[1]
 
 
 def attention_kernel(
@@ -362,12 +368,11 @@
     near, halo = lax.optimization_barrier((near, halo))
     held = [jnp.concatenate([block, near], axis=0)]
     held.append(lax.ppermute(held[0], ROW, second))
-    normed, residual, notes = pl.pallas_call(
+    normed, notes = pl.pallas_call(
         norm_kernel,
         grid=(4,),
         out_shape=(
             jax.ShapeDtypeStruct((256, features), BF16),
-            jax.ShapeDtypeStruct((256, 128), F32),
             jax.ShapeDtypeStruct((16, 8, 128), F32),
         ),
         in_specs=[
@@ -377,14 +382,12 @@
             pl.BlockSpec((WIN * SHIFT, features), lambda i: (i, 0)),
             pl.BlockSpec((16, features), lambda i: (8, 0)),
             pl.BlockSpec((1, features), lambda i: (0, 0)),
-            pl.BlockSpec(w_decode_t.shape, lambda i: (0, 0)),
             pl.BlockSpec((2, 128), lambda i: (0, 0)),
             pl.BlockSpec((16, 2, 128), lambda i: (0, 0, 0)),
             pl.BlockSpec((2, 128), lambda i: (0, 0)),
         ],
         out_specs=(
             pl.BlockSpec((64, features), lambda i: (i, 0)),
-            pl.BlockSpec((64, 128), lambda i: (i, 0)),
             pl.BlockSpec((16, 8, 128), lambda i: (0, 0, 0)),
         ),
         compiler_params=params(),
@@ -396,7 +399,6 @@
         halo,
         halo,
         norm_gain.reshape(1, -1),
-        w_decode_t,
         obs_value[0, 0],
         obs_pert[:, 0, 0],
         obs_index[0, 0],
@@ -417,8 +419,29 @@
     starts = block_starts(y, core)
     held[1], bias, starts, _ = lax.optimization_barrier((held[1], bias, starts, normed))
     held.append(lax.ppermute(held[1], ROW, first))
+    halo, _ = lax.optimization_barrier((halo, held[1]))
+    own, residual = pl.pallas_call(
+        own_kernel,
+        grid=(4,),
+        out_shape=(
+            jax.ShapeDtypeStruct((256, features), BF16),
+            jax.ShapeDtypeStruct((256, 128), F32),
+        ),
+        in_specs=[
+            pl.BlockSpec((1, WIN, WIN, features), lambda i: (0, i, 0, 0)),
+            pl.BlockSpec((WIN * SHIFT, features), lambda i: (i, 0)),
+            pl.BlockSpec((1, features), lambda i: (0, 0)),
+            pl.BlockSpec(w_decode_t.shape, lambda i: (0, 0)),
+        ],
+        out_specs=(
+            pl.BlockSpec((64, features), lambda i: (i, 0)),
+            pl.BlockSpec((64, 128), lambda i: (i, 0)),
+        ),
+        compiler_params=params(),
+        name="own",
+    )(tokens, halo, norm_gain.reshape(1, -1), w_decode_t)
     swapped = [core_swap(held[0]), core_swap(held[1])]
-    held[2], swapped[0] = lax.optimization_barrier((held[2], swapped[0]))
+    held[2], swapped[0], own, residual = lax.optimization_barrier((held[2], swapped[0], own, residual))
     held.append(lax.ppermute(held[2], ROW, second))
     swapped.append(core_swap(held[2]))
 
@@ -469,7 +492,7 @@
         ],
         compiler_params=params(48 * 1024 * 1024),
         name="attention",
-    )(group.reshape(1), starts, normed, mate, residual, blocks, bias, entries)
+    )(group.reshape(1), starts, own, mate, residual, blocks, bias, entries)
 
     previous, following, second = (shift(both, 1), shift(right, -1), shift(left, 2))
     selected = pl.pallas_call(

time: 110 us -> 110 us (level)
  starting transfers between devices: 51.2 us -> 54.4 us
  blocking collectives: 16.9 us -> 14 us
  waiting for transfers between devices: 19.1 us -> 17.4 us
  Pallas kernels: 14.2 us -> 15.9 us
    ppermute x4, starting transfers between devices: 10.5 us -> 13.9 us  [shift(): return lax.ppermute(x, SPACE, [(i, (i + by) % peers) for i in range(peers)])]
    all_to_all x1, blocking collectives: 16.9 us -> 14 us  [body(): lax.all_to_all(selected, MEMBER, split_axis=0, concat_axis=0, tiled=True)]
    ppermute x1, waiting for transfers between devices: 1.79 us -> 0.01 us  [body(): held.append(lax.ppermute(held[1], ROW, first))]
    pallas_call x0 -> x1, Pallas kernels: none -> 1.18 us  [body(): pl.pallas_call(own_kernel, grid=(4,), out_shape=(jax.ShapeDtypeStruct((25...]
  transfers between devices with their start and end apart: 15 -> 15, of which waited for: 6 -> 4; matrix products, arithmetic and copies ran while one was open for 0% -> 0% of each run, Pallas kernels for 2% -> 4%
where the time goes in v5:
time: 110 us; the launch traced here: 109 us
  starting transfers between devices  54.4 us (49%)
  waiting for transfers between devices  17.4 us (16%)
  Pallas kernels  15.9 us (14%)
  blocking collectives  14 us (13%)
  local copies, waits for them, and re-layouts  5.12 us (5%)
  between operations  1.83 us (2%)
    all_to_all x1, blocking collectives, body(): lax.all_to_all(selected, MEMBER, split_axis=0, concat_axis=0, tiled=True)  14 us
    ppermute x4, starting transfers between devices, shift(): return lax.ppermute(x, SPACE, [(i, (i + by) % peers) for i in range(peers)])  13.9 us
    all_to_all x1, starting transfers between devices, body(): lax.all_to_all(notes, MEMBER, split_axis=0, concat_axis=0, tiled=True)  12.5 us
    ppermute x4, starting transfers between devices, core_swap(): return lax.ppermute(x, 'core', [(0, 1), (1, 0)])  10 us
    pallas_call x1, Pallas kernels, body(): pl.pallas_call(attention_kernel, out_shape=(jax.ShapeDtypeStruct((64, 256...  7.54 us
    ppermute x1, waiting for transfers between devices, body(): near = lax.ppermute(block, ROW, first)  6.16 us
    ppermute x4, waiting for transfers between devices, shift(): return lax.ppermute(x, SPACE, [(i, (i + by) % peers) for i in range(peers)])  5.65 us
    unnamed x32, local copies, waits for them, and re-layouts  4.76 us
  transfers between devices with their start and end apart: 15, of which 4 were waited for; matrix products, arithmetic and copies ran while one was open for 0% of the time, Pallas kernels for 4%

profile of v5, /device:TPU:6, one launch (start us, length us, event | category | flops | bytes accessed | tf_op | source)
XLA Modules:
  0.0 108.9 jit_solution(8928940496445202857)
XLA Ops:
  0.0 1.9 %weights.1 = bf16[48,1280]{1,0:T(8,128)(2,1)} custom-call(s32[1]{0:T(128)} %bitcast.2.group_ref, bf16[48,2304]{1,0:T(8,128)(2,1)} %w_qkv_ref.1, bf16[24,1536]{1,0:T(8,128)(2,1)} %w_out_ref.1, bf16[69,1536]{1,0:T(8,128)(2,1)} %bitcast.30), custom_call_target="tpu_custom_call" | custom-call | tf_op jit(solution)/shard_map/weights/pallas_call | solution.py:343
  1.9 4.3 %collective-permute-start = (bf16[48,1280]{1,0:T(8,128)(2,1)}, bf16[48,1280]{1,0:T(8,128)(2,1)S(1)}, u32[]{:S(2)}, u32[]{:S(2)}) collective-permute-start(bf16[48,1280]{1,0:T(8,128)(2,1)} %weights.1), channel_id=1, source_target_pairs={{0,16},{16,0},{1,17},{17,1},{2,18},{18,2},{3,19},{19,3},{4,20},{20... | collective-permute-start | bytes 368648 | tf_op jit(solution)/shard_map/ppermute | solution.py:352
  8.2 4.3 %collective-permute-start.2 = (bf16[144,1536]{1,0:T(8,128)(2,1)S(1)}, bf16[144,1536]{1,0:T(8,128)(2,1)S(1)}, u32[]{:S(2)}, u32[]{:S(2)}) collective-permute-start(bf16[144,1536]{1,0:T(8,128)(2,1)S(1)} %edge.1), channel_id=1, source_target_pairs={{0,31},{1,0},{2,1},{3,2},{4,3},{5,4},{6,5},{7,6},{8,7},{9,8},{10,9... | collective-permute-start | bytes 1327112 | tf_op jit(solution)/shard_map/ppermute | solution.py:276
  12.5 2.1 %collective-permute-start.1 = (bf16[96,1280]{1,0:T(8,128)(2,1)S(1)}, bf16[96,1280]{1,0:T(8,128)(2,1)S(1)}, u32[]{:S(2)}, u32[]{:S(2)}) collective-permute-start(bf16[96,1280]{1,0:T(8,128)(2,1)S(1)} %maximum_select_fusion), channel_id=1, source_target_pairs={{0,2},{1,15},{2,0},{3,5},{4,6},{5,3},{6,4},{7,9},{8,10},{9,7},{10,... | collective-permute-start | bytes 737288 | tf_op jit(solution)/shard_map/ppermute | solution.py:357
  14.6 6.2 %collective-permute-done.1 = bf16[96,1280]{1,0:T(8,128)(2,1)S(1)} collective-permute-done((bf16[96,1280]{1,0:T(8,128)(2,1)S(1)}, bf16[96,1280]{1,0:T(8,128)(2,1)S(1)}, u32[]{:S(2)}, u32[]{:S(2)}) %collective-permute-start.1) | collective-permute-done | bytes 245792 | tf_op jit(solution)/shard_map/ppermute | solution.py:357
  20.8 3.8 %collective-permute-start.3 = (bf16[192,1280]{1,0:T(8,128)(2,1)S(1)}, bf16[192,1280]{1,0:T(8,128)(2,1)}, u32[]{:S(2)}, u32[]{:S(2)}) collective-permute-start(bf16[192,1280]{1,0:T(8,128)(2,1)S(1)} %pad_maximum_fusion.blocks_0_), channel_id=1, source_target_pairs={{0,14},{1,3},{2,4},{3,1},{4,2},{5,7},{6,8},{7,5},{8,6},{9,11},{10,... | collective-permute-start | bytes 1474568 | tf_op jit(solution)/shard_map/ppermute | solution.py:370
  26.5 1.9 %collective-permute-start.5 = (bf16[192,1280]{1,0:T(8,128)(2,1)S(1)}, bf16[192,1280]{1,0:T(8,128)(2,1)S(1)}, u32[]{:S(2)}, u32[]{:S(2)}) collective-permute-start(bf16[192,1280]{1,0:T(8,128)(2,1)S(1)} %pad_maximum_fusion.blocks_0_), channel_id=1, source_target_pairs={{0,1},{1,0},{2,3},{3,2},{4,5},{5,4},{6,7},{7,6},{8,9},{9,8},{10,11... | collective-permute-start | bytes 1474568 | tf_op jit(solution)/shard_map/ppermute | solution.py:297
  28.5 2.7 %norm.1 = (bf16[256,1536]{1,0:T(8,128)(2,1)}, f32[16,8,128]{2,1,0:T(8,128)}) custom-call(s32[4]{0:T(128)S(1)} %bitcast.36, s32[1]{0:T(128)} %bitcast.28.count_ref, bf16[1,32,8,1536]{3,2,1,0:T(8,128)(2,1)S(1)} %copy-done.1, bf16[144,1536]{1,0:T(8,128)(2,1)S(1)} %collective-permute-done.2.halo_ref.extra_ref, ...), custom_call_target="tpu_custom_call" | custom-call | tf_op jit(solution)/shard_map/norm/pallas_call | solution.py:371
  31.3 1.8 %collective-permute-done.3.blocks_1_ = bf16[192,1280]{1,0:T(8,128)(2,1)} collective-permute-done((bf16[192,1280]{1,0:T(8,128)(2,1)S(1)}, bf16[192,1280]{1,0:T(8,128)(2,1)}, u32[]{:S(2)}, u32[]{:S(2)}) %collective-permute-start.3) | collective-permute-done | bytes 491552 | tf_op jit(solution)/shard_map/ppermute | solution.py:370
  33.0 1.9 %collective-permute-start.4 = (bf16[192,1280]{1,0:T(8,128)(2,1)}, bf16[192,1280]{1,0:T(8,128)(2,1)}, u32[]{:S(2)}, u32[]{:S(2)}) collective-permute-start(bf16[192,1280]{1,0:T(8,128)(2,1)} %collective-permute-done.3.blocks_1_), channel_id=1, source_target_pairs={{0,2},{1,15},{2,0},{3,5},{4,6},{5,3},{6,4},{7,9},{8,10},{9,7},{10,... | collective-permute-start | bytes 1474568 | tf_op jit(solution)/shard_map/ppermute | solution.py:421
  34.9 2.7 %collective-permute-start.7 = (bf16[256,1536]{1,0:T(8,128)(2,1)}, bf16[256,1536]{1,0:T(8,128)(2,1)S(1)}, u32[]{:S(2)}, u32[]{:S(2)}) collective-permute-start(bf16[256,1536]{1,0:T(8,128)(2,1)} %get-tuple-element.29), channel_id=1, source_target_pairs={{0,32},{32,0},{64,96},{96,64},{1,33},{33,1},{65,97},{97,65},{2,34}... | collective-permute-start | bytes 2359304 | tf_op jit(solution)/shard_map/ppermute | solution.py:406
  37.7 3.8 %collective-permute-start.8 = (bf16[192,1280]{1,0:T(8,128)(2,1)}, bf16[192,1280]{1,0:T(8,128)(2,1)}, u32[]{:S(2)}, u32[]{:S(2)}) collective-permute-start(bf16[192,1280]{1,0:T(8,128)(2,1)} %collective-permute-done.3.blocks_1_), channel_id=1, source_target_pairs={{0,1},{1,0},{2,3},{3,2},{4,5},{5,4},{6,7},{7,6},{8,9},{9,8},{10,11... | collective-permute-start | bytes 1474568 | tf_op jit(solution)/shard_map/ppermute | solution.py:297
  41.5 1.2 %own.1 = (bf16[256,1536]{1,0:T(8,128)(2,1)S(1)}, f32[256,128]{1,0:T(8,128)S(1)}) custom-call(bf16[1,32,8,1536]{3,2,1,0:T(8,128)(2,1)S(1)} %copy-done.1, bf16[144,1536]{1,0:T(8,128)(2,1)S(1)} %collective-permute-done.2.halo_ref.extra_ref, f32[1,1536]{1,0:T(1,128)S(1)} %reshape.14.gain_ref, bf16[69,1536]{1,0:T(8,128)(2,1)S(1)} %bitcast.31), custom_call_target="tpu_custom_call" | custom-call | tf_op jit(solution)/shard_map/own/pallas_call | solution.py:423
  44.4 3.3 %collective-permute-start.6 = (bf16[192,1280]{1,0:T(8,128)(2,1)}, bf16[192,1280]{1,0:T(8,128)(2,1)}, u32[]{:S(2)}, u32[]{:S(2)}) collective-permute-start(bf16[192,1280]{1,0:T(8,128)(2,1)} %collective-permute-done.4.blocks_2_), channel_id=1, source_target_pairs={{0,14},{1,3},{2,4},{3,1},{4,2},{5,7},{6,8},{7,5},{8,6},{9,11},{10,... | collective-permute-start | bytes 1474568 | tf_op jit(solution)/shard_map/ppermute | solution.py:445
  47.7 12.5 %all-to-all-start = ((f32[16,8,128]{2,1,0:T(8,128)}), f32[16,8,128]{2,1,0:T(8,128)S(1)}, u32[]{:S(2)}, u32[]{:S(2)}) async-start(f32[16,8,128]{2,1,0:T(8,128)} %get-tuple-element.35), calls=%async_computation | async-start | bytes 131072 | tf_op jit(solution)/shard_map/all_to_all | solution.py:449
  60.2 1.9 %collective-permute-start.9 = (bf16[192,1280]{1,0:T(8,128)(2,1)}, bf16[192,1280]{1,0:T(8,128)(2,1)}, u32[]{:S(2)}, u32[]{:S(2)}) collective-permute-start(bf16[192,1280]{1,0:T(8,128)(2,1)} %collective-permute-done.4.blocks_2_), channel_id=1, source_target_pairs={{0,1},{1,0},{2,3},{3,2},{4,5},{5,4},{6,7},{7,6},{8,9},{9,8},{10,11... | collective-permute-start | bytes 1474568 | tf_op jit(solution)/shard_map/ppermute | solution.py:297
  62.2 2.4 %collective-permute-start.10 = (bf16[192,1280]{1,0:T(8,128)(2,1)}, bf16[192,1280]{1,0:T(8,128)(2,1)}, u32[]{:S(2)}, u32[]{:S(2)}) collective-permute-start(bf16[192,1280]{1,0:T(8,128)(2,1)} %collective-permute-done.6.blocks_3_), channel_id=1, source_target_pairs={{0,1},{1,0},{2,3},{3,2},{4,5},{5,4},{6,7},{7,6},{8,9},{9,8},{10,11... | collective-permute-start | bytes 1474568 | tf_op jit(solution)/shard_map/ppermute | solution.py:297
  64.6 3.8 %all-to-all-done.observed_ref = f32[16,8,128]{2,1,0:T(8,128)S(1)} async-done(((f32[16,8,128]{2,1,0:T(8,128)}), f32[16,8,128]{2,1,0:T(8,128)S(1)}, u32[]{:S(2)}, u32[]{:S(2)}) %all-to-all-start) | async-done | bytes 65568 | tf_op jit(solution)/shard_map/all_to_all | solution.py:449
  69.9 7.5 %attention.1 = (bf16[64,256]{1,0:T(8,128)(2,1)S(1)}, bf16[32,256]{1,0:T(8,128)(2,1)S(1)}, bf16[32,256]{1,0:T(8,128)(2,1)S(1)}) custom-call(s32[1]{0:T(128)} %bitcast.2.group_ref, s32[16]{0:T(128)S(1)} %stack.67.starts_ref, bf16[256,1536]{1,0:T(8,128)(2,1)S(1)} %copy-done.5, bf16[256,1536]{1,0:T(8,128)(2,1)S(1)} %collective-permute-done.7.mate_ref, ...), custom_call_target="tpu_custom_call" | custom-call | tf_op jit(solution)/shard_map/attention/pallas_call | solution.py:469
  77.4 1.9 %collective-permute-start.11 = (bf16[64,256]{1,0:T(8,128)(2,1)S(1)}, bf16[64,256]{1,0:T(8,128)(2,1)S(1)}, u32[]{:S(2)}, u32[]{:S(2)}) collective-permute-start(bf16[64,256]{1,0:T(8,128)(2,1)S(1)} %get-tuple-element.44.own_ref), channel_id=1, source_target_pairs={{0,1},{1,2},{2,3},{3,4},{4,5},{5,6},{6,7},{7,8},{8,9},{9,10},{10,1... | collective-permute-start | bytes 98312 | tf_op jit(solution)/shard_map/ppermute | solution.py:276
  79.4 5.8 %collective-permute-start.12 = (bf16[32,256]{1,0:T(8,128)(2,1)S(1)}, bf16[32,256]{1,0:T(8,128)(2,1)S(1)}, u32[]{:S(2)}, u32[]{:S(2)}) collective-permute-start(bf16[32,256]{1,0:T(8,128)(2,1)S(1)} %get-tuple-element.45), channel_id=1, source_target_pairs={{0,31},{1,0},{2,1},{3,2},{4,3},{5,4},{6,5},{7,6},{8,7},{9,8},{10,9... | collective-permute-start | bytes 49160 | tf_op jit(solution)/shard_map/ppermute | solution.py:276
  85.1 1.9 %collective-permute-start.13 = (bf16[32,256]{1,0:T(8,128)(2,1)S(1)}, bf16[32,256]{1,0:T(8,128)(2,1)S(1)}, u32[]{:S(2)}, u32[]{:S(2)}) collective-permute-start(bf16[32,256]{1,0:T(8,128)(2,1)S(1)} %get-tuple-element.46), channel_id=1, source_target_pairs={{0,2},{1,3},{2,4},{3,5},{4,6},{5,7},{6,8},{7,9},{8,10},{9,11},{10,... | collective-permute-start | bytes 49160 | tf_op jit(solution)/shard_map/ppermute | solution.py:276
  87.2 5.6 %collective-permute-done.13.second_ref = bf16[32,256]{1,0:T(8,128)(2,1)S(1)} collective-permute-done((bf16[32,256]{1,0:T(8,128)(2,1)S(1)}, bf16[32,256]{1,0:T(8,128)(2,1)S(1)}, u32[]{:S(2)}, u32[]{:S(2)}) %collective-permute-start.13) | collective-permute-done | bytes 16416 | tf_op jit(solution)/shard_map/ppermute | solution.py:276
  93.6 14.0 %all_to_all.10.arrived_ref = bf16[16,8,128]{2,1,0:T(8,128)(2,1)S(1)} all-to-all(bf16[16,8,128]{2,1,0:T(8,128)(2,1)S(1)} %select.75), channel_id=1, replica_groups=mesh['zhi'=4,'x'=4,'zlo'=2,'y'=8,'core'=2] {'zhi','x'}, dimensions={0} | all-to-all | bytes 65536 | tf_op jit(solution)/shard_map/all_to_all | solution.py:507
  (56 shorter events, 7.8 us)
Async XLA Ops:
  1.9 10.5 %collective-permute-start = (bf16[48,1280]{1,0:T(8,128)(2,1)}, bf16[48,1280]{1,0:T(8,128)(2,1)S(1)}, u32[]{:S(2)}, u32[]{:S(2)}) collective-permute-start(bf16[48,1280]{1,0:T(8,128)(2,1)} %weights.1), channel_id=1, source_target_pairs={{0,16},{16,0},{1,17},{17,1},{2,18},{18,2},{3,19},{19,3},{4,20},{20... | collective-permute-start | bytes 368648 | tf_op jit(solution)/shard_map/ppermute | solution.py:352
  8.2 12.6 %collective-permute-start.2 = (bf16[144,1536]{1,0:T(8,128)(2,1)S(1)}, bf16[144,1536]{1,0:T(8,128)(2,1)S(1)}, u32[]{:S(2)}, u32[]{:S(2)}) collective-permute-start(bf16[144,1536]{1,0:T(8,128)(2,1)S(1)} %edge.1), channel_id=1, source_target_pairs={{0,31},{1,0},{2,1},{3,2},{4,3},{5,4},{6,5},{7,6},{8,7},{9,8},{10,9... | collective-permute-start | bytes 1327112 | tf_op jit(solution)/shard_map/ppermute | solution.py:276
  12.4 13.4 %copy-start.15 = (f32[1536]{0:T(1024)S(1)}, f32[1536]{0:T(1024)}, u32[]{:S(2)}) copy-start(f32[1536]{0:T(1024)} %param.13) | copy-start | bytes 18436
  12.4 13.4 %copy-start.6 = (f32[24,64,64]{2,1,0:T(8,128)S(1)}, f32[24,64,64]{2,1,0:T(8,128)}, u32[]{:S(2)}) copy-start(f32[24,64,64]{2,1,0:T(8,128)} %rel_bias_ref.1) | copy-start | bytes 1179652
  12.5 8.2 %collective-permute-start.1 = (bf16[96,1280]{1,0:T(8,128)(2,1)S(1)}, bf16[96,1280]{1,0:T(8,128)(2,1)S(1)}, u32[]{:S(2)}, u32[]{:S(2)}) collective-permute-start(bf16[96,1280]{1,0:T(8,128)(2,1)S(1)} %maximum_select_fusion), channel_id=1, source_target_pairs={{0,2},{1,15},{2,0},{3,5},{4,6},{5,3},{6,4},{7,9},{8,10},{9,7},{10,... | collective-permute-start | bytes 737288 | tf_op jit(solution)/shard_map/ppermute | solution.py:357
  20.8 7.7 %copy-start.1 = (bf16[1,32,8,1536]{3,2,1,0:T(8,128)(2,1)S(1)}, bf16[1,32,8,1536]{3,2,1,0:T(8,128)(2,1)}, u32[]{:S(2)}) copy-start(bf16[1,32,8,1536]{3,2,1,0:T(8,128)(2,1)} %tokens_ref.5) | copy-start | bytes 2359300
  20.8 7.7 %copy-start.9 = (f32[16,1,1,2,128]{4,3,2,1,0:T(2,128)S(1)}, f32[16,1,1,2,128]{4,3,2,1,0:T(2,128)}, u32[]{:S(2)}) copy-start(f32[16,1,1,2,128]{4,3,2,1,0:T(2,128)} %param.19) | copy-start | bytes 49156
  20.8 7.7 %copy-start.11 = (s32[1,1,2,128]{3,2,1,0:T(2,128)S(1)}, s32[1,1,2,128]{3,2,1,0:T(2,128)}, u32[]{:S(2)}) copy-start(s32[1,1,2,128]{3,2,1,0:T(2,128)} %param.20) | copy-start | bytes 3076
  20.8 7.7 %copy-start.12 = (f32[1,1,2,128]{3,2,1,0:T(2,128)S(1)}, f32[1,1,2,128]{3,2,1,0:T(2,128)}, u32[]{:S(2)}) copy-start(f32[1,1,2,128]{3,2,1,0:T(2,128)} %param.18) | copy-start | bytes 3076
  20.8 7.7 %copy-start.13 = (s32[1,1,4]{2,1,0:T(1,128)S(1)}, s32[1,1,4]{2,1,0:T(1,128)}, u32[]{:S(2)}) copy-start(s32[1,1,4]{2,1,0:T(1,128)} %param.21) | copy-start | bytes 52
  20.8 12.2 %collective-permute-start.3 = (bf16[192,1280]{1,0:T(8,128)(2,1)S(1)}, bf16[192,1280]{1,0:T(8,128)(2,1)}, u32[]{:S(2)}, u32[]{:S(2)}) collective-permute-start(bf16[192,1280]{1,0:T(8,128)(2,1)S(1)} %pad_maximum_fusion.blocks_0_), channel_id=1, source_target_pairs={{0,14},{1,3},{2,4},{3,1},{4,2},{5,7},{6,8},{7,5},{8,6},{9,11},{10,... | collective-permute-start | bytes 1474568 | tf_op jit(solution)/shard_map/ppermute | solution.py:370
  26.2 15.2 %copy-start.3 = (bf16[1536,69]{0,1:T(8,128)(2,1)S(1)}, bf16[1536,69]{0,1:T(8,128)(2,1)}, u32[]{:S(2)}) copy-start(bf16[1536,69]{0,1:T(8,128)(2,1)} %param.17) | copy-start | bytes 635908
  26.5 17.1 %collective-permute-start.5 = (bf16[192,1280]{1,0:T(8,128)(2,1)S(1)}, bf16[192,1280]{1,0:T(8,128)(2,1)S(1)}, u32[]{:S(2)}, u32[]{:S(2)}) collective-permute-start(bf16[192,1280]{1,0:T(8,128)(2,1)S(1)} %pad_maximum_fusion.blocks_0_), channel_id=1, source_target_pairs={{0,1},{1,0},{2,3},{3,2},{4,5},{5,4},{6,7},{7,6},{8,9},{9,8},{10,11... | collective-permute-start | bytes 1474568 | tf_op jit(solution)/shard_map/ppermute | solution.py:297
  33.0 11.4 %collective-permute-start.4 = (bf16[192,1280]{1,0:T(8,128)(2,1)}, bf16[192,1280]{1,0:T(8,128)(2,1)}, u32[]{:S(2)}, u32[]{:S(2)}) collective-permute-start(bf16[192,1280]{1,0:T(8,128)(2,1)} %collective-permute-done.3.blocks_1_), channel_id=1, source_target_pairs={{0,2},{1,15},{2,0},{3,5},{4,6},{5,3},{6,4},{7,9},{8,10},{9,7},{10,... | collective-permute-start | bytes 1474568 | tf_op jit(solution)/shard_map/ppermute | solution.py:421
  34.9 27.2 %collective-permute-start.7 = (bf16[256,1536]{1,0:T(8,128)(2,1)}, bf16[256,1536]{1,0:T(8,128)(2,1)S(1)}, u32[]{:S(2)}, u32[]{:S(2)}) collective-permute-start(bf16[256,1536]{1,0:T(8,128)(2,1)} %get-tuple-element.29), channel_id=1, source_target_pairs={{0,32},{32,0},{64,96},{96,64},{1,33},{33,1},{65,97},{97,65},{2,34}... | collective-permute-start | bytes 2359304 | tf_op jit(solution)/shard_map/ppermute | solution.py:406
  37.7 24.5 %collective-permute-start.8 = (bf16[192,1280]{1,0:T(8,128)(2,1)}, bf16[192,1280]{1,0:T(8,128)(2,1)}, u32[]{:S(2)}, u32[]{:S(2)}) collective-permute-start(bf16[192,1280]{1,0:T(8,128)(2,1)} %collective-permute-done.3.blocks_1_), channel_id=1, source_target_pairs={{0,1},{1,0},{2,3},{3,2},{4,5},{5,4},{6,7},{7,6},{8,9},{9,8},{10,11... | collective-permute-start | bytes 1474568 | tf_op jit(solution)/shard_map/ppermute | solution.py:297
  44.4 17.8 %collective-permute-start.6 = (bf16[192,1280]{1,0:T(8,128)(2,1)}, bf16[192,1280]{1,0:T(8,128)(2,1)}, u32[]{:S(2)}, u32[]{:S(2)}) collective-permute-start(bf16[192,1280]{1,0:T(8,128)(2,1)} %collective-permute-done.4.blocks_2_), channel_id=1, source_target_pairs={{0,14},{1,3},{2,4},{3,1},{4,2},{5,7},{6,8},{7,5},{8,6},{9,11},{10,... | collective-permute-start | bytes 1474568 | tf_op jit(solution)/shard_map/ppermute | solution.py:445
  47.7 20.7 %all-to-all-start = ((f32[16,8,128]{2,1,0:T(8,128)}), f32[16,8,128]{2,1,0:T(8,128)S(1)}, u32[]{:S(2)}, u32[]{:S(2)}) async-start(f32[16,8,128]{2,1,0:T(8,128)} %get-tuple-element.35), calls=%async_computation | async-start | bytes 131072 | tf_op jit(solution)/shard_map/all_to_all | solution.py:449
  60.2 8.5 %collective-permute-start.9 = (bf16[192,1280]{1,0:T(8,128)(2,1)}, bf16[192,1280]{1,0:T(8,128)(2,1)}, u32[]{:S(2)}, u32[]{:S(2)}) collective-permute-start(bf16[192,1280]{1,0:T(8,128)(2,1)} %collective-permute-done.4.blocks_2_), channel_id=1, source_target_pairs={{0,1},{1,0},{2,3},{3,2},{4,5},{5,4},{6,7},{7,6},{8,9},{9,8},{10,11... | collective-permute-start | bytes 1474568 | tf_op jit(solution)/shard_map/ppermute | solution.py:297
  62.2 6.5 %collective-permute-start.10 = (bf16[192,1280]{1,0:T(8,128)(2,1)}, bf16[192,1280]{1,0:T(8,128)(2,1)}, u32[]{:S(2)}, u32[]{:S(2)}) collective-permute-start(bf16[192,1280]{1,0:T(8,128)(2,1)} %collective-permute-done.6.blocks_3_), channel_id=1, source_target_pairs={{0,1},{1,0},{2,3},{3,2},{4,5},{5,4},{6,7},{7,6},{8,9},{9,8},{10,11... | collective-permute-start | bytes 1474568 | tf_op jit(solution)/shard_map/ppermute | solution.py:297
  68.7 39.0 %copy-start.2 = (bf16[1,1,4,128,1104]{3,4,2,1,0:T(8,128)(2,1)S(1)}, bf16[1,1,4,128,1104]{3,4,2,1,0:T(8,128)(2,1)}, u32[]{:S(2)}) copy-start(bf16[1,1,4,128,1104]{3,4,2,1,0:T(8,128)(2,1)} %param.23) | copy-start | bytes 3391492
  77.4 15.4 %collective-permute-start.11 = (bf16[64,256]{1,0:T(8,128)(2,1)S(1)}, bf16[64,256]{1,0:T(8,128)(2,1)S(1)}, u32[]{:S(2)}, u32[]{:S(2)}) collective-permute-start(bf16[64,256]{1,0:T(8,128)(2,1)S(1)} %get-tuple-element.44.own_ref), channel_id=1, source_target_pairs={{0,1},{1,2},{2,3},{3,4},{4,5},{5,6},{6,7},{7,8},{8,9},{9,10},{10,1... | collective-permute-start | bytes 98312 | tf_op jit(solution)/shard_map/ppermute | solution.py:276
  79.4 7.9 %collective-permute-start.12 = (bf16[32,256]{1,0:T(8,128)(2,1)S(1)}, bf16[32,256]{1,0:T(8,128)(2,1)S(1)}, u32[]{:S(2)}, u32[]{:S(2)}) collective-permute-start(bf16[32,256]{1,0:T(8,128)(2,1)S(1)} %get-tuple-element.45), channel_id=1, source_target_pairs={{0,31},{1,0},{2,1},{3,2},{4,3},{5,4},{6,5},{7,6},{8,7},{9,8},{10,9... | collective-permute-start | bytes 49160 | tf_op jit(solution)/shard_map/ppermute | solution.py:276
  85.1 7.7 %collective-permute-start.13 = (bf16[32,256]{1,0:T(8,128)(2,1)S(1)}, bf16[32,256]{1,0:T(8,128)(2,1)S(1)}, u32[]{:S(2)}, u32[]{:S(2)}) collective-permute-start(bf16[32,256]{1,0:T(8,128)(2,1)S(1)} %get-tuple-element.46), channel_id=1, source_target_pairs={{0,2},{1,3},{2,4},{3,5},{4,6},{5,7},{6,8},{7,9},{8,10},{9,11},{10,... | collective-permute-start | bytes 49160 | tf_op jit(solution)/shard_map/ppermute | solution.py:276
  (7 other events, 10.4 us)

commit v6 on v4

--- a/solution.py
+++ b/solution.py
@@ -234,16 +234,17 @@
 
 
 def select_kernel(chosen_ref, own_ref, prev_ref, next_ref, second_ref, out_ref, table, picked):
-    for place, part in enumerate(
-        (prev_ref[:32], own_ref[:32], next_ref[...], second_ref[...], prev_ref[32:], own_ref[32:])
-    ):
-        table[32 * place : 32 * (place + 1)] = part.astype(F32)
-    table[192:200] = jnp.zeros((8, 256), F32)
-    table[288:296] = jnp.zeros((8, 256), F32)
+    parts = (
+        (prev_ref[:32], second_ref[...]),
+        (own_ref[:32], prev_ref[32:]),
+        (next_ref[...], own_ref[32:]),
+    )
+    for place, (late, early) in enumerate(parts):
+        table[32 * place : 32 * (place + 1)] = late.astype(F32) + early.astype(F32)
+    table[96:104] = jnp.zeros((8, 256), F32)
     for band in range(16):
         for j in range(MAXL):
-            row = chosen_ref[MAXL * band + j]
-            found = table[pl.ds(row, 1)] + table[pl.ds(row + 96, 1)]
+            found = table[pl.ds(chosen_ref[MAXL * band + j], 1)]
             for member in range(2):
                 to = MAXL * member + j
                 picked[band, to : to + 1] = found[:, 128 * member : 128 * (member + 1)]
@@ -441,7 +442,7 @@
     listed, count = (meta[:, :MAXL], meta[:, MAXL : MAXL + 1])
     band = jnp.arange(16)[:, None] + listed // 6 - 1
     live = (jnp.arange(MAXL)[None] < count) & (band >= 0) & (band < 16)
-    chosen = jnp.where(live, (listed // 2 % 3) * 32 + band * 2 + listed % 2, 192).reshape(16 * MAXL)
+    chosen = jnp.where(live, (listed // 2 % 3) * 32 + band * 2 + listed % 2, 96).reshape(16 * MAXL)
 
     both, right, left = pl.pallas_call(
         attention_kernel,
@@ -477,7 +478,7 @@
         out_shape=jax.ShapeDtypeStruct((16, 8, 128), BF16),
         in_specs=[smem()] + [vmem()] * 4,
         out_specs=vmem(),
-        scratch_shapes=[pltpu.VMEM((296, 256), F32), pltpu.VMEM((16, 8, 128), F32)],
+        scratch_shapes=[pltpu.VMEM((104, 256), F32), pltpu.VMEM((16, 8, 128), F32)],
         compiler_params=params(),
         name="select",
     )(chosen, both, previous, following, second)

time: 110 us -> 110 us (level)
  no operation moved by 1% of the time
where the time goes in v6:
time: 110 us; the launch traced here: 108 us
  starting transfers between devices  51.2 us (47%)
  waiting for transfers between devices  19.1 us (17%)
  blocking collectives  16.9 us (15%)
  Pallas kernels  14.1 us (13%)
  local copies, waits for them, and re-layouts  5.1 us (5%)
  between operations  1.73 us (2%)
    all_to_all x1, blocking collectives, body(): lax.all_to_all(selected, MEMBER, split_axis=0, concat_axis=0, tiled=True)  16.9 us
    all_to_all x1, starting transfers between devices, body(): lax.all_to_all(notes, MEMBER, split_axis=0, concat_axis=0, tiled=True)  12.4 us
    ppermute x4, starting transfers between devices, shift(): return lax.ppermute(x, SPACE, [(i, (i + by) % peers) for i in range(peers)])  10.5 us
    ppermute x4, starting transfers between devices, core_swap(): return lax.ppermute(x, 'core', [(0, 1), (1, 0)])  10 us
    pallas_call x1, Pallas kernels, body(): pl.pallas_call(attention_kernel, out_shape=(jax.ShapeDtypeStruct((64, 256...  7.63 us
    ppermute x1, waiting for transfers between devices, body(): near = lax.ppermute(block, ROW, first)  6.16 us
    ppermute x4, waiting for transfers between devices, shift(): return lax.ppermute(x, SPACE, [(i, (i + by) % peers) for i in range(peers)])  4.86 us
    unnamed x32, local copies, waits for them, and re-layouts  4.73 us
  transfers between devices with their start and end apart: 15, of which 6 were waited for; matrix products, arithmetic and copies ran while one was open for 0% of the time, Pallas kernels for 2%

profile of v6, /device:TPU:6, one launch (start us, length us, event | category | flops | bytes accessed | tf_op | source)
XLA Modules:
  0.0 108.3 jit_solution(3163650108213179102)
XLA Ops:
  0.0 1.9 %weights.1 = bf16[48,1280]{1,0:T(8,128)(2,1)} custom-call(s32[1]{0:T(128)} %bitcast.2.group_ref, bf16[48,2304]{1,0:T(8,128)(2,1)} %w_qkv_ref.1, bf16[24,1536]{1,0:T(8,128)(2,1)} %w_out_ref.1, bf16[69,1536]{1,0:T(8,128)(2,1)} %bitcast.30), custom_call_target="tpu_custom_call" | custom-call | tf_op jit(solution)/shard_map/weights/pallas_call | solution.py:338
  1.9 4.3 %collective-permute-start = (bf16[48,1280]{1,0:T(8,128)(2,1)}, bf16[48,1280]{1,0:T(8,128)(2,1)S(1)}, u32[]{:S(2)}, u32[]{:S(2)}) collective-permute-start(bf16[48,1280]{1,0:T(8,128)(2,1)} %weights.1), channel_id=1, source_target_pairs={{0,16},{16,0},{1,17},{17,1},{2,18},{18,2},{3,19},{19,3},{4,20},{20... | collective-permute-start | bytes 368648 | tf_op jit(solution)/shard_map/ppermute | solution.py:347
  8.2 4.3 %collective-permute-start.2 = (bf16[144,1536]{1,0:T(8,128)(2,1)S(1)}, bf16[144,1536]{1,0:T(8,128)(2,1)S(1)}, u32[]{:S(2)}, u32[]{:S(2)}) collective-permute-start(bf16[144,1536]{1,0:T(8,128)(2,1)S(1)} %edge.1), channel_id=1, source_target_pairs={{0,31},{1,0},{2,1},{3,2},{4,3},{5,4},{6,5},{7,6},{8,7},{9,8},{10,9... | collective-permute-start | bytes 1327112 | tf_op jit(solution)/shard_map/ppermute | solution.py:271
  12.5 2.1 %collective-permute-start.1 = (bf16[96,1280]{1,0:T(8,128)(2,1)S(1)}, bf16[96,1280]{1,0:T(8,128)(2,1)S(1)}, u32[]{:S(2)}, u32[]{:S(2)}) collective-permute-start(bf16[96,1280]{1,0:T(8,128)(2,1)S(1)} %maximum_select_fusion), channel_id=1, source_target_pairs={{0,2},{1,15},{2,0},{3,5},{4,6},{5,3},{6,4},{7,9},{8,10},{9,7},{10,... | collective-permute-start | bytes 737288 | tf_op jit(solution)/shard_map/ppermute | solution.py:352
  14.6 6.2 %collective-permute-done.1 = bf16[96,1280]{1,0:T(8,128)(2,1)S(1)} collective-permute-done((bf16[96,1280]{1,0:T(8,128)(2,1)S(1)}, bf16[96,1280]{1,0:T(8,128)(2,1)S(1)}, u32[]{:S(2)}, u32[]{:S(2)}) %collective-permute-start.1) | collective-permute-done | bytes 245792 | tf_op jit(solution)/shard_map/ppermute | solution.py:352
  20.9 3.8 %collective-permute-start.3 = (bf16[192,1280]{1,0:T(8,128)(2,1)S(1)}, bf16[192,1280]{1,0:T(8,128)(2,1)}, u32[]{:S(2)}, u32[]{:S(2)}) collective-permute-start(bf16[192,1280]{1,0:T(8,128)(2,1)S(1)} %pad_maximum_fusion.blocks_0_), channel_id=1, source_target_pairs={{0,14},{1,3},{2,4},{3,1},{4,2},{5,7},{6,8},{7,5},{8,6},{9,11},{10,... | collective-permute-start | bytes 1474568 | tf_op jit(solution)/shard_map/ppermute | solution.py:365
  26.5 1.9 %collective-permute-start.5 = (bf16[192,1280]{1,0:T(8,128)(2,1)S(1)}, bf16[192,1280]{1,0:T(8,128)(2,1)S(1)}, u32[]{:S(2)}, u32[]{:S(2)}) collective-permute-start(bf16[192,1280]{1,0:T(8,128)(2,1)S(1)} %pad_maximum_fusion.blocks_0_), channel_id=1, source_target_pairs={{0,1},{1,0},{2,3},{3,2},{4,5},{5,4},{6,7},{7,6},{8,9},{9,8},{10,11... | collective-permute-start | bytes 1474568 | tf_op jit(solution)/shard_map/ppermute | solution.py:292
  28.4 2.2 %norm.1 = (bf16[256,1536]{1,0:T(8,128)(2,1)S(1)}, f32[256,128]{1,0:T(8,128)S(1)}, f32[16,8,128]{2,1,0:T(8,128)}) custom-call(s32[4]{0:T(128)S(1)} %bitcast.36, s32[1]{0:T(128)} %bitcast.28.count_ref, bf16[1,32,8,1536]{3,2,1,0:T(8,128)(2,1)S(1)} %copy-done.1, bf16[144,1536]{1,0:T(8,128)(2,1)S(1)} %collective-permute-done.2.halo_ref.extra_ref, ...), custom_call_target="tpu_custom_call" | custom-call | tf_op jit(solution)/shard_map/norm/pallas_call | solution.py:366
  30.6 2.4 %collective-permute-done.3.blocks_1_ = bf16[192,1280]{1,0:T(8,128)(2,1)} collective-permute-done((bf16[192,1280]{1,0:T(8,128)(2,1)S(1)}, bf16[192,1280]{1,0:T(8,128)(2,1)}, u32[]{:S(2)}, u32[]{:S(2)}) %collective-permute-start.3) | collective-permute-done | bytes 491552 | tf_op jit(solution)/shard_map/ppermute | solution.py:365
  33.0 1.9 %collective-permute-start.4 = (bf16[192,1280]{1,0:T(8,128)(2,1)}, bf16[192,1280]{1,0:T(8,128)(2,1)}, u32[]{:S(2)}, u32[]{:S(2)}) collective-permute-start(bf16[192,1280]{1,0:T(8,128)(2,1)} %collective-permute-done.3.blocks_1_), channel_id=1, source_target_pairs={{0,2},{1,15},{2,0},{3,5},{4,6},{5,3},{6,4},{7,9},{8,10},{9,7},{10,... | collective-permute-start | bytes 1474568 | tf_op jit(solution)/shard_map/ppermute | solution.py:420
  35.0 2.7 %collective-permute-start.7 = (bf16[256,1536]{1,0:T(8,128)(2,1)S(1)}, bf16[256,1536]{1,0:T(8,128)(2,1)S(1)}, u32[]{:S(2)}, u32[]{:S(2)}) collective-permute-start(bf16[256,1536]{1,0:T(8,128)(2,1)S(1)} %get-tuple-element.25.own_ref), channel_id=1, source_target_pairs={{0,32},{32,0},{64,96},{96,64},{1,33},{33,1},{65,97},{97,65},{2,34}... | collective-permute-start | bytes 2359304 | tf_op jit(solution)/shard_map/ppermute | solution.py:405
  37.7 3.8 %collective-permute-start.8 = (bf16[192,1280]{1,0:T(8,128)(2,1)}, bf16[192,1280]{1,0:T(8,128)(2,1)}, u32[]{:S(2)}, u32[]{:S(2)}) collective-permute-start(bf16[192,1280]{1,0:T(8,128)(2,1)} %collective-permute-done.3.blocks_1_), channel_id=1, source_target_pairs={{0,1},{1,0},{2,3},{3,2},{4,5},{5,4},{6,7},{7,6},{8,9},{9,8},{10,11... | collective-permute-start | bytes 1474568 | tf_op jit(solution)/shard_map/ppermute | solution.py:292
  42.3 1.8 %collective-permute-done.4.blocks_2_ = bf16[192,1280]{1,0:T(8,128)(2,1)} collective-permute-done((bf16[192,1280]{1,0:T(8,128)(2,1)}, bf16[192,1280]{1,0:T(8,128)(2,1)}, u32[]{:S(2)}, u32[]{:S(2)}) %collective-permute-start.4) | collective-permute-done | bytes 491552 | tf_op jit(solution)/shard_map/ppermute | solution.py:420
  44.1 3.6 %collective-permute-start.6 = (bf16[192,1280]{1,0:T(8,128)(2,1)}, bf16[192,1280]{1,0:T(8,128)(2,1)}, u32[]{:S(2)}, u32[]{:S(2)}) collective-permute-start(bf16[192,1280]{1,0:T(8,128)(2,1)} %collective-permute-done.4.blocks_2_), channel_id=1, source_target_pairs={{0,14},{1,3},{2,4},{3,1},{4,2},{5,7},{6,8},{7,5},{8,6},{9,11},{10,... | collective-permute-start | bytes 1474568 | tf_op jit(solution)/shard_map/ppermute | solution.py:423
  47.7 12.4 %all-to-all-start = ((f32[16,8,128]{2,1,0:T(8,128)}), f32[16,8,128]{2,1,0:T(8,128)S(1)}, u32[]{:S(2)}, u32[]{:S(2)}) async-start(f32[16,8,128]{2,1,0:T(8,128)} %get-tuple-element.28), calls=%async_computation | async-start | bytes 131072 | tf_op jit(solution)/shard_map/all_to_all | solution.py:427
  60.1 1.9 %collective-permute-start.9 = (bf16[192,1280]{1,0:T(8,128)(2,1)}, bf16[192,1280]{1,0:T(8,128)(2,1)}, u32[]{:S(2)}, u32[]{:S(2)}) collective-permute-start(bf16[192,1280]{1,0:T(8,128)(2,1)} %collective-permute-done.4.blocks_2_), channel_id=1, source_target_pairs={{0,1},{1,0},{2,3},{3,2},{4,5},{5,4},{6,7},{7,6},{8,9},{9,8},{10,11... | collective-permute-start | bytes 1474568 | tf_op jit(solution)/shard_map/ppermute | solution.py:292
  62.0 2.4 %collective-permute-start.10 = (bf16[192,1280]{1,0:T(8,128)(2,1)}, bf16[192,1280]{1,0:T(8,128)(2,1)}, u32[]{:S(2)}, u32[]{:S(2)}) collective-permute-start(bf16[192,1280]{1,0:T(8,128)(2,1)} %collective-permute-done.6.blocks_3_), channel_id=1, source_target_pairs={{0,1},{1,0},{2,3},{3,2},{4,5},{5,4},{6,7},{7,6},{8,9},{9,8},{10,11... | collective-permute-start | bytes 1474568 | tf_op jit(solution)/shard_map/ppermute | solution.py:292
  64.4 3.8 %all-to-all-done.observed_ref = f32[16,8,128]{2,1,0:T(8,128)S(1)} async-done(((f32[16,8,128]{2,1,0:T(8,128)}), f32[16,8,128]{2,1,0:T(8,128)S(1)}, u32[]{:S(2)}, u32[]{:S(2)}) %all-to-all-start) | async-done | bytes 65568 | tf_op jit(solution)/shard_map/all_to_all | solution.py:427
  70.6 7.6 %attention.1 = (bf16[64,256]{1,0:T(8,128)(2,1)S(1)}, bf16[32,256]{1,0:T(8,128)(2,1)S(1)}, bf16[32,256]{1,0:T(8,128)(2,1)S(1)}) custom-call(s32[1]{0:T(128)} %bitcast.2.group_ref, s32[16]{0:T(128)S(1)} %stack.67.starts_ref, bf16[256,1536]{1,0:T(8,128)(2,1)S(1)} %copy-done.5, bf16[256,1536]{1,0:T(8,128)(2,1)S(1)} %collective-permute-done.7.mate_ref, ...), custom_call_target="tpu_custom_call" | custom-call | tf_op jit(solution)/shard_map/attention/pallas_call | solution.py:447
  78.3 1.9 %collective-permute-start.12 = (bf16[32,256]{1,0:T(8,128)(2,1)S(1)}, bf16[32,256]{1,0:T(8,128)(2,1)S(1)}, u32[]{:S(2)}, u32[]{:S(2)}) collective-permute-start(bf16[32,256]{1,0:T(8,128)(2,1)S(1)} %get-tuple-element.37), channel_id=1, source_target_pairs={{0,31},{1,0},{2,1},{3,2},{4,3},{5,4},{6,5},{7,6},{8,7},{9,8},{10,9... | collective-permute-start | bytes 49160 | tf_op jit(solution)/shard_map/ppermute | solution.py:271
  80.2 1.9 %collective-permute-start.13 = (bf16[32,256]{1,0:T(8,128)(2,1)S(1)}, bf16[32,256]{1,0:T(8,128)(2,1)S(1)}, u32[]{:S(2)}, u32[]{:S(2)}) collective-permute-start(bf16[32,256]{1,0:T(8,128)(2,1)S(1)} %get-tuple-element.38), channel_id=1, source_target_pairs={{0,2},{1,3},{2,4},{3,5},{4,6},{5,7},{6,8},{7,9},{8,10},{9,11},{10,... | collective-permute-start | bytes 49160 | tf_op jit(solution)/shard_map/ppermute | solution.py:271
  82.1 2.4 %collective-permute-start.11 = (bf16[64,256]{1,0:T(8,128)(2,1)S(1)}, bf16[64,256]{1,0:T(8,128)(2,1)S(1)}, u32[]{:S(2)}, u32[]{:S(2)}) collective-permute-start(bf16[64,256]{1,0:T(8,128)(2,1)S(1)} %get-tuple-element.36.own_ref), channel_id=1, source_target_pairs={{0,1},{1,2},{2,3},{3,4},{4,5},{5,6},{6,7},{7,8},{8,9},{9,10},{10,1... | collective-permute-start | bytes 98312 | tf_op jit(solution)/shard_map/ppermute | solution.py:271
  84.7 3.2 %collective-permute-done.13.second_ref = bf16[32,256]{1,0:T(8,128)(2,1)S(1)} collective-permute-done((bf16[32,256]{1,0:T(8,128)(2,1)S(1)}, bf16[32,256]{1,0:T(8,128)(2,1)S(1)}, u32[]{:S(2)}, u32[]{:S(2)}) %collective-permute-start.13) | collective-permute-done | bytes 16416 | tf_op jit(solution)/shard_map/ppermute | solution.py:271
  90.3 16.9 %all_to_all.10.arrived_ref = bf16[16,8,128]{2,1,0:T(8,128)(2,1)S(1)} all-to-all(bf16[16,8,128]{2,1,0:T(8,128)(2,1)S(1)} %select.75), channel_id=1, replica_groups=mesh['zhi'=4,'x'=4,'zlo'=2,'y'=8,'core'=2] {'zhi','x'}, dimensions={0} | all-to-all | bytes 65536 | tf_op jit(solution)/shard_map/all_to_all | solution.py:485
  (55 shorter events, 9.3 us)
Async XLA Ops:
  1.9 10.5 %collective-permute-start = (bf16[48,1280]{1,0:T(8,128)(2,1)}, bf16[48,1280]{1,0:T(8,128)(2,1)S(1)}, u32[]{:S(2)}, u32[]{:S(2)}) collective-permute-start(bf16[48,1280]{1,0:T(8,128)(2,1)} %weights.1), channel_id=1, source_target_pairs={{0,16},{16,0},{1,17},{17,1},{2,18},{18,2},{3,19},{19,3},{4,20},{20... | collective-permute-start | bytes 368648 | tf_op jit(solution)/shard_map/ppermute | solution.py:347
  8.2 12.6 %collective-permute-start.2 = (bf16[144,1536]{1,0:T(8,128)(2,1)S(1)}, bf16[144,1536]{1,0:T(8,128)(2,1)S(1)}, u32[]{:S(2)}, u32[]{:S(2)}) collective-permute-start(bf16[144,1536]{1,0:T(8,128)(2,1)S(1)} %edge.1), channel_id=1, source_target_pairs={{0,31},{1,0},{2,1},{3,2},{4,3},{5,4},{6,5},{7,6},{8,7},{9,8},{10,9... | collective-permute-start | bytes 1327112 | tf_op jit(solution)/shard_map/ppermute | solution.py:271
  12.4 13.5 %copy-start.15 = (f32[1536]{0:T(1024)S(1)}, f32[1536]{0:T(1024)}, u32[]{:S(2)}) copy-start(f32[1536]{0:T(1024)} %param.13) | copy-start | bytes 18436
  12.4 13.5 %copy-start.6 = (f32[24,64,64]{2,1,0:T(8,128)S(1)}, f32[24,64,64]{2,1,0:T(8,128)}, u32[]{:S(2)}) copy-start(f32[24,64,64]{2,1,0:T(8,128)} %rel_bias_ref.1) | copy-start | bytes 1179652
  12.5 8.2 %collective-permute-start.1 = (bf16[96,1280]{1,0:T(8,128)(2,1)S(1)}, bf16[96,1280]{1,0:T(8,128)(2,1)S(1)}, u32[]{:S(2)}, u32[]{:S(2)}) collective-permute-start(bf16[96,1280]{1,0:T(8,128)(2,1)S(1)} %maximum_select_fusion), channel_id=1, source_target_pairs={{0,2},{1,15},{2,0},{3,5},{4,6},{5,3},{6,4},{7,9},{8,10},{9,7},{10,... | collective-permute-start | bytes 737288 | tf_op jit(solution)/shard_map/ppermute | solution.py:352
  20.8 7.6 %copy-start.1 = (bf16[1,32,8,1536]{3,2,1,0:T(8,128)(2,1)S(1)}, bf16[1,32,8,1536]{3,2,1,0:T(8,128)(2,1)}, u32[]{:S(2)}) copy-start(bf16[1,32,8,1536]{3,2,1,0:T(8,128)(2,1)} %tokens_ref.3) | copy-start | bytes 2359300
  20.8 7.6 %copy-start.3 = (bf16[1536,69]{0,1:T(8,128)(2,1)S(1)}, bf16[1536,69]{0,1:T(8,128)(2,1)}, u32[]{:S(2)}) copy-start(bf16[1536,69]{0,1:T(8,128)(2,1)} %param.17) | copy-start | bytes 635908
  20.8 7.6 %copy-start.9 = (f32[16,1,1,2,128]{4,3,2,1,0:T(2,128)S(1)}, f32[16,1,1,2,128]{4,3,2,1,0:T(2,128)}, u32[]{:S(2)}) copy-start(f32[16,1,1,2,128]{4,3,2,1,0:T(2,128)} %param.19) | copy-start | bytes 49156
  20.8 7.6 %copy-start.11 = (s32[1,1,2,128]{3,2,1,0:T(2,128)S(1)}, s32[1,1,2,128]{3,2,1,0:T(2,128)}, u32[]{:S(2)}) copy-start(s32[1,1,2,128]{3,2,1,0:T(2,128)} %param.20) | copy-start | bytes 3076
  20.8 7.6 %copy-start.12 = (f32[1,1,2,128]{3,2,1,0:T(2,128)S(1)}, f32[1,1,2,128]{3,2,1,0:T(2,128)}, u32[]{:S(2)}) copy-start(f32[1,1,2,128]{3,2,1,0:T(2,128)} %param.18) | copy-start | bytes 3076
  20.9 12.2 %collective-permute-start.3 = (bf16[192,1280]{1,0:T(8,128)(2,1)S(1)}, bf16[192,1280]{1,0:T(8,128)(2,1)}, u32[]{:S(2)}, u32[]{:S(2)}) collective-permute-start(bf16[192,1280]{1,0:T(8,128)(2,1)S(1)} %pad_maximum_fusion.blocks_0_), channel_id=1, source_target_pairs={{0,14},{1,3},{2,4},{3,1},{4,2},{5,7},{6,8},{7,5},{8,6},{9,11},{10,... | collective-permute-start | bytes 1474568 | tf_op jit(solution)/shard_map/ppermute | solution.py:365
  26.5 15.0 %collective-permute-start.5 = (bf16[192,1280]{1,0:T(8,128)(2,1)S(1)}, bf16[192,1280]{1,0:T(8,128)(2,1)S(1)}, u32[]{:S(2)}, u32[]{:S(2)}) collective-permute-start(bf16[192,1280]{1,0:T(8,128)(2,1)S(1)} %pad_maximum_fusion.blocks_0_), channel_id=1, source_target_pairs={{0,1},{1,0},{2,3},{3,2},{4,5},{5,4},{6,7},{7,6},{8,9},{9,8},{10,11... | collective-permute-start | bytes 1474568 | tf_op jit(solution)/shard_map/ppermute | solution.py:292
  30.6 37.9 %copy-start.4 = (bf16[256,1536]{1,0:T(8,128)(2,1)}, bf16[256,1536]{1,0:T(8,128)(2,1)S(1)}, u32[]{:S(2)}) copy-start(bf16[256,1536]{1,0:T(8,128)(2,1)S(1)} %get-tuple-element.25.own_ref) | copy-start | bytes 2359300
  33.0 11.0 %collective-permute-start.4 = (bf16[192,1280]{1,0:T(8,128)(2,1)}, bf16[192,1280]{1,0:T(8,128)(2,1)}, u32[]{:S(2)}, u32[]{:S(2)}) collective-permute-start(bf16[192,1280]{1,0:T(8,128)(2,1)} %collective-permute-done.3.blocks_1_), channel_id=1, source_target_pairs={{0,2},{1,15},{2,0},{3,5},{4,6},{5,3},{6,4},{7,9},{8,10},{9,7},{10,... | collective-permute-start | bytes 1474568 | tf_op jit(solution)/shard_map/ppermute | solution.py:420
  35.0 27.0 %collective-permute-start.7 = (bf16[256,1536]{1,0:T(8,128)(2,1)S(1)}, bf16[256,1536]{1,0:T(8,128)(2,1)S(1)}, u32[]{:S(2)}, u32[]{:S(2)}) collective-permute-start(bf16[256,1536]{1,0:T(8,128)(2,1)S(1)} %get-tuple-element.25.own_ref), channel_id=1, source_target_pairs={{0,32},{32,0},{64,96},{96,64},{1,33},{33,1},{65,97},{97,65},{2,34}... | collective-permute-start | bytes 2359304 | tf_op jit(solution)/shard_map/ppermute | solution.py:405
  37.7 24.3 %collective-permute-start.8 = (bf16[192,1280]{1,0:T(8,128)(2,1)}, bf16[192,1280]{1,0:T(8,128)(2,1)}, u32[]{:S(2)}, u32[]{:S(2)}) collective-permute-start(bf16[192,1280]{1,0:T(8,128)(2,1)} %collective-permute-done.3.blocks_1_), channel_id=1, source_target_pairs={{0,1},{1,0},{2,3},{3,2},{4,5},{5,4},{6,7},{7,6},{8,9},{9,8},{10,11... | collective-permute-start | bytes 1474568 | tf_op jit(solution)/shard_map/ppermute | solution.py:292
  44.1 17.9 %collective-permute-start.6 = (bf16[192,1280]{1,0:T(8,128)(2,1)}, bf16[192,1280]{1,0:T(8,128)(2,1)}, u32[]{:S(2)}, u32[]{:S(2)}) collective-permute-start(bf16[192,1280]{1,0:T(8,128)(2,1)} %collective-permute-done.4.blocks_2_), channel_id=1, source_target_pairs={{0,14},{1,3},{2,4},{3,1},{4,2},{5,7},{6,8},{7,5},{8,6},{9,11},{10,... | collective-permute-start | bytes 1474568 | tf_op jit(solution)/shard_map/ppermute | solution.py:423
  47.7 20.6 %all-to-all-start = ((f32[16,8,128]{2,1,0:T(8,128)}), f32[16,8,128]{2,1,0:T(8,128)S(1)}, u32[]{:S(2)}, u32[]{:S(2)}) async-start(f32[16,8,128]{2,1,0:T(8,128)} %get-tuple-element.28), calls=%async_computation | async-start | bytes 131072 | tf_op jit(solution)/shard_map/all_to_all | solution.py:427
  60.1 8.5 %collective-permute-start.9 = (bf16[192,1280]{1,0:T(8,128)(2,1)}, bf16[192,1280]{1,0:T(8,128)(2,1)}, u32[]{:S(2)}, u32[]{:S(2)}) collective-permute-start(bf16[192,1280]{1,0:T(8,128)(2,1)} %collective-permute-done.4.blocks_2_), channel_id=1, source_target_pairs={{0,1},{1,0},{2,3},{3,2},{4,5},{5,4},{6,7},{7,6},{8,9},{9,8},{10,11... | collective-permute-start | bytes 1474568 | tf_op jit(solution)/shard_map/ppermute | solution.py:292
  62.0 6.5 %collective-permute-start.10 = (bf16[192,1280]{1,0:T(8,128)(2,1)}, bf16[192,1280]{1,0:T(8,128)(2,1)}, u32[]{:S(2)}, u32[]{:S(2)}) collective-permute-start(bf16[192,1280]{1,0:T(8,128)(2,1)} %collective-permute-done.6.blocks_3_), channel_id=1, source_target_pairs={{0,1},{1,0},{2,3},{3,2},{4,5},{5,4},{6,7},{7,6},{8,9},{9,8},{10,11... | collective-permute-start | bytes 1474568 | tf_op jit(solution)/shard_map/ppermute | solution.py:292
  70.6 36.5 %copy-start.2 = (bf16[1,1,4,128,1104]{3,4,2,1,0:T(8,128)(2,1)S(1)}, bf16[1,1,4,128,1104]{3,4,2,1,0:T(8,128)(2,1)}, u32[]{:S(2)}) copy-start(bf16[1,1,4,128,1104]{3,4,2,1,0:T(8,128)(2,1)} %param.23) | copy-start | bytes 3391492
  78.3 6.4 %collective-permute-start.12 = (bf16[32,256]{1,0:T(8,128)(2,1)S(1)}, bf16[32,256]{1,0:T(8,128)(2,1)S(1)}, u32[]{:S(2)}, u32[]{:S(2)}) collective-permute-start(bf16[32,256]{1,0:T(8,128)(2,1)S(1)} %get-tuple-element.37), channel_id=1, source_target_pairs={{0,31},{1,0},{2,1},{3,2},{4,3},{5,4},{6,5},{7,6},{8,7},{9,8},{10,9... | collective-permute-start | bytes 49160 | tf_op jit(solution)/shard_map/ppermute | solution.py:271
  80.2 7.7 %collective-permute-start.13 = (bf16[32,256]{1,0:T(8,128)(2,1)S(1)}, bf16[32,256]{1,0:T(8,128)(2,1)S(1)}, u32[]{:S(2)}, u32[]{:S(2)}) collective-permute-start(bf16[32,256]{1,0:T(8,128)(2,1)S(1)} %get-tuple-element.38), channel_id=1, source_target_pairs={{0,2},{1,3},{2,4},{3,5},{4,6},{5,7},{6,8},{7,9},{8,10},{9,11},{10,... | collective-permute-start | bytes 49160 | tf_op jit(solution)/shard_map/ppermute | solution.py:271
  82.1 7.4 %collective-permute-start.11 = (bf16[64,256]{1,0:T(8,128)(2,1)S(1)}, bf16[64,256]{1,0:T(8,128)(2,1)S(1)}, u32[]{:S(2)}, u32[]{:S(2)}) collective-permute-start(bf16[64,256]{1,0:T(8,128)(2,1)S(1)} %get-tuple-element.36.own_ref), channel_id=1, source_target_pairs={{0,1},{1,2},{2,3},{3,4},{4,5},{5,6},{6,7},{7,8},{8,9},{9,10},{10,1... | collective-permute-start | bytes 98312 | tf_op jit(solution)/shard_map/ppermute | solution.py:271
  (7 other events, 16.8 us)
